TPU v7x, 256 devices: a whole 4x4x8 slice. The times are simulated.
256 devices in a mesh: seq: 32 (over x, z_hi, core), exp: 8 (over y, z_lo).
Axes of the slice: x: 4, y: 4, z: 8 (z_hi: 4, z_lo: 2; z = z_hi * 2 + z_lo), core: 2. Of those that a mesh axis runs over, the one named last changes fastest.
Arguments:
- tokens: bfloat16 [61440, 1024], P('seq'), may hold values from -24 to 24
- slot_embed: bfloat16 [1024, 2048], P(None, 'exp'), may hold values from -3 to 3
- w_in: bfloat16 [128, 1024, 4096], P('exp', None, 'seq'), may hold values from -0.375 to 0.375
- w_out: bfloat16 [128, 4096, 1024], P('exp', 'seq'), may hold values from -0.125 to 0.125
Outputs:
- mixed_out: bfloat16 [61440, 1024], P('seq', 'exp')
All inputs are finite; a program needn't handle non-finite values.
Results may differ from a plain program's by a relative error of at most 0.012.
Values may be sent and summed in bfloat16 or wider, within the bound.
No kernel may reach another device: no remote copies, remote signals or barrier semaphores. Data moves between devices by JAX's collectives and lax.ppermute only.
A program may use at most 64 MiB of HBM per device.

v0:
```python
import jax
import jax.numpy as jnp
from jax import lax
from jax.sharding import PartitionSpec as P


def gelu_tanh(values):
    return (
        0.5
        * values
        * (1.0 + jnp.tanh(0.7978845608028654 * (values + 0.044715 * values * values * values)))
    )


def on_device(tokens, slot_embed, w_in, w_out):
    experts_here = w_in.shape[0]
    slot_count = slot_embed.shape[1]
    slot_exp = slot_count // experts_here
    features = tokens.shape[1]
    logits = jnp.dot(tokens, slot_embed, preferred_element_type=jnp.float32)
    col_peak = jnp.max(logits, axis=0)
    peak_all = lax.pmax(col_peak, "seq")
    weights = jnp.exp(logits - peak_all[None, :])
    total_all = lax.psum(jnp.sum(weights, axis=0), "seq")
    dispatch = (weights / total_all[None, :]).astype(jnp.bfloat16)
    partial_in = lax.dot_general(
        dispatch, tokens, (((0,), (0,)), ((), ())), preferred_element_type=jnp.float32
    )
    slot_in = lax.psum(partial_in, "seq").astype(jnp.bfloat16)
    grouped = slot_in.reshape(experts_here, slot_exp, features)
    hidden = gelu_tanh(
        jnp.einsum("esd,edh->esh", grouped, w_in, preferred_element_type=jnp.float32)
    ).astype(jnp.bfloat16)
    partial_out = jnp.einsum(
        "esh,ehd->esd", hidden, w_out, preferred_element_type=jnp.float32
    ).reshape(slot_count, features)
    slot_out = lax.psum(partial_out, "seq").astype(jnp.bfloat16)
    row_peak = lax.pmax(jnp.max(logits, axis=1), "exp")
    row_weights = jnp.exp(logits - row_peak[:, None])
    row_sum = lax.psum(jnp.sum(row_weights, axis=1), "exp")
    combine = (row_weights / row_sum[:, None]).astype(jnp.bfloat16)
    term = jnp.dot(combine, slot_out, preferred_element_type=jnp.float32)
    mixed_out = lax.psum_scatter(term.astype(jnp.bfloat16), "exp", scatter_dimension=1, tiled=True)
    return mixed_out


def solution(mesh):
    placed = (P("seq", None), P(None, "exp"), P("exp", None, "seq"), P("exp", "seq", None))
    return jax.shard_map(
        on_device, mesh=mesh, in_specs=placed, out_specs=P("seq", "exp"), check_vma=False
    )
```

profile of v0, /device:TPU:1, one launch (start us, length us, event | category | flops | bytes accessed | tf_op | source)
XLA Modules:
  0.0 604.6 jit_solution(15474171280990773589)
XLA Ops:
  6.5 0.0 copy-start
  6.5 0.0 reduce-scatter.4.cloned.1.call-start
  6.5 1.0 copy-done
  7.6 3.4 fusion.23
  11.0 0.0 copy-start.1
  11.0 73.4 %pmax.15 = f32[256]{0:T(256)S(1)} all-reduce(f32[256]{0:T(256)S(1)} %get-tuple-element.7), channel_id=1, replica_groups=mesh['seq'=32,'exp'=8] {'seq'}, use_global_device_ids=true, to_apply=%region_5.0 | all-reduce | flops 256 | bytes 2048 | tf_op jit(solution)/shard_map/pmax | solution.py:22
  84.3 0.0 copy-start.2
  84.3 16.1 %pmax.14 = f32[1920]{0:T(1024)S(1)} all-reduce(f32[1920]{0:T(1024)S(1)} %get-tuple-element.8), channel_id=1, replica_groups=mesh['seq'=32,'exp'=8] {'exp'}, use_global_device_ids=true, to_apply=%region_1.0 | all-reduce | flops 1920 | bytes 15360 | tf_op jit(solution)/shard_map/pmax | solution.py:38
  100.4 0.8 fusion.1
  101.2 79.5 %psum.29 = f32[256]{0:T(256)} all-reduce(f32[256]{0:T(256)S(1)} %get-tuple-element.5), channel_id=1, replica_groups=mesh['seq'=32,'exp'=8] {'seq'}, use_global_device_ids=true, to_apply=%region_7.0 | all-reduce | flops 256 | bytes 2048 | tf_op jit(solution)/shard_map/psum | solution.py:24
  180.7 0.0 copy-done.2
  180.7 13.1 %psum.28 = f32[1920]{0:T(1024)S(1)} all-reduce(f32[1920]{0:T(1024)S(1)} %get-tuple-element.6), channel_id=1, replica_groups=mesh['seq'=32,'exp'=8] {'exp'}, use_global_device_ids=true, to_apply=%region_3.0 | all-reduce | flops 1920 | bytes 15360 | tf_op jit(solution)/shard_map/psum | solution.py:40
  193.8 0.0 copy-done.1
  193.8 3.4 fusion.2
  197.3 146.0 %all-reduce.2 = bf16[256,1024]{1,0:T(8,128)(2,1)S(1)} all-reduce(f32[256,1024]{1,0:T(8,128)S(1)} %fusion.2), channel_id=1, replica_groups=mesh['seq'=32,'exp'=8] {'seq'}, use_global_device_ids=true, to_apply=%region_8.0 | all-reduce | flops 262144 | bytes 1572864 | tf_op jit(solution)/shard_map/psum | solution.py:29
  343.3 4.7 fusion.13
  348.0 149.2 %all-reduce.3 = bf16[256,1024]{1,0:T(8,128)(2,1)S(1)} all-reduce(f32[256,1024]{1,0:T(8,128)S(1)} %bitcast.12), channel_id=1, replica_groups=mesh['seq'=32,'exp'=8] {'seq'}, use_global_device_ids=true, to_apply=%region_9.0 | all-reduce | flops 262144 | bytes 1572864 | tf_op jit(solution)/shard_map/psum | solution.py:37
  497.2 4.7 convolution_convert_fusion
  501.9 6.3 %copy.5 = bf16[1920,1024]{0,1:T(8,128)(2,1)} copy(bf16[1920,1024]{1,0:T(8,128)(2,1)} %convolution_convert_fusion) | data formatting | bytes 7864320
  508.2 0.0 reduce-scatter.4.cloned.1.call-update
  508.3 87.5 %reduce-scatter.4.cloned.1.call-done = bf16[128,1920]{1,0:T(8,128)(2,1)} async-done(((bf16[1024,1920]{1,0:T(8,128)(2,1)}), bf16[128,1920]{1,0:T(8,128)(2,1)}) %reduce-scatter.4.cloned.1.call-update) | async-done | bytes 491536
  595.8 2.0 copy.6
Async XLA Ops:
  6.5 1.0 copy-start
  6.5 589.2 %reduce-scatter.4.cloned.1.call-start = ((), (), s32[]{:S(2)}) async-start(), calls=%async_computation.1 | async-start | bytes 4423680
  11.0 182.9 %copy-start.1 = (f32[1920,256]{1,0:T(8,128)}, f32[1920,256]{1,0:T(8,128)S(1)}, u32[]{:S(2)}) copy-start(f32[1920,256]{1,0:T(8,128)S(1)} %get-tuple-element.9) | copy-start | bytes 5898244
  84.3 96.4 %copy-start.2 = (f32[256]{0:T(256)}, f32[256]{0:T(256)S(1)}, u32[]{:S(2)}) copy-start(f32[256]{0:T(256)S(1)} %pmax.15) | copy-start | bytes 3076
Sparse Core Ops, SparseCore 0:
  508.4 87.3 reduce-scatter.3
where the time goes:
time: 605 us
  blocking collectives  477 us (79%)
  waiting for transfers between devices  87.5 us (14%)
  matrix products  16.2 us (3%)
  between operations  13.4 us (2%)
  local copies, waits for them, and re-layouts  9.4 us (2%)
    psum x1, blocking collectives, on_device(): slot_out = lax.psum(partial_out, 'seq').astype(jnp.bfloat16)  149 us
    psum x1, blocking collectives, on_device(): slot_in = lax.psum(partial_in, 'seq').astype(jnp.bfloat16)  146 us
    unnamed x2, waiting for transfers between devices  87.5 us
    psum x1, blocking collectives, on_device(): total_all = lax.psum(jnp.sum(weights, axis=0), 'seq')  79.5 us
    pmax x1, blocking collectives, on_device(): peak_all = lax.pmax(col_peak, 'seq')  73.4 us
    pmax x1, blocking collectives, on_device(): row_peak = lax.pmax(jnp.max(logits, axis=1), 'exp')  16.1 us
    psum x1, blocking collectives, on_device(): row_sum = lax.psum(jnp.sum(row_weights, axis=1), 'exp')  13.1 us
  transfers between devices with their start and end apart: 1, of which 1 were waited for; matrix products, arithmetic and copies ran while one was open for 0% of the time, Pallas kernels for 0%

commit v1 on v0

v1 whole, which is shorter than its diff:
```python
import jax
import jax.numpy as jnp
from jax import lax
from jax.sharding import Mesh, PartitionSpec as P

F32 = jnp.float32
BF16 = jnp.bfloat16
RING = ("x", "zh")
EXP = ("y", "zl")
SWAP = [(0, 1), (1, 0)]


def gelu_tanh(values):
    return (
        0.5
        * values
        * (1.0 + jnp.tanh(0.7978845608028654 * (values + 0.044715 * values * values * values)))
    )


def split3(column):
    high = lax.reduce_precision(column, 8, 7)
    rest = column - high
    mid = lax.reduce_precision(rest, 8, 7)
    return [high, mid, rest - mid]


def pack(total, peak):
    rows = peak.shape[:-1]
    columns = split3(total) + split3(peak)
    fill = jnp.zeros(rows + (128 - len(columns),), F32)
    return jnp.concatenate(columns + [fill], axis=-1).astype(BF16)


def unpack(tail):
    tail = tail.astype(F32)
    total = tail[..., 0:1] + tail[..., 1:2] + tail[..., 2:3]
    peak = tail[..., 3:4] + tail[..., 4:5] + tail[..., 5:6]
    return total, peak


def half_of(values, core):
    half = values.shape[0] // 2
    return lax.dynamic_slice_in_dim(values, core * half, half, 0)


def in_order(own, other, core):
    return jnp.where(
        core == 0, jnp.concatenate([own, other], 0), jnp.concatenate([other, own], 0)
    )


def on_device(tokens, slot_embed, w_in, w_out):
    experts_here = w_in.shape[0]
    slots = slot_embed.shape[1]
    slot_exp = slots // experts_here
    count, features = tokens.shape
    core = lax.axis_index("core")
    ring = lax.axis_size(RING)
    groups = lax.axis_size(EXP)
    half = slots // 2
    part = half // ring
    width = features // groups

    mine = lax.dynamic_slice_in_dim(slot_embed, core * half, half, 1)
    table_own = lax.all_gather(mine, EXP, axis=1, tiled=True)
    table_other = lax.ppermute(table_own, "core", SWAP)

    logits = lax.dot_general(
        slot_embed, tokens, (((0,), (1,)), ((), ())), preferred_element_type=F32
    )
    peak = jnp.max(logits, axis=1, keepdims=True)
    weights = jnp.exp(logits - peak)
    total = jnp.sum(weights, axis=1, keepdims=True)
    partial_in = jnp.dot(weights.astype(BF16), tokens, preferred_element_type=F32)

    send = jnp.concatenate([partial_in.astype(BF16), pack(total, peak)], axis=1)
    got = lax.ppermute(half_of(send, 1 - core), "core", SWAP)
    got_total, got_peak = unpack(got[:, features:])
    own_total, own_peak = half_of(total, core), half_of(peak, core)
    top = jnp.maximum(own_peak, got_peak)
    own_scale, got_scale = jnp.exp(own_peak - top), jnp.exp(got_peak - top)
    merged = half_of(partial_in, core) * own_scale + got[:, :features].astype(F32) * got_scale
    merged_total = own_total * own_scale + got_total * got_scale

    send = jnp.concatenate([merged.astype(BF16), pack(merged_total, top)], axis=1)
    got = lax.all_to_all(send.reshape(ring, part, -1), RING, 0, 0)
    got_total, got_peak = unpack(got[:, :, features:])
    scale = jnp.exp(got_peak - jnp.max(got_peak, axis=0, keepdims=True))
    summed = jnp.sum(got[:, :, :features].astype(F32) * scale, axis=0)
    slot_part = (summed / jnp.sum(got_total * scale, axis=0)).astype(BF16)
    own = lax.all_to_all(
        jnp.broadcast_to(slot_part[None], (ring, part, features)), RING, 0, 0
    ).reshape(half, features)
    other = lax.ppermute(own, "core", SWAP)
    slot_in = in_order(own, other, core)

    grouped = slot_in.reshape(experts_here, slot_exp, features)
    hidden = gelu_tanh(
        jnp.einsum("esd,edh->esh", grouped, w_in, preferred_element_type=F32)
    ).astype(BF16)
    partial_out = jnp.einsum("esh,ehd->esd", hidden, w_out, preferred_element_type=F32)
    partial_out = partial_out.reshape(slots, features)

    got = lax.ppermute(half_of(partial_out, 1 - core).astype(BF16), "core", SWAP)
    merged = half_of(partial_out, core) + got.astype(F32)
    got = lax.all_to_all(merged.astype(BF16).reshape(ring, part, features), RING, 0, 0)
    out_part = jnp.sum(got.astype(F32), axis=0).astype(BF16)
    got = lax.all_to_all(out_part.reshape(part, groups, width), EXP, 1, 0)
    got = lax.all_to_all(
        jnp.broadcast_to(got[None], (ring, groups, part, width)), RING, 0, 0
    )
    out_own = got.transpose(1, 0, 2, 3).reshape(groups * half, width)
    out_other = lax.ppermute(out_own, "core", SWAP)

    logits_own = jnp.dot(tokens, table_own, preferred_element_type=F32)
    logits_other = jnp.dot(tokens, table_other, preferred_element_type=F32)
    row_peak = jnp.maximum(
        jnp.max(logits_own, axis=1, keepdims=True), jnp.max(logits_other, axis=1, keepdims=True)
    )
    weights_own = jnp.exp(logits_own - row_peak)
    weights_other = jnp.exp(logits_other - row_peak)
    row_total = jnp.sum(weights_own, axis=1, keepdims=True) + jnp.sum(
        weights_other, axis=1, keepdims=True
    )
    mixed = jnp.dot(weights_own.astype(BF16), out_own, preferred_element_type=F32)
    mixed += jnp.dot(weights_other.astype(BF16), out_other, preferred_element_type=F32)
    return (mixed / row_total).astype(BF16)


def solution(mesh):
    grid = Mesh(mesh.devices.reshape(4, 4, 2, 4, 2), ("x", "zh", "core", "y", "zl"))
    seq = ("x", "zh", "core")
    placed = (P(seq, None), P(None, EXP), P(EXP, None, seq), P(EXP, seq, None))
    return jax.shard_map(
        on_device, mesh=grid, in_specs=placed, out_specs=P(seq, EXP), check_vma=False
    )
```

time: 605 us -> 159 us (0.26)
  blocking collectives: 477 us -> 88 us
  waiting for transfers between devices: 87.5 us -> 11.2 us
  starting transfers between devices: 0.01 us -> 11.5 us
  matrix products: 16.2 us -> 27.5 us
  local copies, waits for them, and re-layouts: 9.4 us -> 3.33 us
    psum x4 -> x0, blocking collectives: 388 us -> none  [the longest x1 149 us: on_device(): slot_out = lax.psum(partial_out, 'seq').astype(jnp.bfloat16)]
    pmax x2 -> x0, blocking collectives: 89.4 us -> none  [the longest x1 73.4 us: on_device(): peak_all = lax.pmax(col_peak, 'seq')]
    all_to_all x0 -> x5, blocking collectives: none -> 88 us  [the longest x1 24.1 us: on_device(): got = lax.all_to_all(send.reshape(ring, part, -1), RING, 0, 0)]
    unnamed x2 -> x1, waiting for transfers between devices: 87.5 us -> 0.02 us
    ppermute x0 -> x5, starting transfers between devices: none -> 11.5 us  [the longest x1 3.33 us: on_device(): got = lax.ppermute(half_of(send, 1 - core), 'core', SWAP)]
    dot_general x4 -> x7, matrix products: 16.2 us -> 27.5 us  [the longest x1 7.3 us: on_device(): logits_own = jnp.dot(tokens, table_own, preferred_element_type=F32)]
    all_gather x0 -> x1, waiting for transfers between devices: none -> 9.57 us  [on_device(): table_own = lax.all_gather(mine, EXP, axis=1, tiled=True)]
    unnamed x8 -> x6, local copies, waits for them, and re-layouts: 9.4 us -> 1.05 us
  transfers between devices with their start and end apart: 1 -> 6, of which waited for: 1 -> 3; matrix products, arithmetic and copies ran while one was open for 0% -> 16% of each run, Pallas kernels for 0% -> 0%
where the time goes in v1:
time: 159 us
  blocking collectives  88 us (55%)
  matrix products  27.5 us (17%)
  between operations  13.6 us (9%)
  starting transfers between devices  11.5 us (7%)
  waiting for transfers between devices  11.2 us (7%)
  other arithmetic  3.81 us (2%)
  local copies, waits for them, and re-layouts  3.33 us (2%)
    all_to_all x1, blocking collectives, on_device(): got = lax.all_to_all(send.reshape(ring, part, -1), RING, 0, 0)  24.1 us
    all_to_all x1, blocking collectives, on_device(): lax.all_to_all(merged.astype(BF16).reshape(ring, part, features), RING, 0...  20.9 us
    all_to_all x1, blocking collectives, on_device(): lax.all_to_all(jnp.broadcast_to(slot_part[None], (ring, part, features)),...  18.5 us
    all_to_all x1, blocking collectives, on_device(): lax.all_to_all(jnp.broadcast_to(got[None], (ring, groups, part, width)),...  14.9 us
    all_to_all x1, blocking collectives, on_device(): got = lax.all_to_all(out_part.reshape(part, groups, width), EXP, 1, 0)  9.62 us
    all_gather x1, waiting for transfers between devices, on_device(): table_own = lax.all_gather(mine, EXP, axis=1, tiled=True)  9.57 us
    dot_general x1, matrix products, on_device(): logits_own = jnp.dot(tokens, table_own, preferred_element_type=F32)  7.3 us
    dot_general x1, matrix products, on_device(): logits_other = jnp.dot(tokens, table_other, preferred_element_type=F32)  6.15 us
  transfers between devices with their start and end apart: 6, of which 3 were waited for; matrix products, arithmetic and copies ran while one was open for 16% of the time, Pallas kernels for 0%

profile of v1, /device:TPU:1, one launch (start us, length us, event | category | flops | bytes accessed | tf_op | source)
XLA Modules:
  0.0 159.0 jit_solution(5407755224149707036)
XLA Ops:
  6.5 0.0 copy-start
  6.5 0.0 all-gather.2.cloned.1.call-start
  6.5 0.0 copy-start.1
  6.5 1.0 copy-done
  7.6 3.8 %fusion.54 = (f32[256]{0:T(256)S(1)}, f32[256,1920]{1,0:T(8,128)S(1)}) fusion(bf16[1024,256]{1,0:T(8,128)(2,1)S(1)} %copy-done, bf16[1920,1024]{1,0:T(8,128)(2,1)} %param.4), kind=kOutput, calls=%fused_computation.85 | convolution fusion | flops 1007124224 | bytes 6423552 | tf_op jit(solution)/shard_map/dot_general | solution.py:69
  11.4 0.0 copy-done.1
  11.4 1.7 %fusion.55 = (bf16[256,1024]{0,1:T(8,128)(2,1)S(1)}, f32[256,1024]{0,1:T(8,128)S(1)}) fusion(bf16[1920,1024]{1,0:T(8,128)(2,1)S(1)} %copy-done.1, f32[256,1920]{1,0:T(8,128)S(1)} %get-tuple-element.29, f32[256]{0:T(256)S(1)} %get-tuple-element.28), kind=kOutput, calls=%fused_computation.86 | convolution fusion | flops 1007878144 | bytes 7472128 | tf_op jit(solution)/shard_map/dot_general | solution.py:75
  13.1 0.4 fusion.19
  13.6 0.5 concatenate.18
  14.1 3.3 %collective-permute-start.1 = (bf16[128,1152]{0,1:T(8,128)(2,1)S(1)}, bf16[128,1152]{0,1:T(8,128)(2,1)S(1)}, u32[]{:S(2)}, u32[]{:S(2)}) collective-permute-start(bf16[128,1152]{0,1:T(8,128)(2,1)S(1)} %constant_dynamic-slice_fusion), channel_id=1, source_target_pairs={{0,8},{8,0},{1,9},{9,1},{2,10},{10,2},{3,11},{11,3},{4,12},{12,4},... | collective-permute-start | bytes 884744 | tf_op jit(solution)/shard_map/ppermute | solution.py:78
  17.4 0.7 constant_dynamic-slice_fusion.1
  18.1 0.0 all-gather.2.cloned.1.call-update
  18.2 0.5 collective-permute-done.1
  18.6 0.1 fusion.42
  18.7 0.1 fusion.41
  18.8 0.1 add_convert_fusion.1
  18.9 0.4 concatenate.19
  19.4 0.2 copy.39
  19.6 24.1 %all_to_all.35 = bf16[16,8,1152]{2,1,0:T(8,128)(2,1)S(1)} all-to-all(bf16[16,8,1152]{2,1,0:T(8,128)(2,1)S(1)} %bitcast.54), channel_id=1, replica_groups=mesh['x'=4,'zh'=4,'core'=2,'y'=4,'zl'=2] {'x','zh'}, dimensions={0} | all-to-all | bytes 589824 | tf_op jit(solution)/shard_map/all_to_all | solution.py:87
  43.6 0.2 copy.40
  43.9 0.1 fusion.52
  44.0 0.2 fusion.37
  44.2 0.1 copy.41
  44.3 0.1 multiply_reduce_fusion
  44.4 0.1 divide_convert_fusion
  44.5 18.5 %all_to_all.36 = bf16[16,8,1024]{2,1,0:T(8,128)(2,1)S(1)} all-to-all(bf16[16,8,1024]{2,1,0:T(8,128)(2,1)S(1)} %broadcast_in_dim.12), channel_id=1, replica_groups=mesh['x'=4,'zh'=4,'core'=2,'y'=4,'zl'=2] {'x','zh'}, dimensions={0} | all-to-all | bytes 524288 | tf_op jit(solution)/shard_map/all_to_all | solution.py:92
  63.0 2.8 %collective-permute-start.2 = (bf16[128,1024]{1,0:T(8,128)(2,1)S(1)}, bf16[128,1024]{1,0:T(8,128)(2,1)S(1)}, u32[]{:S(2)}, u32[]{:S(2)}) collective-permute-start(bf16[128,1024]{1,0:T(8,128)(2,1)S(1)} %bitcast.57), channel_id=1, source_target_pairs={{0,8},{8,0},{1,9},{9,1},{2,10},{10,2},{3,11},{11,3},{4,12},{12,4},... | collective-permute-start | bytes 786440 | tf_op jit(solution)/shard_map/ppermute | solution.py:95
  65.9 1.2 collective-permute-done.2
  67.0 0.1 maximum_select_fusion
  67.2 4.7 %fusion.30 = f32[16,16,1024]{2,1,0:T(8,128)S(1)} fusion(bf16[16,128,1024]{2,1,0:T(8,128)(2,1)} %param.7, bf16[16,16,1024]{2,1,0:T(8,128)(2,1)S(1)} %bitcast.53, bf16[16,1024,128]{2,1,0:T(8,128)(2,1)} %param.6), kind=kOutput, calls=%fused_computation.30 | convolution fusion | flops 134512640 | bytes 9961472 | tf_op jit(solution)/shard_map/esh,ehd->esd/dot_general | solution.py:102
  71.9 0.5 collective-permute-start.3
  72.4 9.6 %all-gather.2.cloned.1.call-done = bf16[1024,1024]{1,0:T(8,128)(2,1)} async-done(((bf16[1024,128]{1,0:T(8,128)(2,1)}), bf16[1024,1024]{1,0:T(8,128)(2,1)}) %all-gather.2.cloned.1.call-update) | async-done | bytes 2097168 | tf_op jit(solution)/shard_map/all_gather | solution.py:66
  82.0 1.8 %collective-permute-start = (bf16[1024,1024]{1,0:T(8,128)(2,1)}, bf16[1024,1024]{1,0:T(8,128)(2,1)}, u32[]{:S(2)}, u32[]{:S(2)}) collective-permute-start(bf16[1024,1024]{1,0:T(8,128)(2,1)} %all-gather.2.cloned.1.call-done), channel_id=1, source_target_pairs={{0,8},{8,0},{1,9},{9,1},{2,10},{10,2},{3,11},{11,3},{4,12},{12,4},... | collective-permute-start | bytes 6291464 | tf_op jit(solution)/shard_map/ppermute | solution.py:67
  83.7 0.0 collective-permute-done.3
  83.7 0.1 fusion.24
  83.8 20.9 %all_to_all.37 = bf16[16,8,1024]{2,1,0:T(8,128)(2,1)S(1)} all-to-all(bf16[16,8,1024]{2,1,0:T(8,128)(2,1)S(1)} %fusion.24), channel_id=1, replica_groups=mesh['x'=4,'zh'=4,'core'=2,'y'=4,'zl'=2] {'x','zh'}, dimensions={0} | all-to-all | bytes 524288 | tf_op jit(solution)/shard_map/all_to_all | solution.py:107
  104.7 9.6 %all_to_all.38 = bf16[1,8,8,128]{3,1,0,2:T(8,128)(2,1)S(1)} all-to-all(bf16[1,8,8,128]{3,1,0,2:T(8,128)(2,1)S(1)} %bitcast.59), channel_id=1, replica_groups=mesh['x'=4,'zh'=4,'core'=2,'y'=4,'zl'=2] {'y','zl'}, dimensions={2} | all-to-all | bytes 32768 | tf_op jit(solution)/shard_map/all_to_all | solution.py:109
  114.4 14.9 %all_to_all.39 = bf16[16,8,8,128]{3,2,1,0:T(8,128)(2,1)S(1)} all-to-all(bf16[16,8,8,128]{3,2,1,0:T(8,128)(2,1)S(1)} %broadcast_in_dim.14), channel_id=1, replica_groups=mesh['x'=4,'zh'=4,'core'=2,'y'=4,'zl'=2] {'x','zh'}, dimensions={0} | all-to-all | bytes 524288 | tf_op jit(solution)/shard_map/all_to_all | solution.py:110
  129.4 0.0 copy-start.2
  129.4 3.1 %collective-permute-start.4 = (bf16[1024,128]{1,0:T(8,128)(2,1)S(1)}, bf16[1024,128]{1,0:T(8,128)(2,1)S(1)}, u32[]{:S(2)}, u32[]{:S(2)}) collective-permute-start(bf16[1024,128]{1,0:T(8,128)(2,1)S(1)} %bitcast.55), channel_id=1, source_target_pairs={{0,8},{8,0},{1,9},{9,1},{2,10},{10,2},{3,11},{11,3},{4,12},{12,4},... | collective-permute-start | bytes 786440 | tf_op jit(solution)/shard_map/ppermute | solution.py:114
  132.5 7.3 %fusion.56 = (f32[1920]{0:T(1024)S(1)}, f32[1024,1920]{1,0:T(8,128)S(1)}) fusion(bf16[1024,1024]{1,0:T(8,128)(2,1)} %all-gather.2.cloned.1.call-done, bf16[1920,1024]{1,0:T(8,128)(2,1)} %param.4), kind=kOutput, calls=%fused_computation.87 | convolution fusion | flops 4028495872 | bytes 13901312 | tf_op jit(solution)/shard_map/dot_general | solution.py:116
  139.8 0.0 collective-permute-done
  139.8 0.0 copy-done.2
  139.8 6.2 %fusion.57 = (f32[1920]{0:T(1024)S(1)}, f32[1024,1920]{1,0:T(8,128)S(1)}) fusion(bf16[1024,1024]{1,0:T(8,128)(2,1)} %collective-permute-done, bf16[1920,1024]{1,0:T(8,128)(2,1)S(1)} %copy-done.2), kind=kOutput, calls=%fused_computation.88 | convolution fusion | flops 4028495872 | bytes 13901312 | tf_op jit(solution)/shard_map/dot_general | solution.py:117
  146.0 2.3 %fusion.2 = (f32[1920]{0:T(1024)S(1)}, f32[1920]{0:T(1024)S(1)}) fusion(f32[1024,1920]{1,0:T(8,128)S(1)} %get-tuple-element.35, f32[1920]{0:T(1024)S(1)} %max.11, f32[1024,1920]{1,0:T(8,128)S(1)} %get-tuple-element.33), kind=kLoop, calls=%fused_computation.4 | loop fusion | flops 7860480 | bytes 15751680 | tf_op jit(solution)/shard_map/reduce_sum | solution.py:123
  148.3 1.4 fusion.6
  149.7 0.0 collective-permute-done.4
  149.8 2.4 %fusion.16 = bf16[1920,128]{1,0:T(8,128)(2,1)} fusion(f32[1920,128]{1,0:T(8,128)S(1)} %fusion.6, bf16[1024,128]{1,0:T(8,128)(2,1)S(1)} %collective-permute-done.4, f32[1024,1920]{1,0:T(8,128)S(1)} %get-tuple-element.35, f32[1920]{0:T(1024)S(1)} %max.11, f32[1920]{0:T(1024)S(1)} %add.81), kind=kOutput, calls=%fused_computation.12 | convolution fusion | flops 507985920 | bytes 9616384 | tf_op jit(solution)/shard_map/dot_general | solution.py:127
  (15 shorter events, 0.3 us)
Async XLA Ops:
  6.5 1.0 copy-start
  6.5 75.4 %all-gather.2.cloned.1.call-start = ((), (), s32[]{:S(2)}) async-start(), calls=%async_computation.5 | async-start | bytes 2359296 | tf_op jit(solution)/shard_map/all_gather | solution.py:66
  6.5 4.8 %copy-start.1 = (bf16[1920,1024]{1,0:T(8,128)(2,1)S(1)}, bf16[1920,1024]{1,0:T(8,128)(2,1)}, u32[]{:S(2)}) copy-start(bf16[1920,1024]{1,0:T(8,128)(2,1)} %param.4) | copy-start | bytes 11796484
  14.1 4.5 %collective-permute-start.1 = (bf16[128,1152]{0,1:T(8,128)(2,1)S(1)}, bf16[128,1152]{0,1:T(8,128)(2,1)S(1)}, u32[]{:S(2)}, u32[]{:S(2)}) collective-permute-start(bf16[128,1152]{0,1:T(8,128)(2,1)S(1)} %constant_dynamic-slice_fusion), channel_id=1, source_target_pairs={{0,8},{8,0},{1,9},{9,1},{2,10},{10,2},{3,11},{11,3},{4,12},{12,4},... | collective-permute-start | bytes 884744 | tf_op jit(solution)/shard_map/ppermute | solution.py:78
  63.0 4.0 %collective-permute-start.2 = (bf16[128,1024]{1,0:T(8,128)(2,1)S(1)}, bf16[128,1024]{1,0:T(8,128)(2,1)S(1)}, u32[]{:S(2)}, u32[]{:S(2)}) collective-permute-start(bf16[128,1024]{1,0:T(8,128)(2,1)S(1)} %bitcast.57), channel_id=1, source_target_pairs={{0,8},{8,0},{1,9},{9,1},{2,10},{10,2},{3,11},{11,3},{4,12},{12,4},... | collective-permute-start | bytes 786440 | tf_op jit(solution)/shard_map/ppermute | solution.py:95
  71.9 11.8 %collective-permute-start.3 = (bf16[128,1024]{1,0:T(8,128)(2,1)S(1)}, bf16[128,1024]{1,0:T(8,128)(2,1)S(1)}, u32[]{:S(2)}, u32[]{:S(2)}) collective-permute-start(bf16[128,1024]{1,0:T(8,128)(2,1)S(1)} %dynamic-slice_convert_fusion), channel_id=1, source_target_pairs={{0,8},{8,0},{1,9},{9,1},{2,10},{10,2},{3,11},{11,3},{4,12},{12,4},... | collective-permute-start | bytes 786440 | tf_op jit(solution)/shard_map/ppermute | solution.py:105
  82.0 57.8 %collective-permute-start = (bf16[1024,1024]{1,0:T(8,128)(2,1)}, bf16[1024,1024]{1,0:T(8,128)(2,1)}, u32[]{:S(2)}, u32[]{:S(2)}) collective-permute-start(bf16[1024,1024]{1,0:T(8,128)(2,1)} %all-gather.2.cloned.1.call-done), channel_id=1, source_target_pairs={{0,8},{8,0},{1,9},{9,1},{2,10},{10,2},{3,11},{11,3},{4,12},{12,4},... | collective-permute-start | bytes 6291464 | tf_op jit(solution)/shard_map/ppermute | solution.py:67
  129.4 10.4 %copy-start.2 = (bf16[1920,1024]{1,0:T(8,128)(2,1)S(1)}, bf16[1920,1024]{1,0:T(8,128)(2,1)}, u32[]{:S(2)}) copy-start(bf16[1920,1024]{1,0:T(8,128)(2,1)} %param.4) | copy-start | bytes 11796484
  129.4 20.4 %collective-permute-start.4 = (bf16[1024,128]{1,0:T(8,128)(2,1)S(1)}, bf16[1024,128]{1,0:T(8,128)(2,1)S(1)}, u32[]{:S(2)}, u32[]{:S(2)}) collective-permute-start(bf16[1024,128]{1,0:T(8,128)(2,1)S(1)} %bitcast.55), channel_id=1, source_target_pairs={{0,8},{8,0},{1,9},{9,1},{2,10},{10,2},{3,11},{11,3},{4,12},{12,4},... | collective-permute-start | bytes 786440 | tf_op jit(solution)/shard_map/ppermute | solution.py:114
Sparse Core Ops, SparseCore 0:
  18.3 63.6 all-gather.1

commit v2 on v0

v2 whole, which is shorter than its diff:
```python
import functools

import jax
import jax.numpy as jnp
from jax import lax
from jax.experimental import pallas as pl
from jax.experimental.pallas import tpu as pltpu
from jax.sharding import Mesh, PartitionSpec as P

F32 = jnp.float32
BF16 = jnp.bfloat16
SEQ = ("x", "zh", "core")
EXP = ("y", "zl")
SWAP = [(0, 1), (1, 0)]
TAIL = 128
VMEM_LIMIT = 16 << 20


def whole():
    return pl.BlockSpec(memory_space=pltpu.VMEM)


def anywhere(count=1):
    return [pl.BlockSpec(memory_space=pl.ANY)] * count


def kept(shape, kind):
    return pltpu.VMEM(shape, kind)


def far_memory(values):
    return pltpu.with_memory_space_constraint(values, pltpu.HBM)


def after(kernel, first, count):
    def ordered(*refs):
        kernel(*refs[:first], *refs[first + count :])

    return ordered


def call(kernel, outs, micros=1, limit=VMEM_LIMIT, **more):
    return pl.pallas_call(
        kernel,
        out_shape=outs,
        compiler_params=pltpu.CompilerParams(vmem_limit_bytes=limit),
        cost_estimate=pl.CostEstimate(
            flops=0, bytes_accessed=micros * 3_000_000, transcendentals=0
        ),
        **more,
    )


def gelu_tanh(values):
    return (
        0.5
        * values
        * (1.0 + jnp.tanh(0.7978845608028654 * (values + 0.044715 * values * values * values)))
    )


def pieces_of(column):
    high = column.astype(BF16).astype(F32)
    rest = column - high
    mid = rest.astype(BF16).astype(F32)
    return [high, mid, rest - mid]


def tail_of(total, peak):
    lane = lax.broadcasted_iota(jnp.int32, (total.shape[0], TAIL), 1)
    tail = jnp.zeros((total.shape[0], TAIL), F32)
    for at, column in enumerate(pieces_of(total) + pieces_of(peak)):
        tail = jnp.where(lane == at, column, tail)
    return tail


def read_tail(tail):
    total = tail[:, 0:1] + tail[:, 1:2] + tail[:, 2:3]
    peak = tail[:, 3:4] + tail[:, 4:5] + tail[:, 5:6]
    return total, peak


def dispatch_kernel(parts, core, tok_any, embed_any, own, send, tok, embed, logits, full, sems):
    rows = tok.shape[0] // parts
    width = tok.shape[1]
    half = own.shape[0]
    first = pltpu.make_async_copy(embed_any, embed, sems.at[parts])
    first.start()
    copies = []
    for at in range(parts):
        here = pl.ds(at * rows, rows)
        copies.append(pltpu.make_async_copy(tok_any.at[here], tok.at[here], sems.at[at]))
        copies[-1].start()
    first.wait()
    peak = None
    for at in range(parts):
        here = pl.ds(at * rows, rows)
        copies[at].wait()
        block = jnp.dot(tok[here, :], embed[...], preferred_element_type=F32)
        logits[here, :] = block
        top = jnp.max(block, axis=0, keepdims=True)
        peak = top if peak is None else jnp.maximum(peak, top)
    weights = jnp.exp(logits[...] - peak)
    total = jnp.sum(weights, axis=0, keepdims=True)
    full[:, :width] = lax.dot_general(
        weights.astype(BF16), tok[...], (((0,), (0,)), ((), ())), preferred_element_type=F32
    )
    stats = jnp.concatenate([total, peak, jnp.zeros((6, total.shape[1]), F32)], axis=0).T
    full[:, width:] = tail_of(stats[:, 0:1], stats[:, 1:2])
    mine = core[0]
    own[...] = full[pl.ds(pl.multiple_of(mine * half, half), half), :]
    send[...] = full[pl.ds(pl.multiple_of((1 - mine) * half, half), half), :].astype(BF16)


def dispatch(core, tokens, slot_embed, parts=5):
    count, width = tokens.shape
    slots = slot_embed.shape[1]
    shape = (slots // 2, width + TAIL)
    return call(
        functools.partial(dispatch_kernel, parts),
        micros=6,
        outs=[kept(shape, F32), kept(shape, BF16)],
        in_specs=[
            pl.BlockSpec(memory_space=pltpu.SMEM),
            pl.BlockSpec(memory_space=pltpu.HBM),
            pl.BlockSpec(memory_space=pltpu.HBM),
        ],
        out_specs=[whole(), whole()],
        scratch_shapes=[
            pltpu.VMEM(tokens.shape, BF16),
            pltpu.VMEM(slot_embed.shape, BF16),
            pltpu.VMEM((count, slots), F32),
            pltpu.VMEM((slots, width + TAIL), F32),
            pltpu.SemaphoreType.DMA((parts + 1,)),
        ],
    )(core, far_memory(tokens), far_memory(slot_embed))


def merge_kernel(own, got, out):
    width = own.shape[1] - TAIL
    own_total, own_peak = read_tail(own[:, width:])
    got_total, got_peak = read_tail(got[:, width:].astype(F32))
    top = jnp.maximum(own_peak, got_peak)
    own_scale, got_scale = jnp.exp(own_peak - top), jnp.exp(got_peak - top)
    merged = own[:, :width] * own_scale + got[:, :width].astype(F32) * got_scale
    out[:, :width] = merged.astype(BF16)
    out[:, width:] = tail_of(own_total * own_scale + got_total * got_scale, top).astype(BF16)


def merge(own, got):
    return call(
        merge_kernel,
        kept(own.shape, BF16),
        in_specs=[whole(), whole()],
        out_specs=whole(),
    )(own, got)


def reduce_in_kernel(got, out):
    count, rows = got.shape[0], got.shape[1]
    width = got.shape[2] - TAIL
    tails = [read_tail(got[at, :, width:].astype(F32)) for at in range(count)]
    top = functools.reduce(jnp.maximum, [peak for _, peak in tails])
    total = jnp.zeros((rows, 1), F32)
    summed = jnp.zeros((rows, width), F32)
    for at, (part_total, part_peak) in enumerate(tails):
        scale = jnp.exp(part_peak - top)
        total += part_total * scale
        summed += got[at, :, :width].astype(F32) * scale
    result = (summed / total).astype(BF16)
    for at in range(count):
        out[at] = result


def reduce_in(got, wait_for):
    count, rows, wide = got.shape
    return call(
        after(reduce_in_kernel, 1, len(wait_for)),
        kept((count, rows, wide - TAIL), BF16),
        in_specs=[whole()] + anywhere(len(wait_for)),
        out_specs=whole(),
    )(got, *wait_for)


def expert_kernel(slot_exp, half_at, slots, w_in_any, w_out_any, out, w_in, w_out, sems):
    count, _, hid = w_in.shape
    rows = 2 * slot_exp
    copies = []
    for at in range(count):
        expert = half_at[0] * count + at
        copies.append(
            (
                pltpu.make_async_copy(w_in_any.at[expert], w_in.at[at], sems.at[2 * at]),
                pltpu.make_async_copy(w_out_any.at[expert], w_out.at[at], sems.at[2 * at + 1]),
            )
        )
        for copy in copies[at]:
            copy.start()
    for at in range(0, count, 2):
        here = slice(at * slot_exp, at * slot_exp + rows)
        copies[at][0].wait()
        copies[at + 1][0].wait()
        first = jnp.concatenate([w_in[at], w_in[at + 1]], axis=1)
        hidden = gelu_tanh(jnp.dot(slots[here, :], first, preferred_element_type=F32))
        row = lax.broadcasted_iota(jnp.int32, hidden.shape, 0) // slot_exp
        column = lax.broadcasted_iota(jnp.int32, hidden.shape, 1) // hid
        hidden = jnp.where(row == column, hidden, 0.0).astype(BF16)
        copies[at][1].wait()
        copies[at + 1][1].wait()
        second = jnp.concatenate([w_out[at], w_out[at + 1]], axis=0)
        out[here, :] = jnp.dot(hidden, second, preferred_element_type=F32).astype(out.dtype)


def experts(half_at, slots, w_in, w_out, kind, wait_for=()):
    count = w_in.shape[0] // 2
    return call(
        after(functools.partial(expert_kernel, slots.shape[0] // count), 4, len(wait_for)),
        kept(slots.shape, kind),
        micros=3,
        in_specs=[pl.BlockSpec(memory_space=pltpu.SMEM), whole()]
        + [pl.BlockSpec(memory_space=pltpu.HBM)] * 2
        + anywhere(len(wait_for)),
        out_specs=whole(),
        scratch_shapes=[
            pltpu.VMEM((count,) + w_in.shape[1:], BF16),
            pltpu.VMEM((count,) + w_out.shape[1:], BF16),
            pltpu.SemaphoreType.DMA((2 * count,)),
        ],
    )(half_at, slots, far_memory(w_in), far_memory(w_out), *wait_for)


def add_kernel(across, own, got, out):
    rows, wide = out.shape[1], out.shape[2]
    merged = own[...] + got[...].astype(F32)
    for at in range(out.shape[0]):
        down, along = at // across, at % across
        out[at] = merged[down * rows : (down + 1) * rows, along * wide : (along + 1) * wide].astype(BF16)


def add_and_cut(own, got, down, across, wait_for):
    rows, wide = own.shape[0] // down, own.shape[1] // across
    return call(
        after(functools.partial(add_kernel, across), 2, len(wait_for)),
        kept((down * across, rows, wide), BF16),
        in_specs=[whole(), whole()] + anywhere(len(wait_for)),
        out_specs=whole(),
    )(own, got, *wait_for)


def reduce_mid_kernel(down, got, out):
    across, rows, wide = out.shape[1], out.shape[2], out.shape[3]
    n_down = got.shape[0] // across
    n_wide = out.shape[0] // down
    for y in range(across):
        summed = got[y].astype(F32)
        for x in range(1, n_down):
            summed += got[x * across + y].astype(F32)
        for h in range(down):
            for l in range(n_wide):
                out[h * n_wide + l, y] = summed[
                    h * rows : (h + 1) * rows, l * wide : (l + 1) * wide
                ].astype(BF16)


def reduce_mid(got, across, down, n_wide, wait_for):
    rows, wide = got.shape[1] // down, got.shape[2] // n_wide
    return call(
        after(functools.partial(reduce_mid_kernel, down), 1, 1),
        kept((down * n_wide, across, rows, wide), BF16),
        in_specs=[whole(), pl.BlockSpec(memory_space=pltpu.HBM)],
        out_specs=whole(),
    )(got, far_memory(wait_for))


def reduce_out_kernel(down, got, out):
    n_wide = got.shape[0] // down
    for y in range(got.shape[1]):
        for l in range(n_wide):
            summed = got[l, y].astype(F32)
            for h in range(1, down):
                summed += got[h * n_wide + l, y].astype(F32)
            result = summed.astype(BF16)
            for at in range(out.shape[0]):
                out[at, y * n_wide + l] = result


def reduce_out(got, down, copies):
    n_wide = got.shape[0] // down
    return call(
        functools.partial(reduce_out_kernel, down),
        kept((copies, got.shape[1] * n_wide) + got.shape[2:], BF16),
        in_specs=[whole()],
        out_specs=whole(),
    )(got)


def combine_kernel(pieces, core, tok_own, tok_other, *refs):
    own, other = refs[: pieces // 2], refs[pieces // 2 : pieces]
    weights, total, logits, table_own, table_other, sems = refs[pieces:]

    def copies():
        at = 0
        for to, which in ((table_own, own), (table_other, other)):
            start = 0
            for piece in which:
                here = pl.ds(start, piece.shape[0])
                yield start, pltpu.make_async_copy(piece, to.at[here], sems.at[at])
                start += piece.shape[0]
                at += 1

    @pl.when(pl.program_id(0) == 0)
    def _():
        started = [copy for _, copy in copies()]
        for copy in started:
            copy.start()
        for copy in started:
            copy.wait()

    peak = None
    wide = table_own.shape[2]
    for at in range(table_own.shape[0]):
        block = jnp.dot(tok_own[...], table_own[at], preferred_element_type=F32)
        block += jnp.dot(tok_other[...], table_other[at], preferred_element_type=F32)
        logits[:, at * wide : (at + 1) * wide] = block
        top = jnp.max(block, axis=1, keepdims=True)
        peak = top if peak is None else jnp.maximum(peak, top)
    sums = jnp.zeros_like(peak)
    for at in range(table_own.shape[0]):
        here = slice(at * wide, (at + 1) * wide)
        block = jnp.exp(logits[:, here] - peak)
        weights[:, here] = block.astype(BF16)
        sums += jnp.sum(block, axis=1, keepdims=True)
    total[...] = jnp.broadcast_to(sums, total.shape)


def combine_weights(core, tokens, own, other, wait_for, steps=8):
    count, width = tokens.shape
    blocks = sum(piece.shape[0] for piece in own)
    depth, wide = own[0].shape[1:]
    slots = blocks * wide
    rows = count // steps
    pieces = own + other
    tokens = far_memory(tokens)
    return call(
        after(functools.partial(combine_kernel, len(pieces)), 3 + len(pieces), 1),
        [pltpu.HBM((count, slots), BF16), pltpu.HBM((count, 128), F32)],
        micros=12,
        grid_spec=pltpu.PrefetchScalarGridSpec(
            num_scalar_prefetch=1,
            grid=(steps,),
            in_specs=[
                pl.BlockSpec((rows, width // 2), lambda i, core: (i, core[0])),
                pl.BlockSpec((rows, width // 2), lambda i, core: (i, 1 - core[0])),
            ]
            + anywhere(len(pieces) + 1),
            out_specs=[
                pl.BlockSpec((rows, slots), lambda i, core: (i, 0)),
                pl.BlockSpec((rows, 128), lambda i, core: (i, 0)),
            ],
            scratch_shapes=[
                pltpu.VMEM((rows, slots), F32),
                pltpu.VMEM((blocks, depth, wide), BF16),
                pltpu.VMEM((blocks, depth, wide), BF16),
                pltpu.SemaphoreType.DMA((len(pieces),)),
            ],
        ),
    )(core, tokens, tokens, *pieces, wait_for)


def output_kernel(place, weights, total, own, other, out, table):
    half = own.shape[0] * own.shape[2]
    groups = own.shape[1]

    @pl.when(pl.program_id(0) == 0)
    def _():
        for at in range(groups):
            group = place[1 + at]
            for rows, start in ((own, place[0]), (other, 1 - place[0])):
                block = rows[:, group].astype(F32).reshape(half, own.shape[3])
                here = pl.multiple_of(at * 2 * half + start * half, half)
                table[pl.ds(here, half), :] = block.astype(BF16)

    mixed = jnp.dot(weights[...], table[...], preferred_element_type=F32)
    out[...] = (mixed / total[...]).astype(BF16)


def output(place, weights, total, own, other, steps=5):
    count, slots = weights.shape
    wide = own.shape[3]
    return call(
        output_kernel,
        jax.ShapeDtypeStruct((count, wide), BF16),
        grid=(steps,),
        in_specs=[
            pl.BlockSpec(memory_space=pltpu.SMEM),
            pl.BlockSpec((count // steps, slots), lambda i: (i, 0)),
            pl.BlockSpec((count // steps, wide), lambda i: (i, 0)),
            whole(),
            whole(),
        ],
        out_specs=pl.BlockSpec((count // steps, wide), lambda i: (i, 0)),
        scratch_shapes=[pltpu.VMEM((slots, wide), BF16)],
    )(place, far_memory(weights), far_memory(total), own, other)


def shift(by):
    return [(i, (i + by) % 4) for i in range(4)]


def on_device(tokens, slot_embed, w_in, w_out):
    count, features = tokens.shape
    slots = slot_embed.shape[1]
    core = lax.axis_index("core").reshape(1)
    y, zl = lax.axis_index("y"), lax.axis_index("zl")
    nx, nh, ny, nl = (lax.axis_size(axis) for axis in ("x", "zh", "y", "zl"))
    half = slots // 2
    part = half // (nx * nh)

    mine = lax.dynamic_slice_in_dim(slot_embed, core[0] * (features // 2), features // 2, 0)
    near = lax.ppermute(mine, "zl", SWAP)
    rows_y = jnp.stack([y, y, y - 1, y - 1, y + 1, y + 1, y + 2, y + 2]) % ny
    rows_l = jnp.stack([zl, 1 - zl] * 4)
    place = jnp.concatenate([core, rows_y * nl + rows_l]).astype(jnp.int32)

    own, send = dispatch(core, tokens, slot_embed)
    merged = merge(own, lax.ppermute(send, "core", SWAP))
    here = jnp.stack([mine, near])
    down = lax.ppermute(here, "y", shift(1))
    up = lax.ppermute(here, "y", shift(-1))
    got = lax.all_to_all(merged.reshape(nx * nh, part, -1), ("x", "zh"), 0, 0)
    spread = reduce_in(got, [down, up])
    far = [lax.ppermute(down[:1], "y", shift(1)), lax.ppermute(up[1:], "y", shift(-1))]
    near_table = [here, down, up]
    near_there = [lax.ppermute(piece, "core", SWAP) for piece in near_table]
    slots_own = lax.all_to_all(spread, ("x", "zh"), 0, 0).reshape(half, features)
    slots_other = lax.ppermute(slots_own, "core", SWAP)

    done_own = experts(core, slots_own, w_in, w_out, F32, far + near_there)
    done_other = experts(1 - core, slots_other, w_in, w_out, BF16)
    far_there = [lax.ppermute(piece, "core", SWAP) for piece in far]
    cut = add_and_cut(done_own, lax.ppermute(done_other, "core", SWAP), nx, ny, far_there)

    weights, total = combine_weights(core, tokens, near_table + far, near_there + far_there, cut)

    got = lax.all_to_all(cut, ("x", "y"), 0, 0)
    got = lax.all_to_all(reduce_mid(got, ny, nh, nl, weights), ("zh", "zl"), 0, 0)
    spread = reduce_out(got, nh, nx * nh)
    out_own = lax.all_to_all(spread, ("x", "zh"), 0, 0)
    out_other = lax.ppermute(out_own, "core", SWAP)
    return output(place, weights, total, out_own, out_other)


def solution(mesh):
    grid = Mesh(mesh.devices.reshape(4, 4, 2, 4, 2), ("x", "zh", "core", "y", "zl"))
    placed = (P(SEQ, None), P(None, EXP), P(EXP, None, SEQ), P(EXP, SEQ, None))
    return jax.shard_map(
        on_device, mesh=grid, in_specs=placed, out_specs=P(SEQ, EXP), check_vma=False
    )
```

time: 605 us -> 136 us (0.22)
  blocking collectives: 477 us -> 13.4 us
  waiting for transfers between devices: 87.5 us -> 31.3 us
  starting transfers between devices: 0.01 us -> 45.4 us
  Pallas kernels: 0 us -> 40.7 us
  matrix products: 16.2 us -> 0 us
  between operations: 13.4 us -> 0.19 us
    psum x4 -> x0, blocking collectives: 388 us -> none  [the longest x1 149 us: on_device(): slot_out = lax.psum(partial_out, 'seq').astype(jnp.bfloat16)]
    pmax x2 -> x0, blocking collectives: 89.4 us -> none  [the longest x1 73.4 us: on_device(): peak_all = lax.pmax(col_peak, 'seq')]
    unnamed x2 -> x0, waiting for transfers between devices: 87.5 us -> none
    pallas_call x0 -> x10, Pallas kernels: none -> 40.7 us  [the longest x1 16 us: combine_weights(): call(after(functools.partial(combine_kernel, len(pieces)), 3 + len(pieces...]
    all_to_all x0 -> x4, starting transfers between devices: none -> 26.5 us  [the longest x1 9.01 us: on_device(): got = lax.all_to_all(merged.reshape(nx * nh, part, -1), ('x', 'zh'), 0, 0)]
    ppermute x0 -> x14, starting transfers between devices: none -> 18.9 us  [the longest x1 3.33 us: on_device(): merged = merge(own, lax.ppermute(send, 'core', SWAP))]
    all_to_all x0 -> x4, waiting for transfers between devices: none -> 16.7 us  [the longest x1 11.5 us: on_device(): out_own = lax.all_to_all(spread, ('x', 'zh'), 0, 0)]
    dot_general x4 -> x0, matrix products: 16.2 us -> none  [the longest x1 4.74 us: on_device(): term = jnp.dot(combine, slot_out, preferred_element_type=jnp.float32)]
  transfers between devices with their start and end apart: 1 -> 18, of which waited for: 1 -> 6; matrix products, arithmetic and copies ran while one was open for 0% -> 1% of each run, Pallas kernels for 0% -> 18%
where the time goes in v2:
time: 136 us; the launch traced here: 135 us
  starting transfers between devices  45.4 us (33%)
  Pallas kernels  40.7 us (30%)
  waiting for transfers between devices  31.3 us (23%)
  blocking collectives  13.4 us (10%)
  local copies, waits for them, and re-layouts  4.27 us (3%)
    pallas_call x1, Pallas kernels, combine_weights(): call(after(functools.partial(combine_kernel, len(pieces)), 3 + len(pieces...  16 us
    all_to_all x1, blocking collectives, on_device(): lax.all_to_all(reduce_mid(got, ny, nh, nl, weights), ('zh', 'zl'), 0, 0)  13.4 us
    all_to_all x1, waiting for transfers between devices, on_device(): out_own = lax.all_to_all(spread, ('x', 'zh'), 0, 0)  11.5 us
    ppermute x1, waiting for transfers between devices, on_device(): down = lax.ppermute(here, 'y', shift(1))  11.3 us
    all_to_all x1, starting transfers between devices, on_device(): got = lax.all_to_all(merged.reshape(nx * nh, part, -1), ('x', 'zh'), 0, 0)  9.01 us
    all_to_all x1, starting transfers between devices, on_device(): lax.all_to_all(spread, ('x', 'zh'), 0, 0).reshape(half, features)  8.79 us
    pallas_call x2, Pallas kernels, experts(): call(after(functools.partial(expert_kernel, slots.shape[0] // count), 4,...  7.69 us
    pallas_call x1, Pallas kernels, output(): call(output_kernel, jax.ShapeDtypeStruct((count, wide), BF16), grid=(step...  6.93 us
  transfers between devices with their start and end apart: 18, of which 6 were waited for; matrix products, arithmetic and copies ran while one was open for 1% of the time, Pallas kernels for 18%

profile of v2, /device:TPU:1, one launch (start us, length us, event | category | flops | bytes accessed | tf_op | source)
XLA Modules:
  0.0 135.4 jit_solution(6665524751665157052)
XLA Ops:
  0.0 5.5 %shard_map.46 = (f32[128,1152]{1,0:T(8,128)S(1)}, bf16[128,1152]{1,0:T(8,128)(2,1)S(1)}) custom-call(s32[1]{0:T(128)} %bitcast.core.refs_0_, bf16[1920,1024]{1,0:T(8,128)(2,1)} %refs_2_.5, bf16[1024,256]{1,0:T(8,128)(2,1)} %embed_any.1), custom_call_target="tpu_custom_call" | custom-call | bytes 18000000 | tf_op jit(solution)/shard_map/pallas_call | solution.py:119
  5.5 3.3 %collective-permute-start.10 = (bf16[128,1152]{1,0:T(8,128)(2,1)S(1)}, bf16[128,1152]{1,0:T(8,128)(2,1)S(1)}, u32[]{:S(2)}, u32[]{:S(2)}) collective-permute-start(bf16[128,1152]{1,0:T(8,128)(2,1)S(1)} %get-tuple-element.10), channel_id=1, source_target_pairs={{0,8},{8,0},{1,9},{9,1},{2,10},{10,2},{3,11},{11,3},{4,12},{12,4},... | collective-permute-start | bytes 884744 | tf_op jit(solution)/shard_map/ppermute | solution.py:426
  8.8 0.1 collective-permute-start
  9.0 1.0 collective-permute-done.10.got
  10.0 1.1 shard_map.47
  11.1 9.0 %all-to-all-start = ((bf16[16,8,1152]{2,1,0:T(8,128)(2,1)}), bf16[16,8,1152]{2,1,0:T(8,128)(2,1)S(1)}, u32[]{:S(2)}, u32[]{:S(2)}) async-start(bf16[16,8,1152]{2,1,0:T(8,128)(2,1)} %bitcast.9), calls=%async_computation | async-start | bytes 589824 | tf_op jit(solution)/shard_map/all_to_all | solution.py:430
  20.2 0.1 pad_maximum_fusion.refs_3_
  20.2 1.4 %collective-permute-start.1 = (bf16[2,512,256]{2,1,0:T(8,128)(2,1)S(1)}, bf16[2,512,256]{2,1,0:T(8,128)(2,1)S(1)}, u32[]{:S(2)}, u32[]{:S(2)}) collective-permute-start(bf16[2,512,256]{2,1,0:T(8,128)(2,1)S(1)} %pad_maximum_fusion.refs_3_), channel_id=1, source_target_pairs={{0,2},{2,4},{4,6},{6,0},{1,3},{3,5},{5,7},{7,1},{8,10},{10,12},{12... | collective-permute-start | bytes 1572872 | tf_op jit(solution)/shard_map/ppermute | solution.py:428
  21.6 1.5 %collective-permute-start.2 = (bf16[2,512,256]{2,1,0:T(8,128)(2,1)S(1)}, bf16[2,512,256]{2,1,0:T(8,128)(2,1)S(1)}, u32[]{:S(2)}, u32[]{:S(2)}) collective-permute-start(bf16[2,512,256]{2,1,0:T(8,128)(2,1)S(1)} %pad_maximum_fusion.refs_3_), channel_id=1, source_target_pairs={{0,6},{2,0},{4,2},{6,4},{1,7},{3,1},{5,3},{7,5},{8,14},{10,8},{12,... | collective-permute-start | bytes 1572872 | tf_op jit(solution)/shard_map/ppermute | solution.py:429
  23.1 11.3 %collective-permute-done.1.refs_1_.refs_4_ = bf16[2,512,256]{2,1,0:T(8,128)(2,1)S(1)} collective-permute-done((bf16[2,512,256]{2,1,0:T(8,128)(2,1)S(1)}, bf16[2,512,256]{2,1,0:T(8,128)(2,1)S(1)}, u32[]{:S(2)}, u32[]{:S(2)}) %collective-permute-start.1) | collective-permute-done | bytes 524320 | tf_op jit(solution)/shard_map/ppermute | solution.py:428
  34.5 0.0 collective-permute-done.2.refs_2_.refs_5_
  34.5 0.0 all-to-all-done.refs_0_
  34.5 1.0 shard_map.48
  35.4 8.8 %all-to-all-start.1 = ((bf16[16,8,1024]{2,1,0:T(8,128)(2,1)}), bf16[16,8,1024]{2,1,0:T(8,128)(2,1)}, u32[]{:S(2)}, u32[]{:S(2)}) async-start(bf16[16,8,1024]{2,1,0:T(8,128)(2,1)} %shard_map.48), calls=%async_computation.1 | async-start | bytes 524288 | tf_op jit(solution)/shard_map/all_to_all | solution.py:435
  44.3 1.0 collective-permute-start.3
  45.3 2.7 %collective-permute-start.5 = (bf16[2,512,256]{2,1,0:T(8,128)(2,1)S(1)}, bf16[2,512,256]{2,1,0:T(8,128)(2,1)S(1)}, u32[]{:S(2)}, u32[]{:S(2)}) collective-permute-start(bf16[2,512,256]{2,1,0:T(8,128)(2,1)S(1)} %pad_maximum_fusion.refs_3_), channel_id=1, source_target_pairs={{0,8},{8,0},{1,9},{9,1},{2,10},{10,2},{3,11},{11,3},{4,12},{12,4},... | collective-permute-start | bytes 1572872 | tf_op jit(solution)/shard_map/ppermute | solution.py:434
  48.0 0.7 slice.9
  48.7 1.4 %collective-permute-start.4 = (bf16[1,512,256]{2,1,0:T(8,128)(2,1)}, bf16[1,512,256]{2,1,0:T(8,128)(2,1)}, u32[]{:S(2)}, u32[]{:S(2)}) collective-permute-start(bf16[1,512,256]{2,1,0:T(8,128)(2,1)} %slice.9), channel_id=1, source_target_pairs={{0,6},{2,0},{4,2},{6,4},{1,7},{3,1},{5,3},{7,5},{8,14},{10,8},{12,... | collective-permute-start | bytes 786440 | tf_op jit(solution)/shard_map/ppermute | solution.py:432
  50.1 0.3 collective-permute-start.6
  50.4 5.2 %all-to-all-done.1 = bf16[16,8,1024]{2,1,0:T(8,128)(2,1)} async-done(((bf16[16,8,1024]{2,1,0:T(8,128)(2,1)}), bf16[16,8,1024]{2,1,0:T(8,128)(2,1)}, u32[]{:S(2)}, u32[]{:S(2)}) %all-to-all-start.1) | async-done | bytes 262176 | tf_op jit(solution)/shard_map/all_to_all | solution.py:435
  55.6 3.1 %collective-permute-start.11 = (bf16[128,1024]{1,0:T(8,128)(2,1)}, bf16[128,1024]{1,0:T(8,128)(2,1)S(1)}, u32[]{:S(2)}, u32[]{:S(2)}) collective-permute-start(bf16[128,1024]{1,0:T(8,128)(2,1)} %bitcast.10.refs_1_), channel_id=1, source_target_pairs={{0,8},{8,0},{1,9},{9,1},{2,10},{10,2},{3,11},{11,3},{4,12},{12,4},... | collective-permute-start | bytes 786440 | tf_op jit(solution)/shard_map/ppermute | solution.py:436
  58.7 0.0 collective-permute-done.3.refs_4_.refs_6_
  58.7 0.0 collective-permute-start.7
  58.7 0.5 collective-permute-start.8
  59.2 1.1 collective-permute-done.11.refs_1_
  60.4 0.4 collective-permute-start.9
  60.7 3.4 %shard_map.50 = bf16[128,1024]{1,0:T(8,128)(2,1)S(1)} custom-call(s32[1]{0:T(128)S(6)} %sub.12.refs_0_, bf16[128,1024]{1,0:T(8,128)(2,1)S(1)} %collective-permute-done.11.refs_1_, bf16[16,1024,128]{2,1,0:T(8,128)(2,1)} %refs_2_.4, bf16[16,128,1024]{2,1,0:T(8,128)(2,1)} %refs_3_.3), custom_call_target="tpu_custom_call" | custom-call | bytes 9000000 | tf_op jit(solution)/shard_map/pallas_call | solution.py:216
  64.1 0.2 collective-permute-start.12
  64.4 4.3 %shard_map.49.refs_0_ = f32[128,1024]{1,0:T(8,128)S(1)} custom-call(s32[1]{0:T(128)} %bitcast.core.refs_0_, bf16[128,1024]{1,0:T(8,128)(2,1)} %bitcast.10.refs_1_, bf16[16,1024,128]{2,1,0:T(8,128)(2,1)} %refs_2_.4, bf16[16,128,1024]{2,1,0:T(8,128)(2,1)} %refs_3_.3, bf16[1,512,256]{2,1,0:T(8,128)(2,1)S(1)} %collective-permute-done.3.refs_4_.refs_6_, ...), custom_call_target="tpu_custom_call" | custom-call | bytes 9000000 | tf_op jit(solution)/shard_map/pallas_call | solution.py:216
  68.7 0.8 shard_map.51.refs_13_
  69.5 0.7 copy-done
  70.2 0.7 copy-done.2
  70.9 4.3 %all-to-all-start.2 = ((bf16[16,32,256]{2,1,0:T(8,128)(2,1)}), bf16[16,32,256]{2,1,0:T(8,128)(2,1)}, u32[]{:S(2)}, u32[]{:S(2)}) async-start(bf16[16,32,256]{2,1,0:T(8,128)(2,1)} %shard_map.51.refs_13_), calls=%async_computation.2 | async-start | bytes 524288 | tf_op jit(solution)/shard_map/all_to_all | solution.py:445
  75.2 0.0 copy-start.1
  75.2 0.9 copy-done.1
  76.1 0.9 copy-done.3
  77.1 16.0 %shard_map.52 = (bf16[1920,2048]{1,0:T(8,128)(2,1)}, f32[1920,128]{1,0:T(8,128)}) custom-call(s32[1]{0:T(128)} %bitcast.core.refs_0_, bf16[1920,1024]{1,0:T(8,128)(2,1)} %refs_2_.5, bf16[1920,1024]{1,0:T(8,128)(2,1)} %refs_2_.5, bf16[2,512,256]{2,1,0:T(8,128)(2,1)S(1)} %pad_maximum_fusion.refs_3_, ...), custom_call_target="tpu_custom_call" | custom-call | bytes 36000000 | tf_op jit(solution)/shard_map/pallas_call | solution.py:344
  93.1 1.0 shard_map.53
  94.1 13.4 %all_to_all.25.got = bf16[8,4,8,128]{3,2,1,0:T(8,128)(2,1)S(1)} all-to-all(bf16[8,4,8,128]{3,2,1,0:T(8,128)(2,1)S(1)} %shard_map.53), channel_id=1, replica_groups=mesh['x'=4,'zh'=4,'core'=2,'y'=4,'zl'=2] {'zh','zl'}, dimensions={0} | all-to-all | bytes 131072 | tf_op jit(solution)/shard_map/all_to_all | solution.py:446
  107.5 0.8 shard_map.54
  108.2 4.5 %all-to-all-start.4 = ((bf16[16,8,8,128]{3,2,1,0:T(8,128)(2,1)}), bf16[16,8,8,128]{3,2,1,0:T(8,128)(2,1)S(1)}, u32[]{:S(2)}, u32[]{:S(2)}) async-start(bf16[16,8,8,128]{3,2,1,0:T(8,128)(2,1)} %shard_map.54), calls=%async_computation.4 | async-start | bytes 524288 | tf_op jit(solution)/shard_map/all_to_all | solution.py:448
  112.7 0.1 stack.50
  112.8 0.1 stack.47
  112.9 11.5 %all-to-all-done.4.own = bf16[16,8,8,128]{3,2,1,0:T(8,128)(2,1)S(1)} async-done(((bf16[16,8,8,128]{3,2,1,0:T(8,128)(2,1)}), bf16[16,8,8,128]{3,2,1,0:T(8,128)(2,1)S(1)}, u32[]{:S(2)}, u32[]{:S(2)}) %all-to-all-start.4) | async-done | bytes 262176 | tf_op jit(solution)/shard_map/all_to_all | solution.py:448
  124.4 2.9 %collective-permute-start.13 = (bf16[16,8,8,128]{3,2,1,0:T(8,128)(2,1)S(1)}, bf16[16,8,8,128]{3,2,1,0:T(8,128)(2,1)S(1)}, u32[]{:S(2)}, u32[]{:S(2)}) collective-permute-start(bf16[16,8,8,128]{3,2,1,0:T(8,128)(2,1)S(1)} %all-to-all-done.4.own), channel_id=1, source_target_pairs={{0,8},{8,0},{1,9},{9,1},{2,10},{10,2},{3,11},{11,3},{4,12},{12,4},... | collective-permute-start | bytes 786440 | tf_op jit(solution)/shard_map/ppermute | solution.py:449
  127.3 0.1 pad_add_fusion.place
  127.4 1.1 collective-permute-done.13.other
  128.5 6.9 %shard_map.55 = bf16[1920,128]{1,0:T(8,128)(2,1)} custom-call(s32[9]{0:T(128)S(1)} %pad_add_fusion.place, bf16[1920,2048]{1,0:T(8,128)(2,1)} %get-tuple-element.11.refs_1_.weights, f32[1920,128]{1,0:T(8,128)} %get-tuple-element.12.total, bf16[16,8,8,128]{3,2,1,0:T(8,128)(2,1)S(1)} %all-to-all-done.4.own, ...), custom_call_target="tpu_custom_call" | custom-call | bytes 3000000 | tf_op jit(solution)/shard_map/pallas_call | solution.py:390
  (18 shorter events, 0.1 us)
Async XLA Ops:
  0.0 8.8 %copy-start.4 = (bf16[1024,256]{1,0:T(8,128)(2,1)S(1)}, bf16[1024,256]{1,0:T(8,128)(2,1)}, u32[]{:S(2)}) copy-start(bf16[1024,256]{1,0:T(8,128)(2,1)} %embed_any.1) | copy-start | bytes 1572868
  5.5 4.5 %collective-permute-start.10 = (bf16[128,1152]{1,0:T(8,128)(2,1)S(1)}, bf16[128,1152]{1,0:T(8,128)(2,1)S(1)}, u32[]{:S(2)}, u32[]{:S(2)}) collective-permute-start(bf16[128,1152]{1,0:T(8,128)(2,1)S(1)} %get-tuple-element.10), channel_id=1, source_target_pairs={{0,8},{8,0},{1,9},{9,1},{2,10},{10,2},{3,11},{11,3},{4,12},{12,4},... | collective-permute-start | bytes 884744 | tf_op jit(solution)/shard_map/ppermute | solution.py:426
  8.8 11.3 %collective-permute-start = (bf16[512,256]{1,0:T(8,128)(2,1)S(1)}, bf16[512,256]{1,0:T(8,128)(2,1)S(1)}, u32[]{:S(2)}, u32[]{:S(2)}) collective-permute-start(bf16[512,256]{1,0:T(8,128)(2,1)S(1)} %constant_dynamic-slice_fusion), channel_id=1, source_target_pairs={{0,1},{1,0},{2,3},{3,2},{4,5},{5,4},{6,7},{7,6},{8,9},{9,8},{10,11... | collective-permute-start | bytes 786440 | tf_op jit(solution)/shard_map/ppermute | solution.py:420
  11.1 23.3 %all-to-all-start = ((bf16[16,8,1152]{2,1,0:T(8,128)(2,1)}), bf16[16,8,1152]{2,1,0:T(8,128)(2,1)S(1)}, u32[]{:S(2)}, u32[]{:S(2)}) async-start(bf16[16,8,1152]{2,1,0:T(8,128)(2,1)} %bitcast.9), calls=%async_computation | async-start | bytes 589824 | tf_op jit(solution)/shard_map/all_to_all | solution.py:430
  20.2 14.2 %collective-permute-start.1 = (bf16[2,512,256]{2,1,0:T(8,128)(2,1)S(1)}, bf16[2,512,256]{2,1,0:T(8,128)(2,1)S(1)}, u32[]{:S(2)}, u32[]{:S(2)}) collective-permute-start(bf16[2,512,256]{2,1,0:T(8,128)(2,1)S(1)} %pad_maximum_fusion.refs_3_), channel_id=1, source_target_pairs={{0,2},{2,4},{4,6},{6,0},{1,3},{3,5},{5,7},{7,1},{8,10},{10,12},{12... | collective-permute-start | bytes 1572872 | tf_op jit(solution)/shard_map/ppermute | solution.py:428
  21.6 12.9 %collective-permute-start.2 = (bf16[2,512,256]{2,1,0:T(8,128)(2,1)S(1)}, bf16[2,512,256]{2,1,0:T(8,128)(2,1)S(1)}, u32[]{:S(2)}, u32[]{:S(2)}) collective-permute-start(bf16[2,512,256]{2,1,0:T(8,128)(2,1)S(1)} %pad_maximum_fusion.refs_3_), channel_id=1, source_target_pairs={{0,6},{2,0},{4,2},{6,4},{1,7},{3,1},{5,3},{7,5},{8,14},{10,8},{12,... | collective-permute-start | bytes 1572872 | tf_op jit(solution)/shard_map/ppermute | solution.py:429
  35.4 20.1 %all-to-all-start.1 = ((bf16[16,8,1024]{2,1,0:T(8,128)(2,1)}), bf16[16,8,1024]{2,1,0:T(8,128)(2,1)}, u32[]{:S(2)}, u32[]{:S(2)}) async-start(bf16[16,8,1024]{2,1,0:T(8,128)(2,1)} %shard_map.48), calls=%async_computation.1 | async-start | bytes 524288 | tf_op jit(solution)/shard_map/all_to_all | solution.py:435
  44.3 14.4 %collective-permute-start.3 = (bf16[1,512,256]{2,1,0:T(8,128)(2,1)S(1)}, bf16[1,512,256]{2,1,0:T(8,128)(2,1)S(1)}, u32[]{:S(2)}, u32[]{:S(2)}) collective-permute-start(bf16[1,512,256]{2,1,0:T(8,128)(2,1)S(1)} %slice.8), channel_id=1, source_target_pairs={{0,2},{2,4},{4,6},{6,0},{1,3},{3,5},{5,7},{7,1},{8,10},{10,12},{12... | collective-permute-start | bytes 786440 | tf_op jit(solution)/shard_map/ppermute | solution.py:432
  45.3 18.8 %collective-permute-start.5 = (bf16[2,512,256]{2,1,0:T(8,128)(2,1)S(1)}, bf16[2,512,256]{2,1,0:T(8,128)(2,1)S(1)}, u32[]{:S(2)}, u32[]{:S(2)}) collective-permute-start(bf16[2,512,256]{2,1,0:T(8,128)(2,1)S(1)} %pad_maximum_fusion.refs_3_), channel_id=1, source_target_pairs={{0,8},{8,0},{1,9},{9,1},{2,10},{10,2},{3,11},{11,3},{4,12},{12,4},... | collective-permute-start | bytes 1572872 | tf_op jit(solution)/shard_map/ppermute | solution.py:434
  48.7 10.0 %collective-permute-start.4 = (bf16[1,512,256]{2,1,0:T(8,128)(2,1)}, bf16[1,512,256]{2,1,0:T(8,128)(2,1)}, u32[]{:S(2)}, u32[]{:S(2)}) collective-permute-start(bf16[1,512,256]{2,1,0:T(8,128)(2,1)} %slice.9), channel_id=1, source_target_pairs={{0,6},{2,0},{4,2},{6,4},{1,7},{3,1},{5,3},{7,5},{8,14},{10,8},{12,... | collective-permute-start | bytes 786440 | tf_op jit(solution)/shard_map/ppermute | solution.py:432
  50.1 14.3 %collective-permute-start.6 = (bf16[2,512,256]{2,1,0:T(8,128)(2,1)S(1)}, bf16[2,512,256]{2,1,0:T(8,128)(2,1)S(1)}, u32[]{:S(2)}, u32[]{:S(2)}) collective-permute-start(bf16[2,512,256]{2,1,0:T(8,128)(2,1)S(1)} %collective-permute-done.1.refs_1_.refs_4_), channel_id=1, source_target_pairs={{0,8},{8,0},{1,9},{9,1},{2,10},{10,2},{3,11},{11,3},{4,12},{12,4},... | collective-permute-start | bytes 1572872 | tf_op jit(solution)/shard_map/ppermute | solution.py:434
  55.6 4.8 %collective-permute-start.11 = (bf16[128,1024]{1,0:T(8,128)(2,1)}, bf16[128,1024]{1,0:T(8,128)(2,1)S(1)}, u32[]{:S(2)}, u32[]{:S(2)}) collective-permute-start(bf16[128,1024]{1,0:T(8,128)(2,1)} %bitcast.10.refs_1_), channel_id=1, source_target_pairs={{0,8},{8,0},{1,9},{9,1},{2,10},{10,2},{3,11},{11,3},{4,12},{12,4},... | collective-permute-start | bytes 786440 | tf_op jit(solution)/shard_map/ppermute | solution.py:436
  58.7 5.7 %collective-permute-start.7 = (bf16[2,512,256]{2,1,0:T(8,128)(2,1)S(1)}, bf16[2,512,256]{2,1,0:T(8,128)(2,1)S(1)}, u32[]{:S(2)}, u32[]{:S(2)}) collective-permute-start(bf16[2,512,256]{2,1,0:T(8,128)(2,1)S(1)} %collective-permute-done.2.refs_2_.refs_5_), channel_id=1, source_target_pairs={{0,8},{8,0},{1,9},{9,1},{2,10},{10,2},{3,11},{11,3},{4,12},{12,4},... | collective-permute-start | bytes 1572872 | tf_op jit(solution)/shard_map/ppermute | solution.py:434
  58.7 10.0 %collective-permute-start.8 = (bf16[1,512,256]{2,1,0:T(8,128)(2,1)S(1)}, bf16[1,512,256]{2,1,0:T(8,128)(2,1)S(1)}, u32[]{:S(2)}, u32[]{:S(2)}) collective-permute-start(bf16[1,512,256]{2,1,0:T(8,128)(2,1)S(1)} %collective-permute-done.3.refs_4_.refs_6_), channel_id=1, source_target_pairs={{0,8},{8,0},{1,9},{9,1},{2,10},{10,2},{3,11},{11,3},{4,12},{12,4},... | collective-permute-start | bytes 786440 | tf_op jit(solution)/shard_map/ppermute | solution.py:440
  60.4 8.3 %collective-permute-start.9 = (bf16[1,512,256]{2,1,0:T(8,128)(2,1)}, bf16[1,512,256]{2,1,0:T(8,128)(2,1)S(1)}, u32[]{:S(2)}, u32[]{:S(2)}) collective-permute-start(bf16[1,512,256]{2,1,0:T(8,128)(2,1)} %collective-permute-done.4.refs_5_.refs_7_), channel_id=1, source_target_pairs={{0,8},{8,0},{1,9},{9,1},{2,10},{10,2},{3,11},{11,3},{4,12},{12,4},... | collective-permute-start | bytes 786440 | tf_op jit(solution)/shard_map/ppermute | solution.py:440
  64.1 4.6 %collective-permute-start.12 = (bf16[128,1024]{1,0:T(8,128)(2,1)S(1)}, bf16[128,1024]{1,0:T(8,128)(2,1)S(1)}, u32[]{:S(2)}, u32[]{:S(2)}) collective-permute-start(bf16[128,1024]{1,0:T(8,128)(2,1)S(1)} %shard_map.50), channel_id=1, source_target_pairs={{0,8},{8,0},{1,9},{9,1},{2,10},{10,2},{3,11},{11,3},{4,12},{12,4},... | collective-permute-start | bytes 786440 | tf_op jit(solution)/shard_map/ppermute | solution.py:441
  69.5 0.7 copy-start
  70.2 0.7 copy-start.2
  70.9 22.2 %all-to-all-start.2 = ((bf16[16,32,256]{2,1,0:T(8,128)(2,1)}), bf16[16,32,256]{2,1,0:T(8,128)(2,1)}, u32[]{:S(2)}, u32[]{:S(2)}) async-start(bf16[16,32,256]{2,1,0:T(8,128)(2,1)} %shard_map.51.refs_13_), calls=%async_computation.2 | async-start | bytes 524288 | tf_op jit(solution)/shard_map/all_to_all | solution.py:445
  75.2 1.0 copy-start.1
  76.1 0.9 copy-start.3
  108.2 16.1 %all-to-all-start.4 = ((bf16[16,8,8,128]{3,2,1,0:T(8,128)(2,1)}), bf16[16,8,8,128]{3,2,1,0:T(8,128)(2,1)S(1)}, u32[]{:S(2)}, u32[]{:S(2)}) async-start(bf16[16,8,8,128]{3,2,1,0:T(8,128)(2,1)} %shard_map.54), calls=%async_computation.4 | async-start | bytes 524288 | tf_op jit(solution)/shard_map/all_to_all | solution.py:448
  124.4 4.1 %collective-permute-start.13 = (bf16[16,8,8,128]{3,2,1,0:T(8,128)(2,1)S(1)}, bf16[16,8,8,128]{3,2,1,0:T(8,128)(2,1)S(1)}, u32[]{:S(2)}, u32[]{:S(2)}) collective-permute-start(bf16[16,8,8,128]{3,2,1,0:T(8,128)(2,1)S(1)} %all-to-all-done.4.own), channel_id=1, source_target_pairs={{0,8},{8,0},{1,9},{9,1},{2,10},{10,2},{3,11},{11,3},{4,12},{12,4},... | collective-permute-start | bytes 786440 | tf_op jit(solution)/shard_map/ppermute | solution.py:449

commit v3 on v2

--- a/solution.py
+++ b/solution.py
@@ -45,7 +45,7 @@
         out_shape=outs,
         compiler_params=pltpu.CompilerParams(vmem_limit_bytes=limit),
         cost_estimate=pl.CostEstimate(
-            flops=0, bytes_accessed=micros * 3_000_000, transcendentals=0
+            flops=0, bytes_accessed=micros * 30_000, transcendentals=0
         ),
         **more,
     )
@@ -196,19 +196,23 @@
         )
         for copy in copies[at]:
             copy.start()
-    for at in range(0, count, 2):
+    pairs = range(0, count, 2)
+    for at in range(count):
+        copies[at][0].wait()
+    before = []
+    for at in pairs:
+        first = jnp.concatenate([w_in[at], w_in[at + 1]], axis=1)
         here = slice(at * slot_exp, at * slot_exp + rows)
-        copies[at][0].wait()
-        copies[at + 1][0].wait()
-        first = jnp.concatenate([w_in[at], w_in[at + 1]], axis=1)
-        hidden = gelu_tanh(jnp.dot(slots[here, :], first, preferred_element_type=F32))
-        row = lax.broadcasted_iota(jnp.int32, hidden.shape, 0) // slot_exp
-        column = lax.broadcasted_iota(jnp.int32, hidden.shape, 1) // hid
-        hidden = jnp.where(row == column, hidden, 0.0).astype(BF16)
+        before.append(jnp.dot(slots[here, :], first, preferred_element_type=F32))
+    row = lax.broadcasted_iota(jnp.int32, before[0].shape, 0) // slot_exp
+    column = lax.broadcasted_iota(jnp.int32, before[0].shape, 1) // hid
+    hidden = [jnp.where(row == column, gelu_tanh(block), 0.0).astype(BF16) for block in before]
+    for at in range(count):
         copies[at][1].wait()
-        copies[at + 1][1].wait()
+    for at, block in zip(pairs, hidden, strict=True):
+        here = slice(at * slot_exp, at * slot_exp + rows)
         second = jnp.concatenate([w_out[at], w_out[at + 1]], axis=0)
-        out[here, :] = jnp.dot(hidden, second, preferred_element_type=F32).astype(out.dtype)
+        out[here, :] = jnp.dot(block, second, preferred_element_type=F32).astype(out.dtype)
 
 
 def experts(half_at, slots, w_in, w_out, kind, wait_for=()):
@@ -229,145 +233,76 @@
     )(half_at, slots, far_memory(w_in), far_memory(w_out), *wait_for)
 
 
-def add_kernel(across, own, got, out):
-    rows, wide = out.shape[1], out.shape[2]
-    merged = own[...] + got[...].astype(F32)
-    for at in range(out.shape[0]):
-        down, along = at // across, at % across
-        out[at] = merged[down * rows : (down + 1) * rows, along * wide : (along + 1) * wide].astype(BF16)
-
-
-def add_and_cut(own, got, down, across, wait_for):
-    rows, wide = own.shape[0] // down, own.shape[1] // across
-    return call(
-        after(functools.partial(add_kernel, across), 2, len(wait_for)),
-        kept((down * across, rows, wide), BF16),
-        in_specs=[whole(), whole()] + anywhere(len(wait_for)),
-        out_specs=whole(),
-    )(own, got, *wait_for)
-
-
-def reduce_mid_kernel(down, got, out):
-    across, rows, wide = out.shape[1], out.shape[2], out.shape[3]
-    n_down = got.shape[0] // across
-    n_wide = out.shape[0] // down
-    for y in range(across):
-        summed = got[y].astype(F32)
-        for x in range(1, n_down):
-            summed += got[x * across + y].astype(F32)
-        for h in range(down):
-            for l in range(n_wide):
-                out[h * n_wide + l, y] = summed[
-                    h * rows : (h + 1) * rows, l * wide : (l + 1) * wide
-                ].astype(BF16)
-
-
-def reduce_mid(got, across, down, n_wide, wait_for):
-    rows, wide = got.shape[1] // down, got.shape[2] // n_wide
-    return call(
-        after(functools.partial(reduce_mid_kernel, down), 1, 1),
-        kept((down * n_wide, across, rows, wide), BF16),
-        in_specs=[whole(), pl.BlockSpec(memory_space=pltpu.HBM)],
-        out_specs=whole(),
-    )(got, far_memory(wait_for))
-
-
-def reduce_out_kernel(down, got, out):
-    n_wide = got.shape[0] // down
-    for y in range(got.shape[1]):
-        for l in range(n_wide):
-            summed = got[l, y].astype(F32)
-            for h in range(1, down):
-                summed += got[h * n_wide + l, y].astype(F32)
-            result = summed.astype(BF16)
-            for at in range(out.shape[0]):
-                out[at, y * n_wide + l] = result
-
-
-def reduce_out(got, down, copies):
-    n_wide = got.shape[0] // down
-    return call(
-        functools.partial(reduce_out_kernel, down),
-        kept((copies, got.shape[1] * n_wide) + got.shape[2:], BF16),
-        in_specs=[whole()],
-        out_specs=whole(),
-    )(got)
-
-
-def combine_kernel(pieces, core, tok_own, tok_other, *refs):
-    own, other = refs[: pieces // 2], refs[pieces // 2 : pieces]
-    weights, total, logits, table_own, table_other, sems = refs[pieces:]
-
-    def copies():
-        at = 0
-        for to, which in ((table_own, own), (table_other, other)):
-            start = 0
-            for piece in which:
-                here = pl.ds(start, piece.shape[0])
-                yield start, pltpu.make_async_copy(piece, to.at[here], sems.at[at])
-                start += piece.shape[0]
-                at += 1
+def weights_kernel(pieces, core, tok, *refs):
+    weights, stats, logits, table, sems = refs[pieces:]
+    blocks, width, wide = table.shape
+    half = width // 2
 
     @pl.when(pl.program_id(0) == 0)
     def _():
-        started = [copy for _, copy in copies()]
-        for copy in started:
-            copy.start()
-        for copy in started:
+        copies = []
+        for which in range(2):
+            side = core[0] if which == 0 else 1 - core[0]
+            features = pl.ds(pl.multiple_of(side * half, half), half)
+            start = 0
+            for piece in refs[which * pieces // 2 : (which + 1) * pieces // 2]:
+                to = table.at[pl.ds(start, piece.shape[0]), features]
+                copies.append(pltpu.make_async_copy(piece, to, sems.at[len(copies)]))
+                copies[-1].start()
+                start += piece.shape[0]
+        for copy in copies:
             copy.wait()
 
-    peak = None
-    wide = table_own.shape[2]
-    for at in range(table_own.shape[0]):
-        block = jnp.dot(tok_own[...], table_own[at], preferred_element_type=F32)
-        block += jnp.dot(tok_other[...], table_other[at], preferred_element_type=F32)
+    peaks = None
+    for at in range(blocks):
+        block = jnp.dot(tok[...], table[at], preferred_element_type=F32)
         logits[:, at * wide : (at + 1) * wide] = block
-        top = jnp.max(block, axis=1, keepdims=True)
-        peak = top if peak is None else jnp.maximum(peak, top)
-    sums = jnp.zeros_like(peak)
-    for at in range(table_own.shape[0]):
-        here = slice(at * wide, (at + 1) * wide)
-        block = jnp.exp(logits[:, here] - peak)
-        weights[:, here] = block.astype(BF16)
-        sums += jnp.sum(block, axis=1, keepdims=True)
-    total[...] = jnp.broadcast_to(sums, total.shape)
-
-
-def combine_weights(core, tokens, own, other, wait_for, steps=8):
+        for lanes in range(0, wide, 128):
+            some = block[:, lanes : lanes + 128]
+            peaks = some if peaks is None else jnp.maximum(peaks, some)
+    peak = jnp.max(peaks, axis=1, keepdims=True)
+    sums = jnp.zeros_like(peaks)
+    for lanes in range(0, blocks * wide, 128):
+        block = jnp.exp(logits[:, lanes : lanes + 128] - peak)
+        weights[:, lanes : lanes + 128] = block.astype(BF16)
+        sums += block
+    lane = lax.broadcasted_iota(jnp.int32, stats.shape, 1)
+    stats[...] = jnp.where(lane < 64, peak, jnp.sum(sums, axis=1, keepdims=True))
+
+
+def combine_weights(core, tokens, own, other, wait_for, steps=3):
     count, width = tokens.shape
     blocks = sum(piece.shape[0] for piece in own)
-    depth, wide = own[0].shape[1:]
-    slots = blocks * wide
+    wide = own[0].shape[2]
     rows = count // steps
-    pieces = own + other
-    tokens = far_memory(tokens)
-    return call(
-        after(functools.partial(combine_kernel, len(pieces)), 3 + len(pieces), 1),
-        [pltpu.HBM((count, slots), BF16), pltpu.HBM((count, 128), F32)],
-        micros=12,
+    pieces = [far_memory(piece) for piece in own + other]
+    return call(
+        after(functools.partial(weights_kernel, len(pieces)), 2 + len(pieces), len(wait_for)),
+        [pltpu.HBM((count, blocks * wide), BF16), pltpu.HBM((count, 128), F32)],
+        micros=2 * blocks,
+        limit=40 << 20,
         grid_spec=pltpu.PrefetchScalarGridSpec(
             num_scalar_prefetch=1,
             grid=(steps,),
-            in_specs=[
-                pl.BlockSpec((rows, width // 2), lambda i, core: (i, core[0])),
-                pl.BlockSpec((rows, width // 2), lambda i, core: (i, 1 - core[0])),
-            ]
-            + anywhere(len(pieces) + 1),
+            in_specs=[pl.BlockSpec((rows, width), lambda i, core: (i, 0))]
+            + [pl.BlockSpec(memory_space=pltpu.HBM)] * len(pieces)
+            + anywhere(len(wait_for)),
             out_specs=[
-                pl.BlockSpec((rows, slots), lambda i, core: (i, 0)),
+                pl.BlockSpec((rows, blocks * wide), lambda i, core: (i, 0)),
                 pl.BlockSpec((rows, 128), lambda i, core: (i, 0)),
             ],
             scratch_shapes=[
-                pltpu.VMEM((rows, slots), F32),
-                pltpu.VMEM((blocks, depth, wide), BF16),
-                pltpu.VMEM((blocks, depth, wide), BF16),
+                pltpu.VMEM((rows, blocks * wide), F32),
+                pltpu.VMEM((blocks, width, wide), BF16),
                 pltpu.SemaphoreType.DMA((len(pieces),)),
             ],
         ),
-    )(core, tokens, tokens, *pieces, wait_for)
-
-
-def output_kernel(place, weights, total, own, other, out, table):
+    )(core, far_memory(tokens), *pieces, *wait_for)
+
+
+def output_kernel(parts, place, *refs):
+    weights, stats = refs[:parts], refs[parts : 2 * parts]
+    own, other, out, table = refs[2 * parts :]
     half = own.shape[0] * own.shape[2]
     groups = own.shape[1]
 
@@ -380,27 +315,36 @@
                 here = pl.multiple_of(at * 2 * half + start * half, half)
                 table[pl.ds(here, half), :] = block.astype(BF16)
 
-    mixed = jnp.dot(weights[...], table[...], preferred_element_type=F32)
-    out[...] = (mixed / total[...]).astype(BF16)
-
-
-def output(place, weights, total, own, other, steps=5):
-    count, slots = weights.shape
+    peaks = [part[:, 0:1] for part in stats]
+    top = functools.reduce(jnp.maximum, peaks)
+    scales = [jnp.exp(peak - top) for peak in peaks]
+    total = sum(part[:, 64:65] * scale for part, scale in zip(stats, scales, strict=True))
+    mixed = jnp.zeros(out.shape, F32)
+    start = 0
+    for part, scale in zip(weights, scales, strict=True):
+        rows = table[start : start + part.shape[1], :]
+        mixed += jnp.dot(part[...], rows, preferred_element_type=F32) * (scale / total)
+        start += part.shape[1]
+    out[...] = mixed.astype(BF16)
+
+
+def output(place, weights, stats, own, other, steps=5):
+    count = weights[0].shape[0]
+    slots = sum(part.shape[1] for part in weights)
     wide = own.shape[3]
-    return call(
-        output_kernel,
+    rows = count // steps
+    return call(
+        functools.partial(output_kernel, len(weights)),
         jax.ShapeDtypeStruct((count, wide), BF16),
+        limit=24 << 20,
         grid=(steps,),
-        in_specs=[
-            pl.BlockSpec(memory_space=pltpu.SMEM),
-            pl.BlockSpec((count // steps, slots), lambda i: (i, 0)),
-            pl.BlockSpec((count // steps, wide), lambda i: (i, 0)),
-            whole(),
-            whole(),
-        ],
-        out_specs=pl.BlockSpec((count // steps, wide), lambda i: (i, 0)),
+        in_specs=[pl.BlockSpec(memory_space=pltpu.SMEM)]
+        + [pl.BlockSpec((rows, part.shape[1]), lambda i: (i, 0)) for part in weights]
+        + [pl.BlockSpec((rows, 128), lambda i: (i, 0)) for part in stats]
+        + [whole(), whole()],
+        out_specs=pl.BlockSpec((rows, wide), lambda i: (i, 0)),
         scratch_shapes=[pltpu.VMEM((slots, wide), BF16)],
-    )(place, far_memory(weights), far_memory(total), own, other)
+    )(place, *map(far_memory, weights), *map(far_memory, stats), own, other)
 
 
 def shift(by):
@@ -425,29 +369,51 @@
     own, send = dispatch(core, tokens, slot_embed)
     merged = merge(own, lax.ppermute(send, "core", SWAP))
     here = jnp.stack([mine, near])
+    here_there = lax.ppermute(here, "core", SWAP)
     down = lax.ppermute(here, "y", shift(1))
     up = lax.ppermute(here, "y", shift(-1))
     got = lax.all_to_all(merged.reshape(nx * nh, part, -1), ("x", "zh"), 0, 0)
-    spread = reduce_in(got, [down, up])
+    spread = reduce_in(got, [here_there])
     far = [lax.ppermute(down[:1], "y", shift(1)), lax.ppermute(up[1:], "y", shift(-1))]
-    near_table = [here, down, up]
-    near_there = [lax.ppermute(piece, "core", SWAP) for piece in near_table]
+    first, first_stats = combine_weights(core, tokens, [here], [here_there], [spread] + far)
+    far_there = [lax.ppermute(piece, "core", SWAP) for piece in far]
+    down_there, up_there = (lax.ppermute(piece, "core", SWAP) for piece in (down, up))
     slots_own = lax.all_to_all(spread, ("x", "zh"), 0, 0).reshape(half, features)
+    slots_own, first_stats, down_there, up_there, far_there = lax.optimization_barrier(
+        (slots_own, first_stats, down_there, up_there, far_there)
+    )
     slots_other = lax.ppermute(slots_own, "core", SWAP)
 
-    done_own = experts(core, slots_own, w_in, w_out, F32, far + near_there)
+    done_own = experts(core, slots_own, w_in, w_out, F32)
     done_other = experts(1 - core, slots_other, w_in, w_out, BF16)
-    far_there = [lax.ppermute(piece, "core", SWAP) for piece in far]
-    cut = add_and_cut(done_own, lax.ppermute(done_other, "core", SWAP), nx, ny, far_there)
-
-    weights, total = combine_weights(core, tokens, near_table + far, near_there + far_there, cut)
-
+    got = lax.ppermute(done_other, "core", SWAP)
+
+    cut = (done_own + got.astype(F32)).astype(BF16)
+    cut = cut.reshape(nx, half // nx, ny, features // ny).transpose(0, 2, 1, 3)
+    cut = cut.reshape(nx * ny, half // nx, features // ny)
+    second, second_stats = combine_weights(core, tokens, [down], [down_there], [cut])
     got = lax.all_to_all(cut, ("x", "y"), 0, 0)
-    got = lax.all_to_all(reduce_mid(got, ny, nh, nl, weights), ("zh", "zl"), 0, 0)
-    spread = reduce_out(got, nh, nx * nh)
+    got, second_stats = lax.optimization_barrier((got, second_stats))
+    got = jnp.sum(got.reshape((nx, ny) + got.shape[1:]).astype(F32), axis=0).astype(BF16)
+    cut = got.reshape(ny, nh, part, nl, features // (ny * nl)).transpose(1, 3, 0, 2, 4)
+    cut = cut.reshape((nh * nl, ny, part, -1))
+    third, third_stats = combine_weights(core, tokens, [up], [up_there], [cut])
+    got = lax.all_to_all(cut, ("zh", "zl"), 0, 0)
+    got, third_stats = lax.optimization_barrier((got, third_stats))
+    got = jnp.sum(got.reshape((nh, nl) + got.shape[1:]).astype(F32), axis=0).astype(BF16)
+    got = got.transpose(1, 0, 2, 3).reshape((ny * nl,) + got.shape[2:])
+    spread = jnp.broadcast_to(got[None], (nx * nh,) + got.shape)
+    fourth, fourth_stats = combine_weights(core, tokens, far, far_there, [spread])
     out_own = lax.all_to_all(spread, ("x", "zh"), 0, 0)
+    out_own, fourth_stats = lax.optimization_barrier((out_own, fourth_stats))
     out_other = lax.ppermute(out_own, "core", SWAP)
-    return output(place, weights, total, out_own, out_other)
+    return output(
+        place,
+        [first, second, third, fourth],
+        [first_stats, second_stats, third_stats, fourth_stats],
+        out_own,
+        out_other,
+    )
 
 
 def solution(mesh):

time: 136 us -> 122 us (0.90)
  waiting for transfers between devices: 31.3 us -> 14.5 us
  blocking collectives: 13.4 us -> 0 us
  Pallas kernels: 40.7 us -> 50.7 us
  starting transfers between devices: 45.4 us -> 50.6 us
    all_to_all x1 -> x0, blocking collectives: 13.4 us -> none  [on_device(): lax.all_to_all(reduce_mid(got, ny, nh, nl, weights), ('zh', 'zl'), 0, 0)]
    pallas_call x5, Pallas kernels: 25.4 us -> 36.8 us  [the longest x4 29.1 us: combine_weights(): call(after(functools.partial(weights_kernel, len(pieces)), 2 + len(pieces...]
    ppermute x1, waiting for transfers between devices: 11.3 us -> 0.01 us  [on_device(): down = lax.ppermute(here, 'y', shift(1))]
    all_to_all x1, waiting for transfers between devices: 11.5 us -> 4.67 us  [on_device(): out_own = lax.all_to_all(spread, ('x', 'zh'), 0, 0)]
    all_to_all x1, waiting for transfers between devices: 0.01 us -> 5.92 us  [on_device(): got = lax.all_to_all(merged.reshape(nx * nh, part, -1), ('x', 'zh'), 0, 0)]
    all_to_all x1, starting transfers between devices: 8.79 us -> 3.54 us  [on_device(): lax.all_to_all(spread, ('x', 'zh'), 0, 0).reshape(half, features)]
    all_to_all x0 -> x1, starting transfers between devices: none -> 4.48 us  [on_device(): got = lax.all_to_all(cut, ('zh', 'zl'), 0, 0)]
    all_to_all x1, starting transfers between devices: 4.47 us -> 8.83 us  [on_device(): out_own = lax.all_to_all(spread, ('x', 'zh'), 0, 0)]
  transfers between devices with their start and end apart: 18 -> 19, of which waited for: 6 -> 6; matrix products, arithmetic and copies ran while one was open for 1% -> 1% of each run, Pallas kernels for 18% -> 33%
where the time goes in v3:
time: 122 us; the launch traced here: 121 us
  Pallas kernels  50.7 us (42%)
  starting transfers between devices  50.6 us (41%)
  waiting for transfers between devices  14.5 us (12%)
  local copies, waits for them, and re-layouts  4.99 us (4%)
    pallas_call x4, Pallas kernels, combine_weights(): call(after(functools.partial(weights_kernel, len(pieces)), 2 + len(pieces...  29.1 us
    all_to_all x1, starting transfers between devices, on_device(): got = lax.all_to_all(merged.reshape(nx * nh, part, -1), ('x', 'zh'), 0, 0)  9.85 us
    all_to_all x1, starting transfers between devices, on_device(): out_own = lax.all_to_all(spread, ('x', 'zh'), 0, 0)  8.83 us
    pallas_call x1, Pallas kernels, output(): call(functools.partial(output_kernel, len(weights)), jax.ShapeDtypeStruct...  7.68 us
    pallas_call x2, Pallas kernels, experts(): call(after(functools.partial(expert_kernel, slots.shape[0] // count), 4,...  6.31 us
    all_to_all x1, waiting for transfers between devices, on_device(): got = lax.all_to_all(merged.reshape(nx * nh, part, -1), ('x', 'zh'), 0, 0)  5.92 us
    pallas_call x1, Pallas kernels, dispatch(): call(functools.partial(dispatch_kernel, parts), micros=6, outs=[kept(shap...  5.48 us
    all_to_all x1, waiting for transfers between devices, on_device(): out_own = lax.all_to_all(spread, ('x', 'zh'), 0, 0)  4.67 us
  transfers between devices with their start and end apart: 19, of which 6 were waited for; matrix products, arithmetic and copies ran while one was open for 1% of the time, Pallas kernels for 33%

profile of v3, /device:TPU:1, one launch (start us, length us, event | category | flops | bytes accessed | tf_op | source)
XLA Modules:
  0.0 121.3 jit_solution(9694525165243666440)
XLA Ops:
  0.0 1.0 constant_dynamic-slice_fusion
  1.0 2.6 %collective-permute-start = (bf16[512,256]{1,0:T(8,128)(2,1)S(1)}, bf16[512,256]{1,0:T(8,128)(2,1)S(1)}, u32[]{:S(2)}, u32[]{:S(2)}) collective-permute-start(bf16[512,256]{1,0:T(8,128)(2,1)S(1)} %constant_dynamic-slice_fusion), channel_id=1, source_target_pairs={{0,1},{1,0},{2,3},{3,2},{4,5},{5,4},{6,7},{7,6},{8,9},{9,8},{10,11... | collective-permute-start | bytes 786440 | tf_op jit(solution)/shard_map/ppermute | solution.py:364
  3.5 5.5 %shard_map.46 = (f32[128,1152]{1,0:T(8,128)S(1)}, bf16[128,1152]{1,0:T(8,128)(2,1)S(1)}) custom-call(s32[1]{0:T(128)} %bitcast.core.refs_0_, bf16[1920,1024]{1,0:T(8,128)(2,1)} %refs_1_.7, bf16[1024,256]{1,0:T(8,128)(2,1)} %embed_any.1), custom_call_target="tpu_custom_call" | custom-call | bytes 180000 | tf_op jit(solution)/shard_map/pallas_call | solution.py:119
  9.0 1.0 collective-permute-start.2
  10.1 0.1 pad_maximum_fusion.refs_2_
  10.2 1.4 %collective-permute-start.3 = (bf16[2,512,256]{2,1,0:T(8,128)(2,1)S(1)}, bf16[2,512,256]{2,1,0:T(8,128)(2,1)S(1)}, u32[]{:S(2)}, u32[]{:S(2)}) collective-permute-start(bf16[2,512,256]{2,1,0:T(8,128)(2,1)S(1)} %pad_maximum_fusion.refs_2_), channel_id=1, source_target_pairs={{0,2},{2,4},{4,6},{6,0},{1,3},{3,5},{5,7},{7,1},{8,10},{10,12},{12... | collective-permute-start | bytes 1572872 | tf_op jit(solution)/shard_map/ppermute | solution.py:373
  11.5 1.5 %collective-permute-start.5 = (bf16[2,512,256]{2,1,0:T(8,128)(2,1)S(1)}, bf16[2,512,256]{2,1,0:T(8,128)(2,1)S(1)}, u32[]{:S(2)}, u32[]{:S(2)}) collective-permute-start(bf16[2,512,256]{2,1,0:T(8,128)(2,1)S(1)} %pad_maximum_fusion.refs_2_), channel_id=1, source_target_pairs={{0,6},{2,0},{4,2},{6,4},{1,7},{3,1},{5,3},{7,5},{8,14},{10,8},{12,... | collective-permute-start | bytes 1572872 | tf_op jit(solution)/shard_map/ppermute | solution.py:374
  13.1 1.1 shard_map.47
  14.2 9.8 %all-to-all-start = ((bf16[16,8,1152]{2,1,0:T(8,128)(2,1)}), bf16[16,8,1152]{2,1,0:T(8,128)(2,1)S(1)}, u32[]{:S(2)}, u32[]{:S(2)}) async-start(bf16[16,8,1152]{2,1,0:T(8,128)(2,1)} %bitcast.9), calls=%async_computation | async-start | bytes 589824 | tf_op jit(solution)/shard_map/all_to_all | solution.py:375
  24.0 2.2 %collective-permute-start.1 = (bf16[2,512,256]{2,1,0:T(8,128)(2,1)S(1)}, bf16[2,512,256]{2,1,0:T(8,128)(2,1)S(1)}, u32[]{:S(2)}, u32[]{:S(2)}) collective-permute-start(bf16[2,512,256]{2,1,0:T(8,128)(2,1)S(1)} %pad_maximum_fusion.refs_2_), channel_id=1, source_target_pairs={{0,8},{8,0},{1,9},{9,1},{2,10},{10,2},{3,11},{11,3},{4,12},{12,4},... | collective-permute-start | bytes 1572872 | tf_op jit(solution)/shard_map/ppermute | solution.py:372
  26.2 0.0 collective-permute-done.3.refs_2_
  26.2 0.8 slice.8
  27.0 0.1 collective-permute-start.4
  27.1 0.3 collective-permute-start.7
  27.4 0.2 collective-permute-start.8
  27.6 0.7 slice.9
  28.3 2.6 %collective-permute-start.6 = (bf16[1,512,256]{2,1,0:T(8,128)(2,1)}, bf16[1,512,256]{2,1,0:T(8,128)(2,1)S(1)}, u32[]{:S(2)}, u32[]{:S(2)}) collective-permute-start(bf16[1,512,256]{2,1,0:T(8,128)(2,1)} %slice.9), channel_id=1, source_target_pairs={{0,6},{2,0},{4,2},{6,4},{1,7},{3,1},{5,3},{7,5},{8,14},{10,8},{12,... | collective-permute-start | bytes 786440 | tf_op jit(solution)/shard_map/ppermute | solution.py:377
  30.9 5.9 %all-to-all-done.refs_0_ = bf16[16,8,1152]{2,1,0:T(8,128)(2,1)S(1)} async-done(((bf16[16,8,1152]{2,1,0:T(8,128)(2,1)}), bf16[16,8,1152]{2,1,0:T(8,128)(2,1)S(1)}, u32[]{:S(2)}, u32[]{:S(2)}) %all-to-all-start) | async-done | bytes 294944 | tf_op jit(solution)/shard_map/all_to_all | solution.py:375
  36.8 1.0 shard_map.48.refs_4_
  37.8 3.5 %all-to-all-start.1 = ((bf16[16,8,1024]{2,1,0:T(8,128)(2,1)}), bf16[16,8,1024]{2,1,0:T(8,128)(2,1)S(1)}, u32[]{:S(2)}, u32[]{:S(2)}) async-start(bf16[16,8,1024]{2,1,0:T(8,128)(2,1)} %shard_map.48.refs_4_), calls=%async_computation.1 | async-start | bytes 524288 | tf_op jit(solution)/shard_map/all_to_all | solution.py:381
  41.4 2.2 %collective-permute-start.9 = (bf16[1,512,256]{2,1,0:T(8,128)(2,1)S(1)}, bf16[1,512,256]{2,1,0:T(8,128)(2,1)S(1)}, u32[]{:S(2)}, u32[]{:S(2)}) collective-permute-start(bf16[1,512,256]{2,1,0:T(8,128)(2,1)S(1)} %collective-permute-done.4.refs_5_.refs_2_), channel_id=1, source_target_pairs={{0,8},{8,0},{1,9},{9,1},{2,10},{10,2},{3,11},{11,3},{4,12},{12,4},... | collective-permute-start | bytes 786440 | tf_op jit(solution)/shard_map/ppermute | solution.py:379
  43.6 0.1 collective-permute-start.10
  43.7 7.3 %shard_map.49 = (bf16[1920,512]{1,0:T(8,128)(2,1)}, f32[1920,128]{1,0:T(8,128)}) custom-call(s32[1]{0:T(128)} %bitcast.core.refs_0_, bf16[1920,1024]{1,0:T(8,128)(2,1)} %refs_1_.7, bf16[2,512,256]{2,1,0:T(8,128)(2,1)} %copy-done.4, bf16[2,512,256]{2,1,0:T(8,128)(2,1)} %copy-done, bf16[16,8,1024]{2,1,0:T(8,128)(2,1)} %shard_map.48.refs_4_, ...), custom_call_target="tpu_custom_call" | custom-call | bytes 120000 | tf_op jit(solution)/shard_map/pallas_call | solution.py:279
  51.1 1.0 all-to-all-done.1
  52.1 3.7 %collective-permute-start.11 = (bf16[128,1024]{1,0:T(8,128)(2,1)S(1)}, bf16[128,1024]{1,0:T(8,128)(2,1)S(1)}, u32[]{:S(2)}, u32[]{:S(2)}) collective-permute-start(bf16[128,1024]{1,0:T(8,128)(2,1)S(1)} %bitcast.23), channel_id=1, source_target_pairs={{0,8},{8,0},{1,9},{9,1},{2,10},{10,2},{3,11},{11,3},{4,12},{12,4},... | collective-permute-start | bytes 786440 | tf_op jit(solution)/shard_map/ppermute | solution.py:385
  55.7 1.2 collective-permute-done.11.refs_1_
  56.9 3.2 %shard_map.51 = bf16[128,1024]{1,0:T(8,128)(2,1)S(1)} custom-call(s32[1]{0:T(128)S(6)} %sub.12.refs_0_, bf16[128,1024]{1,0:T(8,128)(2,1)S(1)} %collective-permute-done.11.refs_1_, bf16[16,1024,128]{2,1,0:T(8,128)(2,1)} %refs_2_.3, bf16[16,128,1024]{2,1,0:T(8,128)(2,1)} %refs_3_.3), custom_call_target="tpu_custom_call" | custom-call | bytes 90000 | tf_op jit(solution)/shard_map/pallas_call | solution.py:220
  60.1 0.5 collective-permute-start.12
  60.6 3.2 %shard_map.50 = f32[128,1024]{1,0:T(8,128)S(1)} custom-call(s32[1]{0:T(128)} %bitcast.core.refs_0_, bf16[128,1024]{1,0:T(8,128)(2,1)S(1)} %bitcast.24, bf16[16,1024,128]{2,1,0:T(8,128)(2,1)} %refs_2_.3, bf16[16,128,1024]{2,1,0:T(8,128)(2,1)} %refs_3_.3), custom_call_target="tpu_custom_call" | custom-call | bytes 90000 | tf_op jit(solution)/shard_map/pallas_call | solution.py:220
  63.7 0.1 add_convert_fusion
  63.8 0.2 reshape.31
  64.0 0.7 copy.10
  64.7 3.5 %all-to-all-start.2 = ((bf16[16,32,256]{2,1,0:T(8,128)(2,1)}), bf16[16,32,256]{2,1,0:T(8,128)(2,1)S(1)}, u32[]{:S(2)}, u32[]{:S(2)}) async-start(bf16[16,32,256]{2,1,0:T(8,128)(2,1)} %bitcast.12.refs_4_), calls=%async_computation.2 | async-start | bytes 524288 | tf_op jit(solution)/shard_map/all_to_all | solution.py:395
  68.3 7.3 %shard_map.52 = (bf16[1920,512]{1,0:T(8,128)(2,1)}, f32[1920,128]{1,0:T(8,128)}) custom-call(s32[1]{0:T(128)} %bitcast.core.refs_0_, bf16[1920,1024]{1,0:T(8,128)(2,1)} %refs_1_.7, bf16[2,512,256]{2,1,0:T(8,128)(2,1)} %copy-done.6, bf16[2,512,256]{2,1,0:T(8,128)(2,1)} %collective-permute-done.7.refs_3_, bf16[16,32,256]{2,1,0:T(8,128)(2,1)} %bitcast.12.refs_4_), custom_call_target="tpu_custom_call" | custom-call | bytes 120000 | tf_op jit(solution)/shard_map/pallas_call | solution.py:279
  75.5 0.6 all-to-all-done.2
  76.2 0.6 copy.11
  76.9 4.5 %all-to-all-start.3 = ((bf16[8,4,8,128]{3,2,1,0:T(8,128)(2,1)}), bf16[8,4,8,128]{3,2,1,0:T(8,128)(2,1)S(1)}, u32[]{:S(2)}, u32[]{:S(2)}) async-start(bf16[8,4,8,128]{3,2,1,0:T(8,128)(2,1)} %bitcast.17.refs_4_), calls=%async_computation.3 | async-start | bytes 131072 | tf_op jit(solution)/shard_map/all_to_all | solution.py:401
  81.3 7.3 %shard_map.53 = (bf16[1920,512]{1,0:T(8,128)(2,1)}, f32[1920,128]{1,0:T(8,128)}) custom-call(s32[1]{0:T(128)} %bitcast.core.refs_0_, bf16[1920,1024]{1,0:T(8,128)(2,1)} %refs_1_.7, bf16[2,512,256]{2,1,0:T(8,128)(2,1)} %copy-done.5, bf16[2,512,256]{2,1,0:T(8,128)(2,1)} %copy-done.7, bf16[8,4,8,128]{3,2,1,0:T(8,128)(2,1)} %bitcast.17.refs_4_), custom_call_target="tpu_custom_call" | custom-call | bytes 120000 | tf_op jit(solution)/shard_map/pallas_call | solution.py:279
  88.7 0.8 broadcast_in_dim.8.refs_6_
  89.4 8.8 %all-to-all-start.4 = ((bf16[16,8,8,128]{3,2,1,0:T(8,128)(2,1)}), bf16[16,8,8,128]{3,2,1,0:T(8,128)(2,1)S(1)}, u32[]{:S(2)}, u32[]{:S(2)}) async-start(bf16[16,8,8,128]{3,2,1,0:T(8,128)(2,1)} %broadcast_in_dim.8.refs_6_), calls=%async_computation.4 | async-start | bytes 524288 | tf_op jit(solution)/shard_map/all_to_all | solution.py:407
  98.3 0.1 stack.50
  98.4 0.1 stack.47
  98.4 7.3 %shard_map.54 = (bf16[1920,512]{1,0:T(8,128)(2,1)}, f32[1920,128]{1,0:T(8,128)}) custom-call(s32[1]{0:T(128)} %bitcast.core.refs_0_, bf16[1920,1024]{1,0:T(8,128)(2,1)} %refs_1_.7, bf16[1,512,256]{2,1,0:T(8,128)(2,1)} %copy-done.1, bf16[1,512,256]{2,1,0:T(8,128)(2,1)} %copy-done.2, bf16[1,512,256]{2,1,0:T(8,128)(2,1)} %copy-done.8, ...), custom_call_target="tpu_custom_call" | custom-call | bytes 120000 | tf_op jit(solution)/shard_map/pallas_call | solution.py:279
  105.7 4.7 %all-to-all-done.4.refs_8_ = bf16[16,8,8,128]{3,2,1,0:T(8,128)(2,1)S(1)} async-done(((bf16[16,8,8,128]{3,2,1,0:T(8,128)(2,1)}), bf16[16,8,8,128]{3,2,1,0:T(8,128)(2,1)S(1)}, u32[]{:S(2)}, u32[]{:S(2)}) %all-to-all-start.4) | async-done | bytes 262176 | tf_op jit(solution)/shard_map/all_to_all | solution.py:407
  110.4 2.0 %collective-permute-start.13 = (bf16[16,8,8,128]{3,2,1,0:T(8,128)(2,1)S(1)}, bf16[16,8,8,128]{3,2,1,0:T(8,128)(2,1)S(1)}, u32[]{:S(2)}, u32[]{:S(2)}) collective-permute-start(bf16[16,8,8,128]{3,2,1,0:T(8,128)(2,1)S(1)} %all-to-all-done.4.refs_8_), channel_id=1, source_target_pairs={{0,8},{8,0},{1,9},{9,1},{2,10},{10,2},{3,11},{11,3},{4,12},{12,4},... | collective-permute-start | bytes 786440 | tf_op jit(solution)/shard_map/ppermute | solution.py:409
  112.4 0.1 pad_add_fusion.place
  112.5 1.1 collective-permute-done.13.refs_9_
  113.6 7.7 %shard_map.55 = bf16[1920,128]{1,0:T(8,128)(2,1)} custom-call(s32[9]{0:T(128)S(1)} %pad_add_fusion.place, bf16[1920,512]{1,0:T(8,128)(2,1)} %get-tuple-element.29.refs_0_, bf16[1920,512]{1,0:T(8,128)(2,1)} %get-tuple-element.33.refs_1_, bf16[1920,512]{1,0:T(8,128)(2,1)} %get-tuple-element.37.refs_2_, bf16[1920,512]{1,0:T(8,128)(2,1)} %get-tuple-element.42.refs_3_, ...), custom_call_target="tpu_custom_call" | custom-call | bytes 30000 | tf_op jit(solution)/shard_map/pallas_call | solution.py:336
  (37 shorter events, 0.2 us)
Async XLA Ops:
  1.0 9.1 %collective-permute-start = (bf16[512,256]{1,0:T(8,128)(2,1)S(1)}, bf16[512,256]{1,0:T(8,128)(2,1)S(1)}, u32[]{:S(2)}, u32[]{:S(2)}) collective-permute-start(bf16[512,256]{1,0:T(8,128)(2,1)S(1)} %constant_dynamic-slice_fusion), channel_id=1, source_target_pairs={{0,1},{1,0},{2,3},{3,2},{4,5},{5,4},{6,7},{7,6},{8,9},{9,8},{10,11... | collective-permute-start | bytes 786440 | tf_op jit(solution)/shard_map/ppermute | solution.py:364
  3.5 6.5 %copy-start.3 = (bf16[1024,256]{1,0:T(8,128)(2,1)S(1)}, bf16[1024,256]{1,0:T(8,128)(2,1)}, u32[]{:S(2)}) copy-start(bf16[1024,256]{1,0:T(8,128)(2,1)} %embed_any.1) | copy-start | bytes 1572868
  9.0 4.1 %collective-permute-start.2 = (bf16[128,1152]{1,0:T(8,128)(2,1)S(1)}, bf16[128,1152]{1,0:T(8,128)(2,1)S(1)}, u32[]{:S(2)}, u32[]{:S(2)}) collective-permute-start(bf16[128,1152]{1,0:T(8,128)(2,1)S(1)} %get-tuple-element.28), channel_id=1, source_target_pairs={{0,8},{8,0},{1,9},{9,1},{2,10},{10,2},{3,11},{11,3},{4,12},{12,4},... | collective-permute-start | bytes 884744 | tf_op jit(solution)/shard_map/ppermute | solution.py:370
  10.1 27.7 %copy-start.4 = (bf16[2,512,256]{2,1,0:T(8,128)(2,1)}, bf16[2,512,256]{2,1,0:T(8,128)(2,1)S(1)}, u32[]{:S(2)}) copy-start(bf16[2,512,256]{2,1,0:T(8,128)(2,1)S(1)} %pad_maximum_fusion.refs_2_) | copy-start | bytes 1572868
  10.2 16.1 %collective-permute-start.3 = (bf16[2,512,256]{2,1,0:T(8,128)(2,1)S(1)}, bf16[2,512,256]{2,1,0:T(8,128)(2,1)S(1)}, u32[]{:S(2)}, u32[]{:S(2)}) collective-permute-start(bf16[2,512,256]{2,1,0:T(8,128)(2,1)S(1)} %pad_maximum_fusion.refs_2_), channel_id=1, source_target_pairs={{0,2},{2,4},{4,6},{6,0},{1,3},{3,5},{5,7},{7,1},{8,10},{10,12},{12... | collective-permute-start | bytes 1572872 | tf_op jit(solution)/shard_map/ppermute | solution.py:373
  11.5 15.9 %collective-permute-start.5 = (bf16[2,512,256]{2,1,0:T(8,128)(2,1)S(1)}, bf16[2,512,256]{2,1,0:T(8,128)(2,1)S(1)}, u32[]{:S(2)}, u32[]{:S(2)}) collective-permute-start(bf16[2,512,256]{2,1,0:T(8,128)(2,1)S(1)} %pad_maximum_fusion.refs_2_), channel_id=1, source_target_pairs={{0,6},{2,0},{4,2},{6,4},{1,7},{3,1},{5,3},{7,5},{8,14},{10,8},{12,... | collective-permute-start | bytes 1572872 | tf_op jit(solution)/shard_map/ppermute | solution.py:374
  14.2 22.6 %all-to-all-start = ((bf16[16,8,1152]{2,1,0:T(8,128)(2,1)}), bf16[16,8,1152]{2,1,0:T(8,128)(2,1)S(1)}, u32[]{:S(2)}, u32[]{:S(2)}) async-start(bf16[16,8,1152]{2,1,0:T(8,128)(2,1)} %bitcast.9), calls=%async_computation | async-start | bytes 589824 | tf_op jit(solution)/shard_map/all_to_all | solution.py:375
  24.0 6.9 %collective-permute-start.1 = (bf16[2,512,256]{2,1,0:T(8,128)(2,1)S(1)}, bf16[2,512,256]{2,1,0:T(8,128)(2,1)S(1)}, u32[]{:S(2)}, u32[]{:S(2)}) collective-permute-start(bf16[2,512,256]{2,1,0:T(8,128)(2,1)S(1)} %pad_maximum_fusion.refs_2_), channel_id=1, source_target_pairs={{0,8},{8,0},{1,9},{9,1},{2,10},{10,2},{3,11},{11,3},{4,12},{12,4},... | collective-permute-start | bytes 1572872 | tf_op jit(solution)/shard_map/ppermute | solution.py:372
  26.2 24.8 %copy-start.6 = (bf16[2,512,256]{2,1,0:T(8,128)(2,1)}, bf16[2,512,256]{2,1,0:T(8,128)(2,1)S(1)}, u32[]{:S(2)}) copy-start(bf16[2,512,256]{2,1,0:T(8,128)(2,1)S(1)} %collective-permute-done.3.refs_2_) | copy-start | bytes 1572868
  27.0 14.4 %collective-permute-start.4 = (bf16[1,512,256]{2,1,0:T(8,128)(2,1)}, bf16[1,512,256]{2,1,0:T(8,128)(2,1)S(1)}, u32[]{:S(2)}, u32[]{:S(2)}) collective-permute-start(bf16[1,512,256]{2,1,0:T(8,128)(2,1)} %slice.8), channel_id=1, source_target_pairs={{0,2},{2,4},{4,6},{6,0},{1,3},{3,5},{5,7},{7,1},{8,10},{10,12},{12... | collective-permute-start | bytes 786440 | tf_op jit(solution)/shard_map/ppermute | solution.py:377
  27.1 24.0 %collective-permute-start.7 = (bf16[2,512,256]{2,1,0:T(8,128)(2,1)S(1)}, bf16[2,512,256]{2,1,0:T(8,128)(2,1)}, u32[]{:S(2)}, u32[]{:S(2)}) collective-permute-start(bf16[2,512,256]{2,1,0:T(8,128)(2,1)S(1)} %collective-permute-done.3.refs_2_), channel_id=1, source_target_pairs={{0,8},{8,0},{1,9},{9,1},{2,10},{10,2},{3,11},{11,3},{4,12},{12,4},... | collective-permute-start | bytes 1572872 | tf_op jit(solution)/shard_map/ppermute | solution.py:380
  27.4 23.6 %copy-start.5 = (bf16[2,512,256]{2,1,0:T(8,128)(2,1)}, bf16[2,512,256]{2,1,0:T(8,128)(2,1)S(1)}, u32[]{:S(2)}) copy-start(bf16[2,512,256]{2,1,0:T(8,128)(2,1)S(1)} %collective-permute-done.5.refs_2_) | copy-start | bytes 1572868
  27.4 23.7 %collective-permute-start.8 = (bf16[2,512,256]{2,1,0:T(8,128)(2,1)S(1)}, bf16[2,512,256]{2,1,0:T(8,128)(2,1)S(1)}, u32[]{:S(2)}, u32[]{:S(2)}) collective-permute-start(bf16[2,512,256]{2,1,0:T(8,128)(2,1)S(1)} %collective-permute-done.5.refs_2_), channel_id=1, source_target_pairs={{0,8},{8,0},{1,9},{9,1},{2,10},{10,2},{3,11},{11,3},{4,12},{12,4},... | collective-permute-start | bytes 1572872 | tf_op jit(solution)/shard_map/ppermute | solution.py:380
  28.3 15.3 %collective-permute-start.6 = (bf16[1,512,256]{2,1,0:T(8,128)(2,1)}, bf16[1,512,256]{2,1,0:T(8,128)(2,1)S(1)}, u32[]{:S(2)}, u32[]{:S(2)}) collective-permute-start(bf16[1,512,256]{2,1,0:T(8,128)(2,1)} %slice.9), channel_id=1, source_target_pairs={{0,6},{2,0},{4,2},{6,4},{1,7},{3,1},{5,3},{7,5},{8,14},{10,8},{12,... | collective-permute-start | bytes 786440 | tf_op jit(solution)/shard_map/ppermute | solution.py:377
  30.9 12.8 %copy-start = (bf16[2,512,256]{2,1,0:T(8,128)(2,1)}, bf16[2,512,256]{2,1,0:T(8,128)(2,1)S(1)}, u32[]{:S(2)}) copy-start(bf16[2,512,256]{2,1,0:T(8,128)(2,1)S(1)} %collective-permute-done.1.refs_1_.refs_3_) | copy-start | bytes 1572868
  37.8 14.3 %all-to-all-start.1 = ((bf16[16,8,1024]{2,1,0:T(8,128)(2,1)}), bf16[16,8,1024]{2,1,0:T(8,128)(2,1)S(1)}, u32[]{:S(2)}, u32[]{:S(2)}) async-start(bf16[16,8,1024]{2,1,0:T(8,128)(2,1)} %shard_map.48.refs_4_), calls=%async_computation.1 | async-start | bytes 524288 | tf_op jit(solution)/shard_map/all_to_all | solution.py:381
  41.4 9.7 %copy-start.1 = (bf16[1,512,256]{2,1,0:T(8,128)(2,1)}, bf16[1,512,256]{2,1,0:T(8,128)(2,1)S(1)}, u32[]{:S(2)}) copy-start(bf16[1,512,256]{2,1,0:T(8,128)(2,1)S(1)} %collective-permute-done.4.refs_5_.refs_2_) | copy-start | bytes 786436
  41.4 9.7 %collective-permute-start.9 = (bf16[1,512,256]{2,1,0:T(8,128)(2,1)S(1)}, bf16[1,512,256]{2,1,0:T(8,128)(2,1)S(1)}, u32[]{:S(2)}, u32[]{:S(2)}) collective-permute-start(bf16[1,512,256]{2,1,0:T(8,128)(2,1)S(1)} %collective-permute-done.4.refs_5_.refs_2_), channel_id=1, source_target_pairs={{0,8},{8,0},{1,9},{9,1},{2,10},{10,2},{3,11},{11,3},{4,12},{12,4},... | collective-permute-start | bytes 786440 | tf_op jit(solution)/shard_map/ppermute | solution.py:379
  43.6 7.5 %copy-start.2 = (bf16[1,512,256]{2,1,0:T(8,128)(2,1)}, bf16[1,512,256]{2,1,0:T(8,128)(2,1)S(1)}, u32[]{:S(2)}) copy-start(bf16[1,512,256]{2,1,0:T(8,128)(2,1)S(1)} %collective-permute-done.6.refs_6_.refs_3_) | copy-start | bytes 786436
  43.6 7.5 %collective-permute-start.10 = (bf16[1,512,256]{2,1,0:T(8,128)(2,1)S(1)}, bf16[1,512,256]{2,1,0:T(8,128)(2,1)S(1)}, u32[]{:S(2)}, u32[]{:S(2)}) collective-permute-start(bf16[1,512,256]{2,1,0:T(8,128)(2,1)S(1)} %collective-permute-done.6.refs_6_.refs_3_), channel_id=1, source_target_pairs={{0,8},{8,0},{1,9},{9,1},{2,10},{10,2},{3,11},{11,3},{4,12},{12,4},... | collective-permute-start | bytes 786440 | tf_op jit(solution)/shard_map/ppermute | solution.py:379
  51.1 9.0 %copy-start.7 = (bf16[2,512,256]{2,1,0:T(8,128)(2,1)}, bf16[2,512,256]{2,1,0:T(8,128)(2,1)S(1)}, u32[]{:S(2)}) copy-start(bf16[2,512,256]{2,1,0:T(8,128)(2,1)S(1)} %collective-permute-done.8.refs_3_) | copy-start | bytes 1572868
  51.1 9.0 %copy-start.8 = (bf16[1,512,256]{2,1,0:T(8,128)(2,1)}, bf16[1,512,256]{2,1,0:T(8,128)(2,1)S(1)}, u32[]{:S(2)}) copy-start(bf16[1,512,256]{2,1,0:T(8,128)(2,1)S(1)} %collective-permute-done.9.refs_4_) | copy-start | bytes 786436
  51.1 9.0 %copy-start.9 = (bf16[1,512,256]{2,1,0:T(8,128)(2,1)}, bf16[1,512,256]{2,1,0:T(8,128)(2,1)S(1)}, u32[]{:S(2)}) copy-start(bf16[1,512,256]{2,1,0:T(8,128)(2,1)S(1)} %collective-permute-done.10.refs_5_) | copy-start | bytes 786436
  52.1 4.8 %collective-permute-start.11 = (bf16[128,1024]{1,0:T(8,128)(2,1)S(1)}, bf16[128,1024]{1,0:T(8,128)(2,1)S(1)}, u32[]{:S(2)}, u32[]{:S(2)}) collective-permute-start(bf16[128,1024]{1,0:T(8,128)(2,1)S(1)} %bitcast.23), channel_id=1, source_target_pairs={{0,8},{8,0},{1,9},{9,1},{2,10},{10,2},{3,11},{11,3},{4,12},{12,4},... | collective-permute-start | bytes 786440 | tf_op jit(solution)/shard_map/ppermute | solution.py:385
  60.1 3.6 %collective-permute-start.12 = (bf16[128,1024]{1,0:T(8,128)(2,1)S(1)}, bf16[128,1024]{1,0:T(8,128)(2,1)S(1)}, u32[]{:S(2)}, u32[]{:S(2)}) collective-permute-start(bf16[128,1024]{1,0:T(8,128)(2,1)S(1)} %shard_map.51), channel_id=1, source_target_pairs={{0,8},{8,0},{1,9},{9,1},{2,10},{10,2},{3,11},{11,3},{4,12},{12,4},... | collective-permute-start | bytes 786440 | tf_op jit(solution)/shard_map/ppermute | solution.py:389
  64.7 11.5 %all-to-all-start.2 = ((bf16[16,32,256]{2,1,0:T(8,128)(2,1)}), bf16[16,32,256]{2,1,0:T(8,128)(2,1)S(1)}, u32[]{:S(2)}, u32[]{:S(2)}) async-start(bf16[16,32,256]{2,1,0:T(8,128)(2,1)} %bitcast.12.refs_4_), calls=%async_computation.2 | async-start | bytes 524288 | tf_op jit(solution)/shard_map/all_to_all | solution.py:395
  76.9 11.8 %all-to-all-start.3 = ((bf16[8,4,8,128]{3,2,1,0:T(8,128)(2,1)}), bf16[8,4,8,128]{3,2,1,0:T(8,128)(2,1)S(1)}, u32[]{:S(2)}, u32[]{:S(2)}) async-start(bf16[8,4,8,128]{3,2,1,0:T(8,128)(2,1)} %bitcast.17.refs_4_), calls=%async_computation.3 | async-start | bytes 131072 | tf_op jit(solution)/shard_map/all_to_all | solution.py:401
  89.4 21.0 %all-to-all-start.4 = ((bf16[16,8,8,128]{3,2,1,0:T(8,128)(2,1)}), bf16[16,8,8,128]{3,2,1,0:T(8,128)(2,1)S(1)}, u32[]{:S(2)}, u32[]{:S(2)}) async-start(bf16[16,8,8,128]{3,2,1,0:T(8,128)(2,1)} %broadcast_in_dim.8.refs_6_), calls=%async_computation.4 | async-start | bytes 524288 | tf_op jit(solution)/shard_map/all_to_all | solution.py:407
  110.4 3.2 %collective-permute-start.13 = (bf16[16,8,8,128]{3,2,1,0:T(8,128)(2,1)S(1)}, bf16[16,8,8,128]{3,2,1,0:T(8,128)(2,1)S(1)}, u32[]{:S(2)}, u32[]{:S(2)}) collective-permute-start(bf16[16,8,8,128]{3,2,1,0:T(8,128)(2,1)S(1)} %all-to-all-done.4.refs_8_), channel_id=1, source_target_pairs={{0,8},{8,0},{1,9},{9,1},{2,10},{10,2},{3,11},{11,3},{4,12},{12,4},... | collective-permute-start | bytes 786440 | tf_op jit(solution)/shard_map/ppermute | solution.py:409

commit v4 on v3

--- a/solution.py
+++ b/solution.py
@@ -172,14 +172,14 @@
         out[at] = result
 
 
-def reduce_in(got, wait_for):
+def reduce_in(got):
     count, rows, wide = got.shape
     return call(
-        after(reduce_in_kernel, 1, len(wait_for)),
+        reduce_in_kernel,
         kept((count, rows, wide - TAIL), BF16),
-        in_specs=[whole()] + anywhere(len(wait_for)),
+        in_specs=[whole()],
         out_specs=whole(),
-    )(got, *wait_for)
+    )(got)
 
 
 def expert_kernel(slot_exp, half_at, slots, w_in_any, w_out_any, out, w_in, w_out, sems):
@@ -234,7 +234,9 @@
 
 
 def weights_kernel(pieces, core, tok, *refs):
-    weights, stats, logits, table, sems = refs[pieces:]
+    earlier = refs[: len(refs) - pieces - 6]
+    refs = refs[len(earlier) :]
+    weights, one, two, logits, table, sems = refs[pieces:]
     blocks, width, wide = table.shape
     half = width // 2
 
@@ -260,36 +262,49 @@
         for lanes in range(0, wide, 128):
             some = block[:, lanes : lanes + 128]
             peaks = some if peaks is None else jnp.maximum(peaks, some)
-    peak = jnp.max(peaks, axis=1, keepdims=True)
+    peak = jnp.broadcast_to(jnp.max(peaks, axis=1, keepdims=True), peaks.shape)
     sums = jnp.zeros_like(peaks)
     for lanes in range(0, blocks * wide, 128):
         block = jnp.exp(logits[:, lanes : lanes + 128] - peak)
         weights[:, lanes : lanes + 128] = block.astype(BF16)
         sums += block
-    lane = lax.broadcasted_iota(jnp.int32, stats.shape, 1)
-    stats[...] = jnp.where(lane < 64, peak, jnp.sum(sums, axis=1, keepdims=True))
-
-
-def combine_weights(core, tokens, own, other, wait_for, steps=3):
+    total = jnp.broadcast_to(jnp.sum(sums, axis=1, keepdims=True), peaks.shape)
+    if earlier:
+        top = jnp.maximum(earlier[0][...], peak)
+        before, now = jnp.exp(earlier[0][...] - top), jnp.exp(peak - top)
+        total = earlier[1][...] * before + total * now
+        one[...], two[...] = before / total, now / total
+    else:
+        one[...], two[...] = peak, total
+
+
+def combine_weights(core, tokens, own, other, wait_for, earlier=(), steps=3):
+    stats = pl.BlockSpec((tokens.shape[0] // steps, 128), lambda i, core: (i, 0))
     count, width = tokens.shape
     blocks = sum(piece.shape[0] for piece in own)
     wide = own[0].shape[2]
     rows = count // steps
     pieces = [far_memory(piece) for piece in own + other]
     return call(
-        after(functools.partial(weights_kernel, len(pieces)), 2 + len(pieces), len(wait_for)),
-        [pltpu.HBM((count, blocks * wide), BF16), pltpu.HBM((count, 128), F32)],
+        after(
+            functools.partial(weights_kernel, len(pieces)),
+            2 + len(earlier) + len(pieces),
+            len(wait_for),
+        ),
+        [pltpu.HBM((count, blocks * wide), BF16)] + [pltpu.HBM((count, 128), F32)] * 2,
         micros=2 * blocks,
         limit=40 << 20,
         grid_spec=pltpu.PrefetchScalarGridSpec(
             num_scalar_prefetch=1,
             grid=(steps,),
             in_specs=[pl.BlockSpec((rows, width), lambda i, core: (i, 0))]
+            + [stats] * len(earlier)
             + [pl.BlockSpec(memory_space=pltpu.HBM)] * len(pieces)
             + anywhere(len(wait_for)),
             out_specs=[
                 pl.BlockSpec((rows, blocks * wide), lambda i, core: (i, 0)),
-                pl.BlockSpec((rows, 128), lambda i, core: (i, 0)),
+                stats,
+                stats,
             ],
             scratch_shapes=[
                 pltpu.VMEM((rows, blocks * wide), F32),
@@ -297,54 +312,64 @@
                 pltpu.SemaphoreType.DMA((len(pieces),)),
             ],
         ),
-    )(core, far_memory(tokens), *pieces, *wait_for)
-
-
-def output_kernel(parts, place, *refs):
-    weights, stats = refs[:parts], refs[parts : 2 * parts]
-    own, other, out, table = refs[2 * parts :]
+    )(core, far_memory(tokens), *map(far_memory, earlier), *pieces, *wait_for)
+
+
+def output_kernel(parts, steps, place, *refs):
+    sources = refs[: 2 * parts]
+    own, other, out = refs[2 * parts : 2 * parts + 3]
+    landed, (table, sems) = refs[2 * parts + 3 : -2], refs[-2:]
+    weights, scales = landed[:parts], landed[parts:]
     half = own.shape[0] * own.shape[2]
     groups = own.shape[1]
-
-    @pl.when(pl.program_id(0) == 0)
-    def _():
-        for at in range(groups):
-            group = place[1 + at]
-            for rows, start in ((own, place[0]), (other, 1 - place[0])):
-                block = rows[:, group].astype(F32).reshape(half, own.shape[3])
-                here = pl.multiple_of(at * 2 * half + start * half, half)
-                table[pl.ds(here, half), :] = block.astype(BF16)
-
-    peaks = [part[:, 0:1] for part in stats]
-    top = functools.reduce(jnp.maximum, peaks)
-    scales = [jnp.exp(peak - top) for peak in peaks]
-    total = sum(part[:, 64:65] * scale for part, scale in zip(stats, scales, strict=True))
-    mixed = jnp.zeros(out.shape, F32)
-    start = 0
-    for part, scale in zip(weights, scales, strict=True):
-        rows = table[start : start + part.shape[1], :]
-        mixed += jnp.dot(part[...], rows, preferred_element_type=F32) * (scale / total)
-        start += part.shape[1]
-    out[...] = mixed.astype(BF16)
-
-
-def output(place, weights, stats, own, other, steps=5):
+    count = out.shape[0] // steps
+    copies = []
+    for step in range(steps):
+        rows = pl.ds(step * count, count)
+        for source, to in zip(sources, landed, strict=True):
+            copies.append(
+                pltpu.make_async_copy(source.at[rows], to.at[rows], sems.at[len(copies)])
+            )
+            copies[-1].start()
+    for at in range(groups):
+        group = place[1 + at]
+        for rows, start in ((own, place[0]), (other, 1 - place[0])):
+            block = rows[:, group].astype(F32).reshape(half, own.shape[3])
+            here = pl.multiple_of(at * 2 * half + start * half, half)
+            table[pl.ds(here, half), :] = block.astype(BF16)
+    for step in range(steps):
+        rows = pl.ds(step * count, count)
+        for copy in copies[step * 2 * parts : (step + 1) * 2 * parts]:
+            copy.wait()
+        mixed = jnp.zeros((count, out.shape[1]), F32)
+        start = 0
+        for part, scale in zip(weights, scales, strict=True):
+            slots = table[start : start + part.shape[1], :]
+            product = jnp.dot(part[rows, :], slots, preferred_element_type=F32)
+            mixed += product * scale[rows, :]
+            start += part.shape[1]
+        out[rows, :] = mixed.astype(BF16)
+
+
+def output(place, weights, scales, own, other, steps=5):
     count = weights[0].shape[0]
     slots = sum(part.shape[1] for part in weights)
     wide = own.shape[3]
-    rows = count // steps
-    return call(
-        functools.partial(output_kernel, len(weights)),
+    parts = len(weights)
+    return call(
+        functools.partial(output_kernel, parts, steps),
         jax.ShapeDtypeStruct((count, wide), BF16),
         limit=24 << 20,
-        grid=(steps,),
         in_specs=[pl.BlockSpec(memory_space=pltpu.SMEM)]
-        + [pl.BlockSpec((rows, part.shape[1]), lambda i: (i, 0)) for part in weights]
-        + [pl.BlockSpec((rows, 128), lambda i: (i, 0)) for part in stats]
+        + [pl.BlockSpec(memory_space=pltpu.HBM)] * (2 * parts)
         + [whole(), whole()],
-        out_specs=pl.BlockSpec((rows, wide), lambda i: (i, 0)),
-        scratch_shapes=[pltpu.VMEM((slots, wide), BF16)],
-    )(place, *map(far_memory, weights), *map(far_memory, stats), own, other)
+        out_specs=whole(),
+        scratch_shapes=[pltpu.VMEM(part.shape, part.dtype) for part in weights + scales]
+        + [
+            pltpu.VMEM((slots, wide), BF16),
+            pltpu.SemaphoreType.DMA((steps * 2 * parts,)),
+        ],
+    )(place, *map(far_memory, weights + scales), own, other)
 
 
 def shift(by):
@@ -368,52 +393,39 @@
 
     own, send = dispatch(core, tokens, slot_embed)
     merged = merge(own, lax.ppermute(send, "core", SWAP))
+    near = lax.optimization_barrier((near, merged))[0]
     here = jnp.stack([mine, near])
-    here_there = lax.ppermute(here, "core", SWAP)
     down = lax.ppermute(here, "y", shift(1))
     up = lax.ppermute(here, "y", shift(-1))
     got = lax.all_to_all(merged.reshape(nx * nh, part, -1), ("x", "zh"), 0, 0)
-    spread = reduce_in(got, [here_there])
+    spread = reduce_in(got)
     far = [lax.ppermute(down[:1], "y", shift(1)), lax.ppermute(up[1:], "y", shift(-1))]
-    first, first_stats = combine_weights(core, tokens, [here], [here_there], [spread] + far)
-    far_there = [lax.ppermute(piece, "core", SWAP) for piece in far]
-    down_there, up_there = (lax.ppermute(piece, "core", SWAP) for piece in (down, up))
     slots_own = lax.all_to_all(spread, ("x", "zh"), 0, 0).reshape(half, features)
-    slots_own, first_stats, down_there, up_there, far_there = lax.optimization_barrier(
-        (slots_own, first_stats, down_there, up_there, far_there)
-    )
+    slots_own, far = lax.optimization_barrier((slots_own, far))
     slots_other = lax.ppermute(slots_own, "core", SWAP)
 
     done_own = experts(core, slots_own, w_in, w_out, F32)
     done_other = experts(1 - core, slots_other, w_in, w_out, BF16)
+    table_own = [here, down, up] + far
+    table_other = [lax.ppermute(piece, "core", SWAP) for piece in table_own]
     got = lax.ppermute(done_other, "core", SWAP)
+    got, table_other = lax.optimization_barrier((got, table_other))
 
     cut = (done_own + got.astype(F32)).astype(BF16)
-    cut = cut.reshape(nx, half // nx, ny, features // ny).transpose(0, 2, 1, 3)
-    cut = cut.reshape(nx * ny, half // nx, features // ny)
-    second, second_stats = combine_weights(core, tokens, [down], [down_there], [cut])
-    got = lax.all_to_all(cut, ("x", "y"), 0, 0)
-    got, second_stats = lax.optimization_barrier((got, second_stats))
-    got = jnp.sum(got.reshape((nx, ny) + got.shape[1:]).astype(F32), axis=0).astype(BF16)
-    cut = got.reshape(ny, nh, part, nl, features // (ny * nl)).transpose(1, 3, 0, 2, 4)
-    cut = cut.reshape((nh * nl, ny, part, -1))
-    third, third_stats = combine_weights(core, tokens, [up], [up_there], [cut])
-    got = lax.all_to_all(cut, ("zh", "zl"), 0, 0)
-    got, third_stats = lax.optimization_barrier((got, third_stats))
-    got = jnp.sum(got.reshape((nh, nl) + got.shape[1:]).astype(F32), axis=0).astype(BF16)
-    got = got.transpose(1, 0, 2, 3).reshape((ny * nl,) + got.shape[2:])
-    spread = jnp.broadcast_to(got[None], (nx * nh,) + got.shape)
-    fourth, fourth_stats = combine_weights(core, tokens, far, far_there, [spread])
+    cut = cut.reshape(nx * nh, part, ny * nl, -1).transpose(0, 2, 1, 3)
+    cut = cut.reshape((nx * nh * ny * nl, part, -1))
+    first, *stats = combine_weights(core, tokens, table_own[:2], table_other[:2], [cut])
+    got = lax.all_to_all(cut, ("x", "zh", "y", "zl"), 0, 0)
+    got, stats = lax.optimization_barrier((got, stats))
+    got = jnp.sum(got.reshape((nx * nh, ny * nl) + got.shape[1:]).astype(F32), axis=0)
+    spread = jnp.broadcast_to(got.astype(BF16)[None], (nx * nh,) + got.shape)
+    second, *scales = combine_weights(
+        core, tokens, table_own[2:], table_other[2:], [spread], earlier=stats
+    )
     out_own = lax.all_to_all(spread, ("x", "zh"), 0, 0)
-    out_own, fourth_stats = lax.optimization_barrier((out_own, fourth_stats))
+    out_own, scales = lax.optimization_barrier((out_own, scales))
     out_other = lax.ppermute(out_own, "core", SWAP)
-    return output(
-        place,
-        [first, second, third, fourth],
-        [first_stats, second_stats, third_stats, fourth_stats],
-        out_own,
-        out_other,
-    )
+    return output(place, [first, second], scales, out_own, out_other)
 
 
 def solution(mesh):

time: 122 us -> 112 us (0.918)
  Pallas kernels: 50.7 us -> 40.3 us
  waiting for transfers between devices: 14.5 us -> 24.2 us
  starting transfers between devices: 50.6 us -> 44.7 us
  local copies, waits for them, and re-layouts: 4.99 us -> 1.05 us
    pallas_call x6 -> x4, Pallas kernels: 37.8 us -> 27.5 us  [the longest x2 20.6 us: combine_weights(): call(after(functools.partial(weights_kernel, len(pieces)), 2 + len(earlie...]
    all_to_all x1, waiting for transfers between devices: 5.92 us -> 9.95 us  [on_device(): got = lax.all_to_all(merged.reshape(nx * nh, part, -1), ('x', 'zh'), 0, 0)]
    all_to_all x1, starting transfers between devices: 8.83 us -> 4.85 us  [on_device(): out_own = lax.all_to_all(spread, ('x', 'zh'), 0, 0)]
    all_to_all x1, waiting for transfers between devices: 0.95 us -> 4.46 us  [on_device(): lax.all_to_all(spread, ('x', 'zh'), 0, 0).reshape(half, features)]
    all_to_all x1, waiting for transfers between devices: 4.67 us -> 1.3 us  [on_device(): out_own = lax.all_to_all(spread, ('x', 'zh'), 0, 0)]
    all_to_all x2 -> x1, waiting for transfers between devices: 0.65 us -> 3.86 us  [on_device(): got = lax.all_to_all(cut, ('x', 'zh', 'y', 'zl'), 0, 0)]
    ppermute x1, starting transfers between devices: 2.55 us -> 0.09 us  [on_device(): near = lax.ppermute(mine, 'zl', SWAP)]
    ppermute x1, starting transfers between devices: 1.04 us -> 3.33 us  [on_device(): merged = merge(own, lax.ppermute(send, 'core', SWAP))]
  transfers between devices with their start and end apart: 19 -> 18, of which waited for: 6 -> 8; matrix products, arithmetic and copies ran while one was open for 1% -> 0% of each run, Pallas kernels for 33% -> 26%
where the time goes in v4:
time: 112 us
  starting transfers between devices  44.7 us (40%)
  Pallas kernels  40.3 us (36%)
  waiting for transfers between devices  24.2 us (22%)
  other arithmetic  1.13 us (1%)
    pallas_call x2, Pallas kernels, combine_weights(): call(after(functools.partial(weights_kernel, len(pieces)), 2 + len(earlie...  20.6 us
    all_to_all x1, waiting for transfers between devices, on_device(): got = lax.all_to_all(merged.reshape(nx * nh, part, -1), ('x', 'zh'), 0, 0)  9.95 us
    all_to_all x1, starting transfers between devices, on_device(): got = lax.all_to_all(cut, ('x', 'zh', 'y', 'zl'), 0, 0)  9.59 us
    all_to_all x1, starting transfers between devices, on_device(): got = lax.all_to_all(merged.reshape(nx * nh, part, -1), ('x', 'zh'), 0, 0)  9.01 us
    pallas_call x2, Pallas kernels, experts(): call(after(functools.partial(expert_kernel, slots.shape[0] // count), 4,...  6.3 us
    pallas_call x1, Pallas kernels, output(): call(functools.partial(output_kernel, parts, steps), jax.ShapeDtypeStruct...  5.87 us
    pallas_call x1, Pallas kernels, dispatch(): call(functools.partial(dispatch_kernel, parts), micros=6, outs=[kept(shap...  5.48 us
    all_to_all x1, starting transfers between devices, on_device(): out_own = lax.all_to_all(spread, ('x', 'zh'), 0, 0)  4.85 us
  transfers between devices with their start and end apart: 18, of which 8 were waited for; matrix products, arithmetic and copies ran while one was open for 0% of the time, Pallas kernels for 26%

profile of v4, /device:TPU:1, one launch (start us, length us, event | category | flops | bytes accessed | tf_op | source)
XLA Modules:
  0.0 111.9 jit_solution(1695438074076858006)
XLA Ops:
  0.0 5.5 %shard_map.46 = (f32[128,1152]{1,0:T(8,128)S(1)}, bf16[128,1152]{1,0:T(8,128)(2,1)S(1)}) custom-call(s32[1]{0:T(128)} %bitcast.core.refs_0_, bf16[1920,1024]{1,0:T(8,128)(2,1)} %refs_1_.3, bf16[1024,256]{1,0:T(8,128)(2,1)} %embed_any.1), custom_call_target="tpu_custom_call" | custom-call | bytes 180000 | tf_op jit(solution)/shard_map/pallas_call | solution.py:119
  5.5 3.3 %collective-permute-start.1 = (bf16[128,1152]{1,0:T(8,128)(2,1)S(1)}, bf16[128,1152]{1,0:T(8,128)(2,1)S(1)}, u32[]{:S(2)}, u32[]{:S(2)}) collective-permute-start(bf16[128,1152]{1,0:T(8,128)(2,1)S(1)} %get-tuple-element.30), channel_id=1, source_target_pairs={{0,8},{8,0},{1,9},{9,1},{2,10},{10,2},{3,11},{11,3},{4,12},{12,4},... | collective-permute-start | bytes 884744 | tf_op jit(solution)/shard_map/ppermute | solution.py:395
  8.8 0.1 collective-permute-start
  8.9 1.1 collective-permute-done.1.got
  10.0 1.1 shard_map.47
  11.1 9.0 %all-to-all-start = ((bf16[16,8,1152]{2,1,0:T(8,128)(2,1)}), bf16[16,8,1152]{2,1,0:T(8,128)(2,1)S(1)}, u32[]{:S(2)}, u32[]{:S(2)}) async-start(bf16[16,8,1152]{2,1,0:T(8,128)(2,1)} %bitcast.9), calls=%async_computation | async-start | bytes 589824 | tf_op jit(solution)/shard_map/all_to_all | solution.py:400
  20.2 0.0 collective-permute-done
  20.2 0.1 pad_maximum_fusion.refs_2_
  20.3 1.4 %collective-permute-start.2 = (bf16[2,512,256]{2,1,0:T(8,128)(2,1)S(1)}, bf16[2,512,256]{2,1,0:T(8,128)(2,1)S(1)}, u32[]{:S(2)}, u32[]{:S(2)}) collective-permute-start(bf16[2,512,256]{2,1,0:T(8,128)(2,1)S(1)} %pad_maximum_fusion.refs_2_), channel_id=1, source_target_pairs={{0,2},{2,4},{4,6},{6,0},{1,3},{3,5},{5,7},{7,1},{8,10},{10,12},{12... | collective-permute-start | bytes 1572872 | tf_op jit(solution)/shard_map/ppermute | solution.py:398
  21.6 1.5 %collective-permute-start.4 = (bf16[2,512,256]{2,1,0:T(8,128)(2,1)S(1)}, bf16[2,512,256]{2,1,0:T(8,128)(2,1)S(1)}, u32[]{:S(2)}, u32[]{:S(2)}) collective-permute-start(bf16[2,512,256]{2,1,0:T(8,128)(2,1)S(1)} %pad_maximum_fusion.refs_2_), channel_id=1, source_target_pairs={{0,6},{2,0},{4,2},{6,4},{1,7},{3,1},{5,3},{7,5},{8,14},{10,8},{12,... | collective-permute-start | bytes 1572872 | tf_op jit(solution)/shard_map/ppermute | solution.py:399
  23.2 9.9 %all-to-all-done.got = bf16[16,8,1152]{2,1,0:T(8,128)(2,1)S(1)} async-done(((bf16[16,8,1152]{2,1,0:T(8,128)(2,1)}), bf16[16,8,1152]{2,1,0:T(8,128)(2,1)S(1)}, u32[]{:S(2)}, u32[]{:S(2)}) %all-to-all-start) | async-done | bytes 294944 | tf_op jit(solution)/shard_map/all_to_all | solution.py:400
  33.1 1.0 shard_map.48
  34.1 3.5 %all-to-all-start.1 = ((bf16[16,8,1024]{2,1,0:T(8,128)(2,1)}), bf16[16,8,1024]{2,1,0:T(8,128)(2,1)S(1)}, u32[]{:S(2)}, u32[]{:S(2)}) async-start(bf16[16,8,1024]{2,1,0:T(8,128)(2,1)} %shard_map.48), calls=%async_computation.1 | async-start | bytes 524288 | tf_op jit(solution)/shard_map/all_to_all | solution.py:403
  37.6 0.0 collective-permute-done.2.refs_3_
  37.7 1.4 %collective-permute-start.3 = (bf16[1,512,256]{2,1,0:T(8,128)(2,1)S(1)}, bf16[1,512,256]{2,1,0:T(8,128)(2,1)S(1)}, u32[]{:S(2)}, u32[]{:S(2)}) collective-permute-start(bf16[1,512,256]{2,1,0:T(8,128)(2,1)S(1)} %slice.8), channel_id=1, source_target_pairs={{0,2},{2,4},{4,6},{6,0},{1,3},{3,5},{5,7},{7,1},{8,10},{10,12},{12... | collective-permute-start | bytes 786440 | tf_op jit(solution)/shard_map/ppermute | solution.py:402
  39.1 0.0 collective-permute-done.4.refs_4_
  39.1 1.5 %collective-permute-start.5 = (bf16[1,512,256]{2,1,0:T(8,128)(2,1)S(1)}, bf16[1,512,256]{2,1,0:T(8,128)(2,1)S(1)}, u32[]{:S(2)}, u32[]{:S(2)}) collective-permute-start(bf16[1,512,256]{2,1,0:T(8,128)(2,1)S(1)} %slice.9), channel_id=1, source_target_pairs={{0,6},{2,0},{4,2},{6,4},{1,7},{3,1},{5,3},{7,5},{8,14},{10,8},{12,... | collective-permute-start | bytes 786440 | tf_op jit(solution)/shard_map/ppermute | solution.py:402
  40.7 2.4 %collective-permute-start.8 = (bf16[2,512,256]{2,1,0:T(8,128)(2,1)S(1)}, bf16[2,512,256]{2,1,0:T(8,128)(2,1)S(1)}, u32[]{:S(2)}, u32[]{:S(2)}) collective-permute-start(bf16[2,512,256]{2,1,0:T(8,128)(2,1)S(1)} %pad_maximum_fusion.refs_2_), channel_id=1, source_target_pairs={{0,8},{8,0},{1,9},{9,1},{2,10},{10,2},{3,11},{11,3},{4,12},{12,4},... | collective-permute-start | bytes 1572872 | tf_op jit(solution)/shard_map/ppermute | solution.py:410
  43.1 1.9 %collective-permute-done.3.refs_5_ = bf16[1,512,256]{2,1,0:T(8,128)(2,1)S(1)} collective-permute-done((bf16[1,512,256]{2,1,0:T(8,128)(2,1)S(1)}, bf16[1,512,256]{2,1,0:T(8,128)(2,1)S(1)}, u32[]{:S(2)}, u32[]{:S(2)}) %collective-permute-start.3) | collective-permute-done | bytes 262176 | tf_op jit(solution)/shard_map/ppermute | solution.py:402
  45.0 0.0 collective-permute-done.5.refs_6_
  45.0 4.5 %all-to-all-done.1 = bf16[16,8,1024]{2,1,0:T(8,128)(2,1)S(1)} async-done(((bf16[16,8,1024]{2,1,0:T(8,128)(2,1)}), bf16[16,8,1024]{2,1,0:T(8,128)(2,1)S(1)}, u32[]{:S(2)}, u32[]{:S(2)}) %all-to-all-start.1) | async-done | bytes 262176 | tf_op jit(solution)/shard_map/all_to_all | solution.py:403
  49.4 2.5 %collective-permute-start.6 = (bf16[128,1024]{1,0:T(8,128)(2,1)S(1)}, bf16[128,1024]{1,0:T(8,128)(2,1)S(1)}, u32[]{:S(2)}, u32[]{:S(2)}) collective-permute-start(bf16[128,1024]{1,0:T(8,128)(2,1)S(1)} %bitcast.18), channel_id=1, source_target_pairs={{0,8},{8,0},{1,9},{9,1},{2,10},{10,2},{3,11},{11,3},{4,12},{12,4},... | collective-permute-start | bytes 786440 | tf_op jit(solution)/shard_map/ppermute | solution.py:405
  52.0 0.1 collective-permute-start.9
  52.1 0.4 collective-permute-start.10
  52.5 0.1 collective-permute-start.11
  52.6 0.6 collective-permute-done.6.refs_1_
  53.1 0.4 collective-permute-start.12
  53.5 3.2 %shard_map.49 = bf16[128,1024]{1,0:T(8,128)(2,1)S(1)} custom-call(s32[1]{0:T(128)S(6)} %sub.12.refs_0_, bf16[128,1024]{1,0:T(8,128)(2,1)S(1)} %collective-permute-done.6.refs_1_, bf16[16,1024,128]{2,1,0:T(8,128)(2,1)} %refs_2_.3, bf16[16,128,1024]{2,1,0:T(8,128)(2,1)} %refs_3_.3), custom_call_target="tpu_custom_call" | custom-call | bytes 90000 | tf_op jit(solution)/shard_map/pallas_call | solution.py:220
  56.7 0.0 collective-permute-done.8.refs_4_
  56.7 0.4 collective-permute-start.7
  57.1 3.2 %shard_map.50 = f32[128,1024]{1,0:T(8,128)S(1)} custom-call(s32[1]{0:T(128)} %bitcast.core.refs_0_, bf16[128,1024]{1,0:T(8,128)(2,1)S(1)} %bitcast.19, bf16[16,1024,128]{2,1,0:T(8,128)(2,1)} %refs_2_.3, bf16[16,128,1024]{2,1,0:T(8,128)(2,1)} %refs_3_.3), custom_call_target="tpu_custom_call" | custom-call | bytes 90000 | tf_op jit(solution)/shard_map/pallas_call | solution.py:220
  60.3 0.0 collective-permute-done.9.refs_5_
  60.3 0.0 collective-permute-done.10.refs_7_
  60.3 0.0 collective-permute-done.11.refs_8_
  60.4 0.9 add_convert_fusion
  61.3 9.6 %all-to-all-start.2 = ((bf16[128,8,128]{2,1,0:T(8,128)(2,1)}), bf16[128,8,128]{2,1,0:T(8,128)(2,1)S(1)}, u32[]{:S(2)}, u32[]{:S(2)}) async-start(bf16[128,8,128]{2,1,0:T(8,128)(2,1)} %bitcast.13.refs_6_), calls=%async_computation.2 | async-start | bytes 524288 | tf_op jit(solution)/shard_map/all_to_all | solution.py:418
  70.9 10.1 %shard_map.51 = (bf16[1920,1024]{1,0:T(8,128)(2,1)}, f32[1920,128]{1,0:T(8,128)}, f32[1920,128]{1,0:T(8,128)}) custom-call(s32[1]{0:T(128)} %bitcast.core.refs_0_, bf16[1920,1024]{1,0:T(8,128)(2,1)} %refs_1_.3, bf16[2,512,256]{2,1,0:T(8,128)(2,1)} %copy-done.1, bf16[2,512,256]{2,1,0:T(8,128)(2,1)} %copy-done.3, bf16[2,512,256]{2,1,0:T(8,128)(2,1)} %copy-done.5, ...), custom_call_target="tpu_custom_call" | custom-call | bytes 240000 | tf_op jit(solution)/shard_map/pallas_call | solution.py:288
  81.0 3.9 %all-to-all-done.2 = bf16[128,8,128]{2,1,0:T(8,128)(2,1)S(1)} async-done(((bf16[128,8,128]{2,1,0:T(8,128)(2,1)}), bf16[128,8,128]{2,1,0:T(8,128)(2,1)S(1)}, u32[]{:S(2)}, u32[]{:S(2)}) %all-to-all-start.2) | async-done | bytes 262176 | tf_op jit(solution)/shard_map/all_to_all | solution.py:418
  84.9 0.8 broadcast_in_dim.2.refs_10_
  85.7 4.8 %all-to-all-start.3 = ((bf16[16,8,8,128]{3,2,1,0:T(8,128)(2,1)}), bf16[16,8,8,128]{3,2,1,0:T(8,128)(2,1)S(1)}, u32[]{:S(2)}, u32[]{:S(2)}) async-start(bf16[16,8,8,128]{3,2,1,0:T(8,128)(2,1)} %broadcast_in_dim.2.refs_10_), calls=%async_computation.3 | async-start | bytes 524288 | tf_op jit(solution)/shard_map/all_to_all | solution.py:425
  90.5 0.1 stack.50
  90.6 0.1 stack.47
  90.7 10.6 %shard_map.52 = (bf16[1920,1024]{1,0:T(8,128)(2,1)}, f32[1920,128]{1,0:T(8,128)}, f32[1920,128]{1,0:T(8,128)}) custom-call(s32[1]{0:T(128)} %bitcast.core.refs_0_, bf16[1920,1024]{1,0:T(8,128)(2,1)} %refs_1_.3, f32[1920,128]{1,0:T(8,128)} %get-tuple-element.41.refs_2_, f32[1920,128]{1,0:T(8,128)} %get-tuple-element.42.refs_3_, ...), custom_call_target="tpu_custom_call" | custom-call | bytes 240000 | tf_op jit(solution)/shard_map/pallas_call | solution.py:288
  101.3 1.3 %all-to-all-done.3.refs_4_ = bf16[16,8,8,128]{3,2,1,0:T(8,128)(2,1)S(1)} async-done(((bf16[16,8,8,128]{3,2,1,0:T(8,128)(2,1)}), bf16[16,8,8,128]{3,2,1,0:T(8,128)(2,1)S(1)}, u32[]{:S(2)}, u32[]{:S(2)}) %all-to-all-start.3) | async-done | bytes 262176 | tf_op jit(solution)/shard_map/all_to_all | solution.py:425
  102.6 2.1 %collective-permute-start.13 = (bf16[16,8,8,128]{3,2,1,0:T(8,128)(2,1)S(1)}, bf16[16,8,8,128]{3,2,1,0:T(8,128)(2,1)S(1)}, u32[]{:S(2)}, u32[]{:S(2)}) collective-permute-start(bf16[16,8,8,128]{3,2,1,0:T(8,128)(2,1)S(1)} %all-to-all-done.3.refs_4_), channel_id=1, source_target_pairs={{0,8},{8,0},{1,9},{9,1},{2,10},{10,2},{3,11},{11,3},{4,12},{12,4},... | collective-permute-start | bytes 786440 | tf_op jit(solution)/shard_map/ppermute | solution.py:427
  104.7 0.1 pad_add_fusion.place
  104.8 1.1 collective-permute-done.13.refs_5_
  105.8 5.9 %shard_map.53 = bf16[1920,128]{1,0:T(8,128)(2,1)} custom-call(s32[9]{0:T(128)S(1)} %pad_add_fusion.place, bf16[1920,1024]{1,0:T(8,128)(2,1)} %get-tuple-element.38.refs_0_, bf16[1920,1024]{1,0:T(8,128)(2,1)} %get-tuple-element.47.refs_1_, f32[1920,128]{1,0:T(8,128)} %get-tuple-element.50.refs_2_, f32[1920,128]{1,0:T(8,128)} %get-tuple-element.51.refs_3_, ...), custom_call_target="tpu_custom_call" | custom-call | bytes 30000 | tf_op jit(solution)/shard_map/pallas_call | solution.py:359
  (30 shorter events, 0.2 us)
Async XLA Ops:
  0.0 8.8 %copy-start = (bf16[1024,256]{1,0:T(8,128)(2,1)S(1)}, bf16[1024,256]{1,0:T(8,128)(2,1)}, u32[]{:S(2)}) copy-start(bf16[1024,256]{1,0:T(8,128)(2,1)} %embed_any.1) | copy-start | bytes 1572868
  5.5 4.5 %collective-permute-start.1 = (bf16[128,1152]{1,0:T(8,128)(2,1)S(1)}, bf16[128,1152]{1,0:T(8,128)(2,1)S(1)}, u32[]{:S(2)}, u32[]{:S(2)}) collective-permute-start(bf16[128,1152]{1,0:T(8,128)(2,1)S(1)} %get-tuple-element.30), channel_id=1, source_target_pairs={{0,8},{8,0},{1,9},{9,1},{2,10},{10,2},{3,11},{11,3},{4,12},{12,4},... | collective-permute-start | bytes 884744 | tf_op jit(solution)/shard_map/ppermute | solution.py:395
  8.8 11.3 %collective-permute-start = (bf16[512,256]{1,0:T(8,128)(2,1)S(1)}, bf16[512,256]{1,0:T(8,128)(2,1)S(1)}, u32[]{:S(2)}, u32[]{:S(2)}) collective-permute-start(bf16[512,256]{1,0:T(8,128)(2,1)S(1)} %constant_dynamic-slice_fusion), channel_id=1, source_target_pairs={{0,1},{1,0},{2,3},{3,2},{4,5},{5,4},{6,7},{7,6},{8,9},{9,8},{10,11... | collective-permute-start | bytes 786440 | tf_op jit(solution)/shard_map/ppermute | solution.py:389
  11.1 22.0 %all-to-all-start = ((bf16[16,8,1152]{2,1,0:T(8,128)(2,1)}), bf16[16,8,1152]{2,1,0:T(8,128)(2,1)S(1)}, u32[]{:S(2)}, u32[]{:S(2)}) async-start(bf16[16,8,1152]{2,1,0:T(8,128)(2,1)} %bitcast.9), calls=%async_computation | async-start | bytes 589824 | tf_op jit(solution)/shard_map/all_to_all | solution.py:400
  20.3 36.4 %copy-start.1 = (bf16[2,512,256]{2,1,0:T(8,128)(2,1)}, bf16[2,512,256]{2,1,0:T(8,128)(2,1)S(1)}, u32[]{:S(2)}) copy-start(bf16[2,512,256]{2,1,0:T(8,128)(2,1)S(1)} %pad_maximum_fusion.refs_2_) | copy-start | bytes 1572868
  20.3 17.4 %collective-permute-start.2 = (bf16[2,512,256]{2,1,0:T(8,128)(2,1)S(1)}, bf16[2,512,256]{2,1,0:T(8,128)(2,1)S(1)}, u32[]{:S(2)}, u32[]{:S(2)}) collective-permute-start(bf16[2,512,256]{2,1,0:T(8,128)(2,1)S(1)} %pad_maximum_fusion.refs_2_), channel_id=1, source_target_pairs={{0,2},{2,4},{4,6},{6,0},{1,3},{3,5},{5,7},{7,1},{8,10},{10,12},{12... | collective-permute-start | bytes 1572872 | tf_op jit(solution)/shard_map/ppermute | solution.py:398
  21.6 17.4 %collective-permute-start.4 = (bf16[2,512,256]{2,1,0:T(8,128)(2,1)S(1)}, bf16[2,512,256]{2,1,0:T(8,128)(2,1)S(1)}, u32[]{:S(2)}, u32[]{:S(2)}) collective-permute-start(bf16[2,512,256]{2,1,0:T(8,128)(2,1)S(1)} %pad_maximum_fusion.refs_2_), channel_id=1, source_target_pairs={{0,6},{2,0},{4,2},{6,4},{1,7},{3,1},{5,3},{7,5},{8,14},{10,8},{12,... | collective-permute-start | bytes 1572872 | tf_op jit(solution)/shard_map/ppermute | solution.py:399
  34.1 15.3 %all-to-all-start.1 = ((bf16[16,8,1024]{2,1,0:T(8,128)(2,1)}), bf16[16,8,1024]{2,1,0:T(8,128)(2,1)S(1)}, u32[]{:S(2)}, u32[]{:S(2)}) async-start(bf16[16,8,1024]{2,1,0:T(8,128)(2,1)} %shard_map.48), calls=%async_computation.1 | async-start | bytes 524288 | tf_op jit(solution)/shard_map/all_to_all | solution.py:403
  37.7 19.0 %copy-start.3 = (bf16[2,512,256]{2,1,0:T(8,128)(2,1)}, bf16[2,512,256]{2,1,0:T(8,128)(2,1)S(1)}, u32[]{:S(2)}) copy-start(bf16[2,512,256]{2,1,0:T(8,128)(2,1)S(1)} %collective-permute-done.2.refs_3_) | copy-start | bytes 1572868
  37.7 7.3 %collective-permute-start.3 = (bf16[1,512,256]{2,1,0:T(8,128)(2,1)S(1)}, bf16[1,512,256]{2,1,0:T(8,128)(2,1)S(1)}, u32[]{:S(2)}, u32[]{:S(2)}) collective-permute-start(bf16[1,512,256]{2,1,0:T(8,128)(2,1)S(1)} %slice.8), channel_id=1, source_target_pairs={{0,2},{2,4},{4,6},{6,0},{1,3},{3,5},{5,7},{7,1},{8,10},{10,12},{12... | collective-permute-start | bytes 786440 | tf_op jit(solution)/shard_map/ppermute | solution.py:402
  39.1 17.6 %copy-start.2 = (bf16[2,512,256]{2,1,0:T(8,128)(2,1)}, bf16[2,512,256]{2,1,0:T(8,128)(2,1)S(1)}, u32[]{:S(2)}) copy-start(bf16[2,512,256]{2,1,0:T(8,128)(2,1)S(1)} %collective-permute-done.4.refs_4_) | copy-start | bytes 1572868
  39.1 5.9 %collective-permute-start.5 = (bf16[1,512,256]{2,1,0:T(8,128)(2,1)S(1)}, bf16[1,512,256]{2,1,0:T(8,128)(2,1)S(1)}, u32[]{:S(2)}, u32[]{:S(2)}) collective-permute-start(bf16[1,512,256]{2,1,0:T(8,128)(2,1)S(1)} %slice.9), channel_id=1, source_target_pairs={{0,6},{2,0},{4,2},{6,4},{1,7},{3,1},{5,3},{7,5},{8,14},{10,8},{12,... | collective-permute-start | bytes 786440 | tf_op jit(solution)/shard_map/ppermute | solution.py:402
  40.7 16.0 %collective-permute-start.8 = (bf16[2,512,256]{2,1,0:T(8,128)(2,1)S(1)}, bf16[2,512,256]{2,1,0:T(8,128)(2,1)S(1)}, u32[]{:S(2)}, u32[]{:S(2)}) collective-permute-start(bf16[2,512,256]{2,1,0:T(8,128)(2,1)S(1)} %pad_maximum_fusion.refs_2_), channel_id=1, source_target_pairs={{0,8},{8,0},{1,9},{9,1},{2,10},{10,2},{3,11},{11,3},{4,12},{12,4},... | collective-permute-start | bytes 1572872 | tf_op jit(solution)/shard_map/ppermute | solution.py:410
  45.0 7.0 %copy-start.7 = (bf16[1,512,256]{2,1,0:T(8,128)(2,1)}, bf16[1,512,256]{2,1,0:T(8,128)(2,1)S(1)}, u32[]{:S(2)}) copy-start(bf16[1,512,256]{2,1,0:T(8,128)(2,1)S(1)} %collective-permute-done.3.refs_5_) | copy-start | bytes 786436
  45.0 7.0 %copy-start.8 = (bf16[1,512,256]{2,1,0:T(8,128)(2,1)}, bf16[1,512,256]{2,1,0:T(8,128)(2,1)S(1)}, u32[]{:S(2)}) copy-start(bf16[1,512,256]{2,1,0:T(8,128)(2,1)S(1)} %collective-permute-done.5.refs_6_) | copy-start | bytes 786436
  49.4 3.7 %collective-permute-start.6 = (bf16[128,1024]{1,0:T(8,128)(2,1)S(1)}, bf16[128,1024]{1,0:T(8,128)(2,1)S(1)}, u32[]{:S(2)}, u32[]{:S(2)}) collective-permute-start(bf16[128,1024]{1,0:T(8,128)(2,1)S(1)} %bitcast.18), channel_id=1, source_target_pairs={{0,8},{8,0},{1,9},{9,1},{2,10},{10,2},{3,11},{11,3},{4,12},{12,4},... | collective-permute-start | bytes 786440 | tf_op jit(solution)/shard_map/ppermute | solution.py:405
  52.0 8.3 %collective-permute-start.9 = (bf16[2,512,256]{2,1,0:T(8,128)(2,1)S(1)}, bf16[2,512,256]{2,1,0:T(8,128)(2,1)S(1)}, u32[]{:S(2)}, u32[]{:S(2)}) collective-permute-start(bf16[2,512,256]{2,1,0:T(8,128)(2,1)S(1)} %collective-permute-done.2.refs_3_), channel_id=1, source_target_pairs={{0,8},{8,0},{1,9},{9,1},{2,10},{10,2},{3,11},{11,3},{4,12},{12,4},... | collective-permute-start | bytes 1572872 | tf_op jit(solution)/shard_map/ppermute | solution.py:410
  52.1 8.2 %collective-permute-start.10 = (bf16[2,512,256]{2,1,0:T(8,128)(2,1)S(1)}, bf16[2,512,256]{2,1,0:T(8,128)(2,1)S(1)}, u32[]{:S(2)}, u32[]{:S(2)}) collective-permute-start(bf16[2,512,256]{2,1,0:T(8,128)(2,1)S(1)} %collective-permute-done.4.refs_4_), channel_id=1, source_target_pairs={{0,8},{8,0},{1,9},{9,1},{2,10},{10,2},{3,11},{11,3},{4,12},{12,4},... | collective-permute-start | bytes 1572872 | tf_op jit(solution)/shard_map/ppermute | solution.py:410
  52.5 7.9 %collective-permute-start.11 = (bf16[1,512,256]{2,1,0:T(8,128)(2,1)}, bf16[1,512,256]{2,1,0:T(8,128)(2,1)S(1)}, u32[]{:S(2)}, u32[]{:S(2)}) collective-permute-start(bf16[1,512,256]{2,1,0:T(8,128)(2,1)} %copy-done.7), channel_id=1, source_target_pairs={{0,8},{8,0},{1,9},{9,1},{2,10},{10,2},{3,11},{11,3},{4,12},{12,4},... | collective-permute-start | bytes 786440 | tf_op jit(solution)/shard_map/ppermute | solution.py:410
  53.1 7.2 %collective-permute-start.12 = (bf16[1,512,256]{2,1,0:T(8,128)(2,1)}, bf16[1,512,256]{2,1,0:T(8,128)(2,1)S(1)}, u32[]{:S(2)}, u32[]{:S(2)}) collective-permute-start(bf16[1,512,256]{2,1,0:T(8,128)(2,1)} %copy-done.8), channel_id=1, source_target_pairs={{0,8},{8,0},{1,9},{9,1},{2,10},{10,2},{3,11},{11,3},{4,12},{12,4},... | collective-permute-start | bytes 786440 | tf_op jit(solution)/shard_map/ppermute | solution.py:410
  56.7 3.6 %copy-start.5 = (bf16[2,512,256]{2,1,0:T(8,128)(2,1)}, bf16[2,512,256]{2,1,0:T(8,128)(2,1)S(1)}, u32[]{:S(2)}) copy-start(bf16[2,512,256]{2,1,0:T(8,128)(2,1)S(1)} %collective-permute-done.8.refs_4_) | copy-start | bytes 1572868
  56.7 3.7 %collective-permute-start.7 = (bf16[128,1024]{1,0:T(8,128)(2,1)S(1)}, bf16[128,1024]{1,0:T(8,128)(2,1)S(1)}, u32[]{:S(2)}, u32[]{:S(2)}) collective-permute-start(bf16[128,1024]{1,0:T(8,128)(2,1)S(1)} %shard_map.49), channel_id=1, source_target_pairs={{0,8},{8,0},{1,9},{9,1},{2,10},{10,2},{3,11},{11,3},{4,12},{12,4},... | collective-permute-start | bytes 786440 | tf_op jit(solution)/shard_map/ppermute | solution.py:411
  60.3 10.6 %copy-start.6 = (bf16[2,512,256]{2,1,0:T(8,128)(2,1)}, bf16[2,512,256]{2,1,0:T(8,128)(2,1)S(1)}, u32[]{:S(2)}) copy-start(bf16[2,512,256]{2,1,0:T(8,128)(2,1)S(1)} %collective-permute-done.9.refs_5_) | copy-start | bytes 1572868
  60.3 20.7 %copy-start.4 = (bf16[2,512,256]{2,1,0:T(8,128)(2,1)}, bf16[2,512,256]{2,1,0:T(8,128)(2,1)S(1)}, u32[]{:S(2)}) copy-start(bf16[2,512,256]{2,1,0:T(8,128)(2,1)S(1)} %collective-permute-done.10.refs_7_) | copy-start | bytes 1572868
  60.3 1.0 copy-start.9
  60.4 1.0 copy-start.10
  61.3 23.5 %all-to-all-start.2 = ((bf16[128,8,128]{2,1,0:T(8,128)(2,1)}), bf16[128,8,128]{2,1,0:T(8,128)(2,1)S(1)}, u32[]{:S(2)}, u32[]{:S(2)}) async-start(bf16[128,8,128]{2,1,0:T(8,128)(2,1)} %bitcast.13.refs_6_), calls=%async_computation.2 | async-start | bytes 524288 | tf_op jit(solution)/shard_map/all_to_all | solution.py:418
  85.7 16.9 %all-to-all-start.3 = ((bf16[16,8,8,128]{3,2,1,0:T(8,128)(2,1)}), bf16[16,8,8,128]{3,2,1,0:T(8,128)(2,1)S(1)}, u32[]{:S(2)}, u32[]{:S(2)}) async-start(bf16[16,8,8,128]{3,2,1,0:T(8,128)(2,1)} %broadcast_in_dim.2.refs_10_), calls=%async_computation.3 | async-start | bytes 524288 | tf_op jit(solution)/shard_map/all_to_all | solution.py:425
  102.6 3.3 %collective-permute-start.13 = (bf16[16,8,8,128]{3,2,1,0:T(8,128)(2,1)S(1)}, bf16[16,8,8,128]{3,2,1,0:T(8,128)(2,1)S(1)}, u32[]{:S(2)}, u32[]{:S(2)}) collective-permute-start(bf16[16,8,8,128]{3,2,1,0:T(8,128)(2,1)S(1)} %all-to-all-done.3.refs_4_), channel_id=1, source_target_pairs={{0,8},{8,0},{1,9},{9,1},{2,10},{10,2},{3,11},{11,3},{4,12},{12,4},... | collective-permute-start | bytes 786440 | tf_op jit(solution)/shard_map/ppermute | solution.py:427

commit v5 on v4

--- a/solution.py
+++ b/solution.py
@@ -194,8 +194,9 @@
                 pltpu.make_async_copy(w_out_any.at[expert], w_out.at[at], sems.at[2 * at + 1]),
             )
         )
-        for copy in copies[at]:
-            copy.start()
+    for which in range(2):
+        for pair in copies:
+            pair[which].start()
     pairs = range(0, count, 2)
     for at in range(count):
         copies[at][0].wait()
@@ -389,7 +390,7 @@
     near = lax.ppermute(mine, "zl", SWAP)
     rows_y = jnp.stack([y, y, y - 1, y - 1, y + 1, y + 1, y + 2, y + 2]) % ny
     rows_l = jnp.stack([zl, 1 - zl] * 4)
-    place = jnp.concatenate([core, rows_y * nl + rows_l]).astype(jnp.int32)
+    place = jnp.concatenate([core, rows_l * ny + rows_y]).astype(jnp.int32)
 
     own, send = dispatch(core, tokens, slot_embed)
     merged = merge(own, lax.ppermute(send, "core", SWAP))
@@ -412,18 +413,21 @@
     got, table_other = lax.optimization_barrier((got, table_other))
 
     cut = (done_own + got.astype(F32)).astype(BF16)
-    cut = cut.reshape(nx * nh, part, ny * nl, -1).transpose(0, 2, 1, 3)
-    cut = cut.reshape((nx * nh * ny * nl, part, -1))
+    cut = cut.reshape(nx * nh, part, ny, nl, -1).transpose(0, 2, 3, 1, 4)
+    cut = cut.reshape((nx * nh * ny, nl, part, -1))
     first, *stats = combine_weights(core, tokens, table_own[:2], table_other[:2], [cut])
-    got = lax.all_to_all(cut, ("x", "zh", "y", "zl"), 0, 0)
+    got = lax.all_to_all(cut, ("x", "zh", "y"), 0, 0)
     got, stats = lax.optimization_barrier((got, stats))
-    got = jnp.sum(got.reshape((nx * nh, ny * nl) + got.shape[1:]).astype(F32), axis=0)
-    spread = jnp.broadcast_to(got.astype(BF16)[None], (nx * nh,) + got.shape)
+    got = jnp.sum(got.reshape((nx * nh, ny) + got.shape[1:]).astype(F32), axis=0)
+    got = got.astype(BF16).transpose(1, 0, 2, 3)
+    spread = jnp.broadcast_to(got[None], (nx * nh,) + got.shape)
+    spread = spread.reshape((nx * nh * nl,) + got.shape[1:])
     second, *scales = combine_weights(
         core, tokens, table_own[2:], table_other[2:], [spread], earlier=stats
     )
-    out_own = lax.all_to_all(spread, ("x", "zh"), 0, 0)
+    out_own = lax.all_to_all(spread, ("x", "zh", "zl"), 0, 0)
     out_own, scales = lax.optimization_barrier((out_own, scales))
+    out_own = out_own.reshape((nx * nh, ny * nl) + out_own.shape[2:])
     out_other = lax.ppermute(out_own, "core", SWAP)
     return output(place, [first, second], scales, out_own, out_other)
 

time: 112 us -> 110 us (0.982)
  waiting for transfers between devices: 24.2 us -> 22.2 us
    all_to_all x2, waiting for transfers between devices: 5.16 us -> 3.1 us  [the longest x1 3.1 us: on_device(): got = lax.all_to_all(cut, ('x', 'zh', 'y'), 0, 0)]
  transfers between devices with their start and end apart: 18 -> 18, of which waited for: 8 -> 7; matrix products, arithmetic and copies ran while one was open for 0% -> 0% of each run, Pallas kernels for 26% -> 26%
where the time goes in v5:
time: 110 us; the launch traced here: 109 us
  starting transfers between devices  45.1 us (41%)
  Pallas kernels  39.5 us (36%)
  waiting for transfers between devices  22.2 us (20%)
  other arithmetic  1.13 us (1%)
    pallas_call x2, Pallas kernels, combine_weights(): call(after(functools.partial(weights_kernel, len(pieces)), 2 + len(earlie...  20.6 us
    all_to_all x1, waiting for transfers between devices, on_device(): got = lax.all_to_all(merged.reshape(nx * nh, part, -1), ('x', 'zh'), 0, 0)  9.95 us
    all_to_all x1, starting transfers between devices, on_device(): got = lax.all_to_all(merged.reshape(nx * nh, part, -1), ('x', 'zh'), 0, 0)  9.01 us
    all_to_all x1, starting transfers between devices, on_device(): got = lax.all_to_all(cut, ('x', 'zh', 'y'), 0, 0)  8.37 us
    all_to_all x1, starting transfers between devices, on_device(): out_own = lax.all_to_all(spread, ('x', 'zh', 'zl'), 0, 0)  6.06 us
    pallas_call x1, Pallas kernels, output(): call(functools.partial(output_kernel, parts, steps), jax.ShapeDtypeStruct...  5.87 us
    pallas_call x2, Pallas kernels, experts(): call(after(functools.partial(expert_kernel, slots.shape[0] // count), 4,...  5.48 us
    pallas_call x1, Pallas kernels, dispatch(): call(functools.partial(dispatch_kernel, parts), micros=6, outs=[kept(shap...  5.48 us
  transfers between devices with their start and end apart: 18, of which 7 were waited for; matrix products, arithmetic and copies ran while one was open for 0% of the time, Pallas kernels for 26%

profile of v5, /device:TPU:1, one launch (start us, length us, event | category | flops | bytes accessed | tf_op | source)
XLA Modules:
  0.0 109.4 jit_solution(4987551127133886336)
XLA Ops:
  0.0 5.5 %shard_map.46 = (f32[128,1152]{1,0:T(8,128)S(1)}, bf16[128,1152]{1,0:T(8,128)(2,1)S(1)}) custom-call(s32[1]{0:T(128)} %bitcast.core.refs_0_, bf16[1920,1024]{1,0:T(8,128)(2,1)} %refs_1_.3, bf16[1024,256]{1,0:T(8,128)(2,1)} %embed_any.1), custom_call_target="tpu_custom_call" | custom-call | bytes 180000 | tf_op jit(solution)/shard_map/pallas_call | solution.py:119
  5.5 3.3 %collective-permute-start.1 = (bf16[128,1152]{1,0:T(8,128)(2,1)S(1)}, bf16[128,1152]{1,0:T(8,128)(2,1)S(1)}, u32[]{:S(2)}, u32[]{:S(2)}) collective-permute-start(bf16[128,1152]{1,0:T(8,128)(2,1)S(1)} %get-tuple-element.30), channel_id=1, source_target_pairs={{0,8},{8,0},{1,9},{9,1},{2,10},{10,2},{3,11},{11,3},{4,12},{12,4},... | collective-permute-start | bytes 884744 | tf_op jit(solution)/shard_map/ppermute | solution.py:396
  8.8 0.1 collective-permute-start
  8.9 1.1 collective-permute-done.1.got
  10.0 1.1 %shard_map.47 = bf16[128,1152]{1,0:T(8,128)(2,1)} custom-call(f32[128,1152]{1,0:T(8,128)S(1)} %get-tuple-element.29.own, bf16[128,1152]{1,0:T(8,128)(2,1)S(1)} %collective-permute-done.1.got), custom_call_target="tpu_custom_call" | custom-call | bytes 30000 | tf_op jit(solution)/shard_map/pallas_call | solution.py:151
  11.1 9.0 %all-to-all-start = ((bf16[16,8,1152]{2,1,0:T(8,128)(2,1)}), bf16[16,8,1152]{2,1,0:T(8,128)(2,1)S(1)}, u32[]{:S(2)}, u32[]{:S(2)}) async-start(bf16[16,8,1152]{2,1,0:T(8,128)(2,1)} %bitcast.9), calls=%async_computation | async-start | bytes 589824 | tf_op jit(solution)/shard_map/all_to_all | solution.py:401
  20.2 0.0 collective-permute-done
  20.2 0.1 pad_maximum_fusion.refs_2_
  20.3 1.4 %collective-permute-start.2 = (bf16[2,512,256]{2,1,0:T(8,128)(2,1)S(1)}, bf16[2,512,256]{2,1,0:T(8,128)(2,1)S(1)}, u32[]{:S(2)}, u32[]{:S(2)}) collective-permute-start(bf16[2,512,256]{2,1,0:T(8,128)(2,1)S(1)} %pad_maximum_fusion.refs_2_), channel_id=1, source_target_pairs={{0,2},{2,4},{4,6},{6,0},{1,3},{3,5},{5,7},{7,1},{8,10},{10,12},{12... | collective-permute-start | bytes 1572872 | tf_op jit(solution)/shard_map/ppermute | solution.py:399
  21.6 1.5 %collective-permute-start.4 = (bf16[2,512,256]{2,1,0:T(8,128)(2,1)S(1)}, bf16[2,512,256]{2,1,0:T(8,128)(2,1)S(1)}, u32[]{:S(2)}, u32[]{:S(2)}) collective-permute-start(bf16[2,512,256]{2,1,0:T(8,128)(2,1)S(1)} %pad_maximum_fusion.refs_2_), channel_id=1, source_target_pairs={{0,6},{2,0},{4,2},{6,4},{1,7},{3,1},{5,3},{7,5},{8,14},{10,8},{12,... | collective-permute-start | bytes 1572872 | tf_op jit(solution)/shard_map/ppermute | solution.py:400
  23.2 9.9 %all-to-all-done.got = bf16[16,8,1152]{2,1,0:T(8,128)(2,1)S(1)} async-done(((bf16[16,8,1152]{2,1,0:T(8,128)(2,1)}), bf16[16,8,1152]{2,1,0:T(8,128)(2,1)S(1)}, u32[]{:S(2)}, u32[]{:S(2)}) %all-to-all-start) | async-done | bytes 294944 | tf_op jit(solution)/shard_map/all_to_all | solution.py:401
  33.1 1.0 shard_map.48
  34.1 3.5 %all-to-all-start.1 = ((bf16[16,8,1024]{2,1,0:T(8,128)(2,1)}), bf16[16,8,1024]{2,1,0:T(8,128)(2,1)S(1)}, u32[]{:S(2)}, u32[]{:S(2)}) async-start(bf16[16,8,1024]{2,1,0:T(8,128)(2,1)} %shard_map.48), calls=%async_computation.1 | async-start | bytes 524288 | tf_op jit(solution)/shard_map/all_to_all | solution.py:404
  37.6 0.0 collective-permute-done.2.refs_3_
  37.7 1.4 %collective-permute-start.3 = (bf16[1,512,256]{2,1,0:T(8,128)(2,1)S(1)}, bf16[1,512,256]{2,1,0:T(8,128)(2,1)S(1)}, u32[]{:S(2)}, u32[]{:S(2)}) collective-permute-start(bf16[1,512,256]{2,1,0:T(8,128)(2,1)S(1)} %slice.8), channel_id=1, source_target_pairs={{0,2},{2,4},{4,6},{6,0},{1,3},{3,5},{5,7},{7,1},{8,10},{10,12},{12... | collective-permute-start | bytes 786440 | tf_op jit(solution)/shard_map/ppermute | solution.py:403
  39.1 0.0 collective-permute-done.4.refs_4_
  39.1 1.5 %collective-permute-start.5 = (bf16[1,512,256]{2,1,0:T(8,128)(2,1)S(1)}, bf16[1,512,256]{2,1,0:T(8,128)(2,1)S(1)}, u32[]{:S(2)}, u32[]{:S(2)}) collective-permute-start(bf16[1,512,256]{2,1,0:T(8,128)(2,1)S(1)} %slice.9), channel_id=1, source_target_pairs={{0,6},{2,0},{4,2},{6,4},{1,7},{3,1},{5,3},{7,5},{8,14},{10,8},{12,... | collective-permute-start | bytes 786440 | tf_op jit(solution)/shard_map/ppermute | solution.py:403
  40.7 2.4 %collective-permute-start.8 = (bf16[2,512,256]{2,1,0:T(8,128)(2,1)S(1)}, bf16[2,512,256]{2,1,0:T(8,128)(2,1)S(1)}, u32[]{:S(2)}, u32[]{:S(2)}) collective-permute-start(bf16[2,512,256]{2,1,0:T(8,128)(2,1)S(1)} %pad_maximum_fusion.refs_2_), channel_id=1, source_target_pairs={{0,8},{8,0},{1,9},{9,1},{2,10},{10,2},{3,11},{11,3},{4,12},{12,4},... | collective-permute-start | bytes 1572872 | tf_op jit(solution)/shard_map/ppermute | solution.py:411
  43.1 1.9 %collective-permute-done.3.refs_5_ = bf16[1,512,256]{2,1,0:T(8,128)(2,1)S(1)} collective-permute-done((bf16[1,512,256]{2,1,0:T(8,128)(2,1)S(1)}, bf16[1,512,256]{2,1,0:T(8,128)(2,1)S(1)}, u32[]{:S(2)}, u32[]{:S(2)}) %collective-permute-start.3) | collective-permute-done | bytes 262176 | tf_op jit(solution)/shard_map/ppermute | solution.py:403
  45.0 0.0 collective-permute-done.5.refs_6_
  45.0 4.5 %all-to-all-done.1 = bf16[16,8,1024]{2,1,0:T(8,128)(2,1)S(1)} async-done(((bf16[16,8,1024]{2,1,0:T(8,128)(2,1)}), bf16[16,8,1024]{2,1,0:T(8,128)(2,1)S(1)}, u32[]{:S(2)}, u32[]{:S(2)}) %all-to-all-start.1) | async-done | bytes 262176 | tf_op jit(solution)/shard_map/all_to_all | solution.py:404
  49.4 2.5 %collective-permute-start.6 = (bf16[128,1024]{1,0:T(8,128)(2,1)S(1)}, bf16[128,1024]{1,0:T(8,128)(2,1)S(1)}, u32[]{:S(2)}, u32[]{:S(2)}) collective-permute-start(bf16[128,1024]{1,0:T(8,128)(2,1)S(1)} %bitcast.21), channel_id=1, source_target_pairs={{0,8},{8,0},{1,9},{9,1},{2,10},{10,2},{3,11},{11,3},{4,12},{12,4},... | collective-permute-start | bytes 786440 | tf_op jit(solution)/shard_map/ppermute | solution.py:406
  52.0 0.1 collective-permute-start.9
  52.1 0.4 collective-permute-start.10
  52.5 0.1 collective-permute-start.11
  52.6 0.6 collective-permute-done.6.refs_1_
  53.1 0.4 collective-permute-start.12
  53.5 2.7 %shard_map.49 = bf16[128,1024]{1,0:T(8,128)(2,1)S(1)} custom-call(s32[1]{0:T(128)S(6)} %sub.12.refs_0_, bf16[128,1024]{1,0:T(8,128)(2,1)S(1)} %collective-permute-done.6.refs_1_, bf16[16,1024,128]{2,1,0:T(8,128)(2,1)} %refs_2_.3, bf16[16,128,1024]{2,1,0:T(8,128)(2,1)} %refs_3_.3), custom_call_target="tpu_custom_call" | custom-call | bytes 90000 | tf_op jit(solution)/shard_map/pallas_call | solution.py:221
  56.3 0.0 collective-permute-done.8.refs_4_
  56.3 0.4 collective-permute-start.7
  56.7 2.7 %shard_map.50 = f32[128,1024]{1,0:T(8,128)S(1)} custom-call(s32[1]{0:T(128)} %bitcast.core.refs_0_, bf16[128,1024]{1,0:T(8,128)(2,1)S(1)} %bitcast.22, bf16[16,1024,128]{2,1,0:T(8,128)(2,1)} %refs_2_.3, bf16[16,128,1024]{2,1,0:T(8,128)(2,1)} %refs_3_.3), custom_call_target="tpu_custom_call" | custom-call | bytes 90000 | tf_op jit(solution)/shard_map/pallas_call | solution.py:221
  59.5 0.0 collective-permute-done.9.refs_5_
  59.5 0.0 collective-permute-done.10.refs_7_
  59.5 0.0 collective-permute-done.12.refs_9_
  59.5 0.0 collective-permute-done.7
  59.6 0.9 add_convert_fusion
  60.5 8.4 %all-to-all-start.2 = ((bf16[64,2,8,128]{3,2,1,0:T(8,128)(2,1)}), bf16[64,2,8,128]{3,2,1,0:T(8,128)(2,1)S(1)}, u32[]{:S(2)}, u32[]{:S(2)}) async-start(bf16[64,2,8,128]{3,2,1,0:T(8,128)(2,1)} %bitcast.13.refs_6_), calls=%async_computation.2 | async-start | bytes 524288 | tf_op jit(solution)/shard_map/all_to_all | solution.py:419
  68.9 10.1 %shard_map.51 = (bf16[1920,1024]{1,0:T(8,128)(2,1)}, f32[1920,128]{1,0:T(8,128)}, f32[1920,128]{1,0:T(8,128)}) custom-call(s32[1]{0:T(128)} %bitcast.core.refs_0_, bf16[1920,1024]{1,0:T(8,128)(2,1)} %refs_1_.3, bf16[2,512,256]{2,1,0:T(8,128)(2,1)} %copy-done.1, bf16[2,512,256]{2,1,0:T(8,128)(2,1)} %copy-done.3, bf16[2,512,256]{2,1,0:T(8,128)(2,1)} %copy-done.5, ...), custom_call_target="tpu_custom_call" | custom-call | bytes 240000 | tf_op jit(solution)/shard_map/pallas_call | solution.py:289
  79.0 3.1 %all-to-all-done.2 = bf16[64,2,8,128]{3,2,1,0:T(8,128)(2,1)S(1)} async-done(((bf16[64,2,8,128]{3,2,1,0:T(8,128)(2,1)}), bf16[64,2,8,128]{3,2,1,0:T(8,128)(2,1)S(1)}, u32[]{:S(2)}, u32[]{:S(2)}) %all-to-all-start.2) | async-done | bytes 262176 | tf_op jit(solution)/shard_map/all_to_all | solution.py:419
  82.1 0.8 broadcast_in_dim.2
  82.9 6.1 %all-to-all-start.3 = ((bf16[32,4,8,128]{3,2,1,0:T(8,128)(2,1)}), bf16[32,4,8,128]{3,2,1,0:T(8,128)(2,1)S(1)}, u32[]{:S(2)}, u32[]{:S(2)}) async-start(bf16[32,4,8,128]{3,2,1,0:T(8,128)(2,1)} %bitcast.18.refs_10_), calls=%async_computation.3 | async-start | bytes 524288 | tf_op jit(solution)/shard_map/all_to_all | solution.py:428
  89.0 0.1 stack.45
  89.0 0.1 stack.50
  89.1 10.6 %shard_map.52 = (bf16[1920,1024]{1,0:T(8,128)(2,1)}, f32[1920,128]{1,0:T(8,128)}, f32[1920,128]{1,0:T(8,128)}) custom-call(s32[1]{0:T(128)} %bitcast.core.refs_0_, bf16[1920,1024]{1,0:T(8,128)(2,1)} %refs_1_.3, f32[1920,128]{1,0:T(8,128)} %get-tuple-element.41.refs_2_, f32[1920,128]{1,0:T(8,128)} %get-tuple-element.42.refs_3_, ...), custom_call_target="tpu_custom_call" | custom-call | bytes 240000 | tf_op jit(solution)/shard_map/pallas_call | solution.py:289
  99.7 2.5 %collective-permute-start.13 = (bf16[16,8,8,128]{3,2,1,0:T(8,128)(2,1)S(1)}, bf16[16,8,8,128]{3,2,1,0:T(8,128)(2,1)S(1)}, u32[]{:S(2)}, u32[]{:S(2)}) collective-permute-start(bf16[16,8,8,128]{3,2,1,0:T(8,128)(2,1)S(1)} %bitcast.23), channel_id=1, source_target_pairs={{0,8},{8,0},{1,9},{9,1},{2,10},{10,2},{3,11},{11,3},{4,12},{12,4},... | collective-permute-start | bytes 786440 | tf_op jit(solution)/shard_map/ppermute | solution.py:431
  102.3 0.1 pad_add_fusion.place
  102.3 1.1 collective-permute-done.13.refs_5_
  103.4 5.9 %shard_map.53 = bf16[1920,128]{1,0:T(8,128)(2,1)} custom-call(s32[9]{0:T(128)S(1)} %pad_add_fusion.place, bf16[1920,1024]{1,0:T(8,128)(2,1)} %get-tuple-element.38.refs_0_, bf16[1920,1024]{1,0:T(8,128)(2,1)} %get-tuple-element.47.refs_1_, f32[1920,128]{1,0:T(8,128)} %get-tuple-element.50.refs_2_, f32[1920,128]{1,0:T(8,128)} %get-tuple-element.51.refs_3_, ...), custom_call_target="tpu_custom_call" | custom-call | bytes 30000 | tf_op jit(solution)/shard_map/pallas_call | solution.py:360
  (31 shorter events, 0.2 us)
Async XLA Ops:
  0.0 8.8 %copy-start = (bf16[1024,256]{1,0:T(8,128)(2,1)S(1)}, bf16[1024,256]{1,0:T(8,128)(2,1)}, u32[]{:S(2)}) copy-start(bf16[1024,256]{1,0:T(8,128)(2,1)} %embed_any.1) | copy-start | bytes 1572868
  5.5 4.5 %collective-permute-start.1 = (bf16[128,1152]{1,0:T(8,128)(2,1)S(1)}, bf16[128,1152]{1,0:T(8,128)(2,1)S(1)}, u32[]{:S(2)}, u32[]{:S(2)}) collective-permute-start(bf16[128,1152]{1,0:T(8,128)(2,1)S(1)} %get-tuple-element.30), channel_id=1, source_target_pairs={{0,8},{8,0},{1,9},{9,1},{2,10},{10,2},{3,11},{11,3},{4,12},{12,4},... | collective-permute-start | bytes 884744 | tf_op jit(solution)/shard_map/ppermute | solution.py:396
  8.8 11.3 %collective-permute-start = (bf16[512,256]{1,0:T(8,128)(2,1)S(1)}, bf16[512,256]{1,0:T(8,128)(2,1)S(1)}, u32[]{:S(2)}, u32[]{:S(2)}) collective-permute-start(bf16[512,256]{1,0:T(8,128)(2,1)S(1)} %constant_dynamic-slice_fusion), channel_id=1, source_target_pairs={{0,1},{1,0},{2,3},{3,2},{4,5},{5,4},{6,7},{7,6},{8,9},{9,8},{10,11... | collective-permute-start | bytes 786440 | tf_op jit(solution)/shard_map/ppermute | solution.py:390
  11.1 22.0 %all-to-all-start = ((bf16[16,8,1152]{2,1,0:T(8,128)(2,1)}), bf16[16,8,1152]{2,1,0:T(8,128)(2,1)S(1)}, u32[]{:S(2)}, u32[]{:S(2)}) async-start(bf16[16,8,1152]{2,1,0:T(8,128)(2,1)} %bitcast.9), calls=%async_computation | async-start | bytes 589824 | tf_op jit(solution)/shard_map/all_to_all | solution.py:401
  20.3 36.0 %copy-start.1 = (bf16[2,512,256]{2,1,0:T(8,128)(2,1)}, bf16[2,512,256]{2,1,0:T(8,128)(2,1)S(1)}, u32[]{:S(2)}) copy-start(bf16[2,512,256]{2,1,0:T(8,128)(2,1)S(1)} %pad_maximum_fusion.refs_2_) | copy-start | bytes 1572868
  20.3 17.4 %collective-permute-start.2 = (bf16[2,512,256]{2,1,0:T(8,128)(2,1)S(1)}, bf16[2,512,256]{2,1,0:T(8,128)(2,1)S(1)}, u32[]{:S(2)}, u32[]{:S(2)}) collective-permute-start(bf16[2,512,256]{2,1,0:T(8,128)(2,1)S(1)} %pad_maximum_fusion.refs_2_), channel_id=1, source_target_pairs={{0,2},{2,4},{4,6},{6,0},{1,3},{3,5},{5,7},{7,1},{8,10},{10,12},{12... | collective-permute-start | bytes 1572872 | tf_op jit(solution)/shard_map/ppermute | solution.py:399
  21.6 17.4 %collective-permute-start.4 = (bf16[2,512,256]{2,1,0:T(8,128)(2,1)S(1)}, bf16[2,512,256]{2,1,0:T(8,128)(2,1)S(1)}, u32[]{:S(2)}, u32[]{:S(2)}) collective-permute-start(bf16[2,512,256]{2,1,0:T(8,128)(2,1)S(1)} %pad_maximum_fusion.refs_2_), channel_id=1, source_target_pairs={{0,6},{2,0},{4,2},{6,4},{1,7},{3,1},{5,3},{7,5},{8,14},{10,8},{12,... | collective-permute-start | bytes 1572872 | tf_op jit(solution)/shard_map/ppermute | solution.py:400
  34.1 15.3 %all-to-all-start.1 = ((bf16[16,8,1024]{2,1,0:T(8,128)(2,1)}), bf16[16,8,1024]{2,1,0:T(8,128)(2,1)S(1)}, u32[]{:S(2)}, u32[]{:S(2)}) async-start(bf16[16,8,1024]{2,1,0:T(8,128)(2,1)} %shard_map.48), calls=%async_computation.1 | async-start | bytes 524288 | tf_op jit(solution)/shard_map/all_to_all | solution.py:404
  37.7 18.6 %copy-start.3 = (bf16[2,512,256]{2,1,0:T(8,128)(2,1)}, bf16[2,512,256]{2,1,0:T(8,128)(2,1)S(1)}, u32[]{:S(2)}) copy-start(bf16[2,512,256]{2,1,0:T(8,128)(2,1)S(1)} %collective-permute-done.2.refs_3_) | copy-start | bytes 1572868
  37.7 7.3 %collective-permute-start.3 = (bf16[1,512,256]{2,1,0:T(8,128)(2,1)S(1)}, bf16[1,512,256]{2,1,0:T(8,128)(2,1)S(1)}, u32[]{:S(2)}, u32[]{:S(2)}) collective-permute-start(bf16[1,512,256]{2,1,0:T(8,128)(2,1)S(1)} %slice.8), channel_id=1, source_target_pairs={{0,2},{2,4},{4,6},{6,0},{1,3},{3,5},{5,7},{7,1},{8,10},{10,12},{12... | collective-permute-start | bytes 786440 | tf_op jit(solution)/shard_map/ppermute | solution.py:403
  39.1 17.2 %copy-start.2 = (bf16[2,512,256]{2,1,0:T(8,128)(2,1)}, bf16[2,512,256]{2,1,0:T(8,128)(2,1)S(1)}, u32[]{:S(2)}) copy-start(bf16[2,512,256]{2,1,0:T(8,128)(2,1)S(1)} %collective-permute-done.4.refs_4_) | copy-start | bytes 1572868
  39.1 5.9 %collective-permute-start.5 = (bf16[1,512,256]{2,1,0:T(8,128)(2,1)S(1)}, bf16[1,512,256]{2,1,0:T(8,128)(2,1)S(1)}, u32[]{:S(2)}, u32[]{:S(2)}) collective-permute-start(bf16[1,512,256]{2,1,0:T(8,128)(2,1)S(1)} %slice.9), channel_id=1, source_target_pairs={{0,6},{2,0},{4,2},{6,4},{1,7},{3,1},{5,3},{7,5},{8,14},{10,8},{12,... | collective-permute-start | bytes 786440 | tf_op jit(solution)/shard_map/ppermute | solution.py:403
  40.7 15.6 %collective-permute-start.8 = (bf16[2,512,256]{2,1,0:T(8,128)(2,1)S(1)}, bf16[2,512,256]{2,1,0:T(8,128)(2,1)S(1)}, u32[]{:S(2)}, u32[]{:S(2)}) collective-permute-start(bf16[2,512,256]{2,1,0:T(8,128)(2,1)S(1)} %pad_maximum_fusion.refs_2_), channel_id=1, source_target_pairs={{0,8},{8,0},{1,9},{9,1},{2,10},{10,2},{3,11},{11,3},{4,12},{12,4},... | collective-permute-start | bytes 1572872 | tf_op jit(solution)/shard_map/ppermute | solution.py:411
  45.0 7.0 %copy-start.7 = (bf16[1,512,256]{2,1,0:T(8,128)(2,1)}, bf16[1,512,256]{2,1,0:T(8,128)(2,1)S(1)}, u32[]{:S(2)}) copy-start(bf16[1,512,256]{2,1,0:T(8,128)(2,1)S(1)} %collective-permute-done.3.refs_5_) | copy-start | bytes 786436
  45.0 7.0 %copy-start.8 = (bf16[1,512,256]{2,1,0:T(8,128)(2,1)}, bf16[1,512,256]{2,1,0:T(8,128)(2,1)S(1)}, u32[]{:S(2)}) copy-start(bf16[1,512,256]{2,1,0:T(8,128)(2,1)S(1)} %collective-permute-done.5.refs_6_) | copy-start | bytes 786436
  49.4 3.7 %collective-permute-start.6 = (bf16[128,1024]{1,0:T(8,128)(2,1)S(1)}, bf16[128,1024]{1,0:T(8,128)(2,1)S(1)}, u32[]{:S(2)}, u32[]{:S(2)}) collective-permute-start(bf16[128,1024]{1,0:T(8,128)(2,1)S(1)} %bitcast.21), channel_id=1, source_target_pairs={{0,8},{8,0},{1,9},{9,1},{2,10},{10,2},{3,11},{11,3},{4,12},{12,4},... | collective-permute-start | bytes 786440 | tf_op jit(solution)/shard_map/ppermute | solution.py:406
  52.0 7.5 %collective-permute-start.9 = (bf16[2,512,256]{2,1,0:T(8,128)(2,1)S(1)}, bf16[2,512,256]{2,1,0:T(8,128)(2,1)S(1)}, u32[]{:S(2)}, u32[]{:S(2)}) collective-permute-start(bf16[2,512,256]{2,1,0:T(8,128)(2,1)S(1)} %collective-permute-done.2.refs_3_), channel_id=1, source_target_pairs={{0,8},{8,0},{1,9},{9,1},{2,10},{10,2},{3,11},{11,3},{4,12},{12,4},... | collective-permute-start | bytes 1572872 | tf_op jit(solution)/shard_map/ppermute | solution.py:411
  52.1 7.4 %collective-permute-start.10 = (bf16[2,512,256]{2,1,0:T(8,128)(2,1)S(1)}, bf16[2,512,256]{2,1,0:T(8,128)(2,1)S(1)}, u32[]{:S(2)}, u32[]{:S(2)}) collective-permute-start(bf16[2,512,256]{2,1,0:T(8,128)(2,1)S(1)} %collective-permute-done.4.refs_4_), channel_id=1, source_target_pairs={{0,8},{8,0},{1,9},{9,1},{2,10},{10,2},{3,11},{11,3},{4,12},{12,4},... | collective-permute-start | bytes 1572872 | tf_op jit(solution)/shard_map/ppermute | solution.py:411
  52.5 7.0 %collective-permute-start.11 = (bf16[1,512,256]{2,1,0:T(8,128)(2,1)}, bf16[1,512,256]{2,1,0:T(8,128)(2,1)S(1)}, u32[]{:S(2)}, u32[]{:S(2)}) collective-permute-start(bf16[1,512,256]{2,1,0:T(8,128)(2,1)} %copy-done.7), channel_id=1, source_target_pairs={{0,8},{8,0},{1,9},{9,1},{2,10},{10,2},{3,11},{11,3},{4,12},{12,4},... | collective-permute-start | bytes 786440 | tf_op jit(solution)/shard_map/ppermute | solution.py:411
  53.1 6.4 %collective-permute-start.12 = (bf16[1,512,256]{2,1,0:T(8,128)(2,1)}, bf16[1,512,256]{2,1,0:T(8,128)(2,1)S(1)}, u32[]{:S(2)}, u32[]{:S(2)}) collective-permute-start(bf16[1,512,256]{2,1,0:T(8,128)(2,1)} %copy-done.8), channel_id=1, source_target_pairs={{0,8},{8,0},{1,9},{9,1},{2,10},{10,2},{3,11},{11,3},{4,12},{12,4},... | collective-permute-start | bytes 786440 | tf_op jit(solution)/shard_map/ppermute | solution.py:411
  56.3 3.2 %copy-start.5 = (bf16[2,512,256]{2,1,0:T(8,128)(2,1)}, bf16[2,512,256]{2,1,0:T(8,128)(2,1)S(1)}, u32[]{:S(2)}) copy-start(bf16[2,512,256]{2,1,0:T(8,128)(2,1)S(1)} %collective-permute-done.8.refs_4_) | copy-start | bytes 1572868
  56.3 3.2 %collective-permute-start.7 = (bf16[128,1024]{1,0:T(8,128)(2,1)S(1)}, bf16[128,1024]{1,0:T(8,128)(2,1)S(1)}, u32[]{:S(2)}, u32[]{:S(2)}) collective-permute-start(bf16[128,1024]{1,0:T(8,128)(2,1)S(1)} %shard_map.49), channel_id=1, source_target_pairs={{0,8},{8,0},{1,9},{9,1},{2,10},{10,2},{3,11},{11,3},{4,12},{12,4},... | collective-permute-start | bytes 786440 | tf_op jit(solution)/shard_map/ppermute | solution.py:412
  59.5 9.4 %copy-start.6 = (bf16[2,512,256]{2,1,0:T(8,128)(2,1)}, bf16[2,512,256]{2,1,0:T(8,128)(2,1)S(1)}, u32[]{:S(2)}) copy-start(bf16[2,512,256]{2,1,0:T(8,128)(2,1)S(1)} %collective-permute-done.9.refs_5_) | copy-start | bytes 1572868
  59.5 19.5 %copy-start.4 = (bf16[2,512,256]{2,1,0:T(8,128)(2,1)}, bf16[2,512,256]{2,1,0:T(8,128)(2,1)S(1)}, u32[]{:S(2)}) copy-start(bf16[2,512,256]{2,1,0:T(8,128)(2,1)S(1)} %collective-permute-done.10.refs_7_) | copy-start | bytes 1572868
  59.5 1.0 copy-start.9
  59.5 1.0 copy-start.10
  60.5 21.6 %all-to-all-start.2 = ((bf16[64,2,8,128]{3,2,1,0:T(8,128)(2,1)}), bf16[64,2,8,128]{3,2,1,0:T(8,128)(2,1)S(1)}, u32[]{:S(2)}, u32[]{:S(2)}) async-start(bf16[64,2,8,128]{3,2,1,0:T(8,128)(2,1)} %bitcast.13.refs_6_), calls=%async_computation.2 | async-start | bytes 524288 | tf_op jit(solution)/shard_map/all_to_all | solution.py:419
  82.9 16.8 %all-to-all-start.3 = ((bf16[32,4,8,128]{3,2,1,0:T(8,128)(2,1)}), bf16[32,4,8,128]{3,2,1,0:T(8,128)(2,1)S(1)}, u32[]{:S(2)}, u32[]{:S(2)}) async-start(bf16[32,4,8,128]{3,2,1,0:T(8,128)(2,1)} %bitcast.18.refs_10_), calls=%async_computation.3 | async-start | bytes 524288 | tf_op jit(solution)/shard_map/all_to_all | solution.py:428
  99.7 3.7 %collective-permute-start.13 = (bf16[16,8,8,128]{3,2,1,0:T(8,128)(2,1)S(1)}, bf16[16,8,8,128]{3,2,1,0:T(8,128)(2,1)S(1)}, u32[]{:S(2)}, u32[]{:S(2)}) collective-permute-start(bf16[16,8,8,128]{3,2,1,0:T(8,128)(2,1)S(1)} %bitcast.23), channel_id=1, source_target_pairs={{0,8},{8,0},{1,9},{9,1},{2,10},{10,2},{3,11},{11,3},{4,12},{12,4},... | collective-permute-start | bytes 786440 | tf_op jit(solution)/shard_map/ppermute | solution.py:431

commit v6 on v5

--- a/solution.py
+++ b/solution.py
@@ -235,9 +235,9 @@
 
 
 def weights_kernel(pieces, core, tok, *refs):
-    earlier = refs[: len(refs) - pieces - 6]
+    earlier = refs[:2] if len(refs) == pieces + 7 else ()
     refs = refs[len(earlier) :]
-    weights, one, two, logits, table, sems = refs[pieces:]
+    weights, stats, (logits, table, sems) = refs[pieces], refs[pieces + 1 : -3], refs[-3:]
     blocks, width, wide = table.shape
     half = width // 2
 
@@ -274,9 +274,10 @@
         top = jnp.maximum(earlier[0][...], peak)
         before, now = jnp.exp(earlier[0][...] - top), jnp.exp(peak - top)
         total = earlier[1][...] * before + total * now
-        one[...], two[...] = before / total, now / total
+        lane = lax.broadcasted_iota(jnp.int32, peak.shape, 1)
+        stats[0][...] = jnp.where(lane < 64, before, now) / total
     else:
-        one[...], two[...] = peak, total
+        stats[0][...], stats[1][...] = peak, total
 
 
 def combine_weights(core, tokens, own, other, wait_for, earlier=(), steps=3):
@@ -292,7 +293,8 @@
             2 + len(earlier) + len(pieces),
             len(wait_for),
         ),
-        [pltpu.HBM((count, blocks * wide), BF16)] + [pltpu.HBM((count, 128), F32)] * 2,
+        [pltpu.HBM((count, blocks * wide), BF16)]
+        + [pltpu.HBM((count, 128), F32)] * (1 if earlier else 2),
         micros=2 * blocks,
         limit=40 << 20,
         grid_spec=pltpu.PrefetchScalarGridSpec(
@@ -302,11 +304,8 @@
             + [stats] * len(earlier)
             + [pl.BlockSpec(memory_space=pltpu.HBM)] * len(pieces)
             + anywhere(len(wait_for)),
-            out_specs=[
-                pl.BlockSpec((rows, blocks * wide), lambda i, core: (i, 0)),
-                stats,
-                stats,
-            ],
+            out_specs=[pl.BlockSpec((rows, blocks * wide), lambda i, core: (i, 0))]
+            + [stats] * (1 if earlier else 2),
             scratch_shapes=[
                 pltpu.VMEM((rows, blocks * wide), F32),
                 pltpu.VMEM((blocks, width, wide), BF16),
@@ -317,10 +316,10 @@
 
 
 def output_kernel(parts, steps, place, *refs):
-    sources = refs[: 2 * parts]
-    own, other, out = refs[2 * parts : 2 * parts + 3]
-    landed, (table, sems) = refs[2 * parts + 3 : -2], refs[-2:]
-    weights, scales = landed[:parts], landed[parts:]
+    sources = refs[: parts + 1]
+    own, other, out = refs[parts + 1 : parts + 4]
+    landed, (table, sems) = refs[parts + 4 : -2], refs[-2:]
+    weights, scale = landed[:parts], landed[parts]
     half = own.shape[0] * own.shape[2]
     groups = own.shape[1]
     count = out.shape[0] // steps
@@ -340,14 +339,14 @@
             table[pl.ds(here, half), :] = block.astype(BF16)
     for step in range(steps):
         rows = pl.ds(step * count, count)
-        for copy in copies[step * 2 * parts : (step + 1) * 2 * parts]:
+        for copy in copies[step * (parts + 1) : (step + 1) * (parts + 1)]:
             copy.wait()
         mixed = jnp.zeros((count, out.shape[1]), F32)
         start = 0
-        for part, scale in zip(weights, scales, strict=True):
+        for at, part in enumerate(weights):
             slots = table[start : start + part.shape[1], :]
             product = jnp.dot(part[rows, :], slots, preferred_element_type=F32)
-            mixed += product * scale[rows, :]
+            mixed += product * scale[rows, 64 * at : 64 * at + 1]
             start += part.shape[1]
         out[rows, :] = mixed.astype(BF16)
 
@@ -362,13 +361,13 @@
         jax.ShapeDtypeStruct((count, wide), BF16),
         limit=24 << 20,
         in_specs=[pl.BlockSpec(memory_space=pltpu.SMEM)]
-        + [pl.BlockSpec(memory_space=pltpu.HBM)] * (2 * parts)
+        + [pl.BlockSpec(memory_space=pltpu.HBM)] * (parts + 1)
         + [whole(), whole()],
         out_specs=whole(),
         scratch_shapes=[pltpu.VMEM(part.shape, part.dtype) for part in weights + scales]
         + [
             pltpu.VMEM((slots, wide), BF16),
-            pltpu.SemaphoreType.DMA((steps * 2 * parts,)),
+            pltpu.SemaphoreType.DMA((steps * (parts + 1),)),
         ],
     )(place, *map(far_memory, weights + scales), own, other)
 

time: 110 us -> 110 us (level)
  no operation moved by 1% of the time
where the time goes in v6:
time: 110 us; the launch traced here: 109 us
  starting transfers between devices  45.2 us (41%)
  Pallas kernels  39.3 us (36%)
  waiting for transfers between devices  22.2 us (20%)
  other arithmetic  1.15 us (1%)
    pallas_call x2, Pallas kernels, combine_weights(): call(after(functools.partial(weights_kernel, len(pieces)), 2 + len(earlie...  20.5 us
    all_to_all x1, waiting for transfers between devices, on_device(): got = lax.all_to_all(merged.reshape(nx * nh, part, -1), ('x', 'zh'), 0, 0)  9.95 us
    all_to_all x1, starting transfers between devices, on_device(): got = lax.all_to_all(merged.reshape(nx * nh, part, -1), ('x', 'zh'), 0, 0)  9.01 us
    all_to_all x1, starting transfers between devices, on_device(): got = lax.all_to_all(cut, ('x', 'zh', 'y'), 0, 0)  8.39 us
    all_to_all x1, starting transfers between devices, on_device(): out_own = lax.all_to_all(spread, ('x', 'zh', 'zl'), 0, 0)  6.05 us
    pallas_call x1, Pallas kernels, output(): call(functools.partial(output_kernel, parts, steps), jax.ShapeDtypeStruct...  5.74 us
    pallas_call x2, Pallas kernels, experts(): call(after(functools.partial(expert_kernel, slots.shape[0] // count), 4,...  5.48 us
    pallas_call x1, Pallas kernels, dispatch(): call(functools.partial(dispatch_kernel, parts), micros=6, outs=[kept(shap...  5.48 us
  transfers between devices with their start and end apart: 18, of which 7 were waited for; matrix products, arithmetic and copies ran while one was open for 0% of the time, Pallas kernels for 26%

profile of v6, /device:TPU:1, one launch (start us, length us, event | category | flops | bytes accessed | tf_op | source)
XLA Modules:
  0.0 109.4 jit_solution(17511568240142745769)
XLA Ops:
  0.0 5.5 %shard_map.46 = (f32[128,1152]{1,0:T(8,128)S(1)}, bf16[128,1152]{1,0:T(8,128)(2,1)S(1)}) custom-call(s32[1]{0:T(128)} %bitcast.core.refs_0_, bf16[1920,1024]{1,0:T(8,128)(2,1)} %refs_1_.3, bf16[1024,256]{1,0:T(8,128)(2,1)} %embed_any.1), custom_call_target="tpu_custom_call" | custom-call | bytes 180000 | tf_op jit(solution)/shard_map/pallas_call | solution.py:119
  5.5 3.3 %collective-permute-start.1 = (bf16[128,1152]{1,0:T(8,128)(2,1)S(1)}, bf16[128,1152]{1,0:T(8,128)(2,1)S(1)}, u32[]{:S(2)}, u32[]{:S(2)}) collective-permute-start(bf16[128,1152]{1,0:T(8,128)(2,1)S(1)} %get-tuple-element.28), channel_id=1, source_target_pairs={{0,8},{8,0},{1,9},{9,1},{2,10},{10,2},{3,11},{11,3},{4,12},{12,4},... | collective-permute-start | bytes 884744 | tf_op jit(solution)/shard_map/ppermute | solution.py:395
  8.8 0.1 collective-permute-start
  8.9 1.1 collective-permute-done.1.got
  10.0 1.1 %shard_map.47 = bf16[128,1152]{1,0:T(8,128)(2,1)} custom-call(f32[128,1152]{1,0:T(8,128)S(1)} %get-tuple-element.27.own, bf16[128,1152]{1,0:T(8,128)(2,1)S(1)} %collective-permute-done.1.got), custom_call_target="tpu_custom_call" | custom-call | bytes 30000 | tf_op jit(solution)/shard_map/pallas_call | solution.py:151
  11.1 9.0 %all-to-all-start = ((bf16[16,8,1152]{2,1,0:T(8,128)(2,1)}), bf16[16,8,1152]{2,1,0:T(8,128)(2,1)S(1)}, u32[]{:S(2)}, u32[]{:S(2)}) async-start(bf16[16,8,1152]{2,1,0:T(8,128)(2,1)} %bitcast.9), calls=%async_computation | async-start | bytes 589824 | tf_op jit(solution)/shard_map/all_to_all | solution.py:400
  20.2 0.0 collective-permute-done
  20.2 0.1 pad_maximum_fusion.refs_2_
  20.3 1.4 %collective-permute-start.2 = (bf16[2,512,256]{2,1,0:T(8,128)(2,1)S(1)}, bf16[2,512,256]{2,1,0:T(8,128)(2,1)S(1)}, u32[]{:S(2)}, u32[]{:S(2)}) collective-permute-start(bf16[2,512,256]{2,1,0:T(8,128)(2,1)S(1)} %pad_maximum_fusion.refs_2_), channel_id=1, source_target_pairs={{0,2},{2,4},{4,6},{6,0},{1,3},{3,5},{5,7},{7,1},{8,10},{10,12},{12... | collective-permute-start | bytes 1572872 | tf_op jit(solution)/shard_map/ppermute | solution.py:398
  21.6 1.5 %collective-permute-start.4 = (bf16[2,512,256]{2,1,0:T(8,128)(2,1)S(1)}, bf16[2,512,256]{2,1,0:T(8,128)(2,1)S(1)}, u32[]{:S(2)}, u32[]{:S(2)}) collective-permute-start(bf16[2,512,256]{2,1,0:T(8,128)(2,1)S(1)} %pad_maximum_fusion.refs_2_), channel_id=1, source_target_pairs={{0,6},{2,0},{4,2},{6,4},{1,7},{3,1},{5,3},{7,5},{8,14},{10,8},{12,... | collective-permute-start | bytes 1572872 | tf_op jit(solution)/shard_map/ppermute | solution.py:399
  23.2 9.9 %all-to-all-done.got = bf16[16,8,1152]{2,1,0:T(8,128)(2,1)S(1)} async-done(((bf16[16,8,1152]{2,1,0:T(8,128)(2,1)}), bf16[16,8,1152]{2,1,0:T(8,128)(2,1)S(1)}, u32[]{:S(2)}, u32[]{:S(2)}) %all-to-all-start) | async-done | bytes 294944 | tf_op jit(solution)/shard_map/all_to_all | solution.py:400
  33.1 1.0 shard_map.48
  34.1 3.5 %all-to-all-start.1 = ((bf16[16,8,1024]{2,1,0:T(8,128)(2,1)}), bf16[16,8,1024]{2,1,0:T(8,128)(2,1)S(1)}, u32[]{:S(2)}, u32[]{:S(2)}) async-start(bf16[16,8,1024]{2,1,0:T(8,128)(2,1)} %shard_map.48), calls=%async_computation.1 | async-start | bytes 524288 | tf_op jit(solution)/shard_map/all_to_all | solution.py:403
  37.6 0.0 collective-permute-done.2.refs_3_
  37.7 1.4 %collective-permute-start.3 = (bf16[1,512,256]{2,1,0:T(8,128)(2,1)S(1)}, bf16[1,512,256]{2,1,0:T(8,128)(2,1)S(1)}, u32[]{:S(2)}, u32[]{:S(2)}) collective-permute-start(bf16[1,512,256]{2,1,0:T(8,128)(2,1)S(1)} %slice.8), channel_id=1, source_target_pairs={{0,2},{2,4},{4,6},{6,0},{1,3},{3,5},{5,7},{7,1},{8,10},{10,12},{12... | collective-permute-start | bytes 786440 | tf_op jit(solution)/shard_map/ppermute | solution.py:402
  39.1 0.0 collective-permute-done.4.refs_4_
  39.1 1.5 %collective-permute-start.5 = (bf16[1,512,256]{2,1,0:T(8,128)(2,1)S(1)}, bf16[1,512,256]{2,1,0:T(8,128)(2,1)S(1)}, u32[]{:S(2)}, u32[]{:S(2)}) collective-permute-start(bf16[1,512,256]{2,1,0:T(8,128)(2,1)S(1)} %slice.9), channel_id=1, source_target_pairs={{0,6},{2,0},{4,2},{6,4},{1,7},{3,1},{5,3},{7,5},{8,14},{10,8},{12,... | collective-permute-start | bytes 786440 | tf_op jit(solution)/shard_map/ppermute | solution.py:402
  40.7 2.4 %collective-permute-start.8 = (bf16[2,512,256]{2,1,0:T(8,128)(2,1)S(1)}, bf16[2,512,256]{2,1,0:T(8,128)(2,1)S(1)}, u32[]{:S(2)}, u32[]{:S(2)}) collective-permute-start(bf16[2,512,256]{2,1,0:T(8,128)(2,1)S(1)} %pad_maximum_fusion.refs_2_), channel_id=1, source_target_pairs={{0,8},{8,0},{1,9},{9,1},{2,10},{10,2},{3,11},{11,3},{4,12},{12,4},... | collective-permute-start | bytes 1572872 | tf_op jit(solution)/shard_map/ppermute | solution.py:410
  43.1 1.9 %collective-permute-done.3.refs_5_ = bf16[1,512,256]{2,1,0:T(8,128)(2,1)S(1)} collective-permute-done((bf16[1,512,256]{2,1,0:T(8,128)(2,1)S(1)}, bf16[1,512,256]{2,1,0:T(8,128)(2,1)S(1)}, u32[]{:S(2)}, u32[]{:S(2)}) %collective-permute-start.3) | collective-permute-done | bytes 262176 | tf_op jit(solution)/shard_map/ppermute | solution.py:402
  45.0 0.0 collective-permute-done.5.refs_6_
  45.0 4.5 %all-to-all-done.1 = bf16[16,8,1024]{2,1,0:T(8,128)(2,1)S(1)} async-done(((bf16[16,8,1024]{2,1,0:T(8,128)(2,1)}), bf16[16,8,1024]{2,1,0:T(8,128)(2,1)S(1)}, u32[]{:S(2)}, u32[]{:S(2)}) %all-to-all-start.1) | async-done | bytes 262176 | tf_op jit(solution)/shard_map/all_to_all | solution.py:403
  49.4 2.5 %collective-permute-start.6 = (bf16[128,1024]{1,0:T(8,128)(2,1)S(1)}, bf16[128,1024]{1,0:T(8,128)(2,1)S(1)}, u32[]{:S(2)}, u32[]{:S(2)}) collective-permute-start(bf16[128,1024]{1,0:T(8,128)(2,1)S(1)} %bitcast.21), channel_id=1, source_target_pairs={{0,8},{8,0},{1,9},{9,1},{2,10},{10,2},{3,11},{11,3},{4,12},{12,4},... | collective-permute-start | bytes 786440 | tf_op jit(solution)/shard_map/ppermute | solution.py:405
  52.0 0.1 collective-permute-start.9
  52.1 0.4 collective-permute-start.10
  52.5 0.1 collective-permute-start.11
  52.6 0.6 collective-permute-done.6.refs_1_
  53.1 0.4 collective-permute-start.12
  53.5 2.7 %shard_map.49 = bf16[128,1024]{1,0:T(8,128)(2,1)S(1)} custom-call(s32[1]{0:T(128)S(6)} %sub.12.refs_0_, bf16[128,1024]{1,0:T(8,128)(2,1)S(1)} %collective-permute-done.6.refs_1_, bf16[16,1024,128]{2,1,0:T(8,128)(2,1)} %refs_2_.3, bf16[16,128,1024]{2,1,0:T(8,128)(2,1)} %refs_3_.3), custom_call_target="tpu_custom_call" | custom-call | bytes 90000 | tf_op jit(solution)/shard_map/pallas_call | solution.py:221
  56.3 0.0 collective-permute-done.8.refs_4_
  56.3 0.4 collective-permute-start.7
  56.7 2.7 %shard_map.50 = f32[128,1024]{1,0:T(8,128)S(1)} custom-call(s32[1]{0:T(128)} %bitcast.core.refs_0_, bf16[128,1024]{1,0:T(8,128)(2,1)S(1)} %bitcast.22, bf16[16,1024,128]{2,1,0:T(8,128)(2,1)} %refs_2_.3, bf16[16,128,1024]{2,1,0:T(8,128)(2,1)} %refs_3_.3), custom_call_target="tpu_custom_call" | custom-call | bytes 90000 | tf_op jit(solution)/shard_map/pallas_call | solution.py:221
  59.5 0.0 collective-permute-done.9.refs_5_
  59.5 0.0 collective-permute-done.10.refs_7_
  59.5 0.0 collective-permute-done.7
  59.6 1.0 add_convert_fusion
  60.5 8.4 %all-to-all-start.2 = ((bf16[64,2,8,128]{3,2,1,0:T(8,128)(2,1)}), bf16[64,2,8,128]{3,2,1,0:T(8,128)(2,1)S(1)}, u32[]{:S(2)}, u32[]{:S(2)}) async-start(bf16[64,2,8,128]{3,2,1,0:T(8,128)(2,1)} %bitcast.13.refs_6_), calls=%async_computation.2 | async-start | bytes 524288 | tf_op jit(solution)/shard_map/all_to_all | solution.py:418
  68.9 10.1 %shard_map.51 = (bf16[1920,1024]{1,0:T(8,128)(2,1)}, f32[1920,128]{1,0:T(8,128)}, f32[1920,128]{1,0:T(8,128)}) custom-call(s32[1]{0:T(128)} %bitcast.core.refs_0_, bf16[1920,1024]{1,0:T(8,128)(2,1)} %refs_1_.3, bf16[2,512,256]{2,1,0:T(8,128)(2,1)} %copy-done.1, bf16[2,512,256]{2,1,0:T(8,128)(2,1)} %copy-done.3, bf16[2,512,256]{2,1,0:T(8,128)(2,1)} %copy-done.5, ...), custom_call_target="tpu_custom_call" | custom-call | bytes 240000 | tf_op jit(solution)/shard_map/pallas_call | solution.py:290
  79.0 3.1 %all-to-all-done.2 = bf16[64,2,8,128]{3,2,1,0:T(8,128)(2,1)S(1)} async-done(((bf16[64,2,8,128]{3,2,1,0:T(8,128)(2,1)}), bf16[64,2,8,128]{3,2,1,0:T(8,128)(2,1)S(1)}, u32[]{:S(2)}, u32[]{:S(2)}) %all-to-all-start.2) | async-done | bytes 262176 | tf_op jit(solution)/shard_map/all_to_all | solution.py:418
  82.2 0.8 broadcast_in_dim.2
  82.9 6.1 %all-to-all-start.3 = ((bf16[32,4,8,128]{3,2,1,0:T(8,128)(2,1)}), bf16[32,4,8,128]{3,2,1,0:T(8,128)(2,1)S(1)}, u32[]{:S(2)}, u32[]{:S(2)}) async-start(bf16[32,4,8,128]{3,2,1,0:T(8,128)(2,1)} %bitcast.18.refs_10_), calls=%async_computation.3 | async-start | bytes 524288 | tf_op jit(solution)/shard_map/all_to_all | solution.py:427
  89.0 0.1 stack.45
  89.1 0.1 stack.50
  89.2 10.4 %shard_map.52 = (bf16[1920,1024]{1,0:T(8,128)(2,1)}, f32[1920,128]{1,0:T(8,128)}) custom-call(s32[1]{0:T(128)} %bitcast.core.refs_0_, bf16[1920,1024]{1,0:T(8,128)(2,1)} %refs_1_.3, f32[1920,128]{1,0:T(8,128)} %get-tuple-element.39.refs_2_, f32[1920,128]{1,0:T(8,128)} %get-tuple-element.40.refs_3_, bf16[2,512,256]{2,1,0:T(8,128)(2,1)} %copy-done.2, ...), custom_call_target="tpu_custom_call" | custom-call | bytes 240000 | tf_op jit(solution)/shard_map/pallas_call | solution.py:290
  99.6 0.0 all-to-all-done.3
  99.6 2.7 %collective-permute-start.13 = (bf16[16,8,8,128]{3,2,1,0:T(8,128)(2,1)S(1)}, bf16[16,8,8,128]{3,2,1,0:T(8,128)(2,1)S(1)}, u32[]{:S(2)}, u32[]{:S(2)}) collective-permute-start(bf16[16,8,8,128]{3,2,1,0:T(8,128)(2,1)S(1)} %bitcast.23), channel_id=1, source_target_pairs={{0,8},{8,0},{1,9},{9,1},{2,10},{10,2},{3,11},{11,3},{4,12},{12,4},... | collective-permute-start | bytes 786440 | tf_op jit(solution)/shard_map/ppermute | solution.py:430
  102.3 0.1 pad_add_fusion.place
  102.4 1.1 collective-permute-done.13.refs_4_
  103.5 5.7 %shard_map.53 = bf16[1920,128]{1,0:T(8,128)(2,1)} custom-call(s32[9]{0:T(128)S(1)} %pad_add_fusion.place, bf16[1920,1024]{1,0:T(8,128)(2,1)} %get-tuple-element.36.refs_0_, bf16[1920,1024]{1,0:T(8,128)(2,1)} %get-tuple-element.45.refs_1_, f32[1920,128]{1,0:T(8,128)} %get-tuple-element.47.refs_2_, bf16[16,8,8,128]{3,2,1,0:T(8,128)(2,1)S(1)} %bitcast.24, ...), custom_call_target="tpu_custom_call" | custom-call | bytes 30000 | tf_op jit(solution)/shard_map/pallas_call | solution.py:359
  (31 shorter events, 0.2 us)
Async XLA Ops:
  0.0 8.8 %copy-start = (bf16[1024,256]{1,0:T(8,128)(2,1)S(1)}, bf16[1024,256]{1,0:T(8,128)(2,1)}, u32[]{:S(2)}) copy-start(bf16[1024,256]{1,0:T(8,128)(2,1)} %embed_any.1) | copy-start | bytes 1572868
  5.5 4.5 %collective-permute-start.1 = (bf16[128,1152]{1,0:T(8,128)(2,1)S(1)}, bf16[128,1152]{1,0:T(8,128)(2,1)S(1)}, u32[]{:S(2)}, u32[]{:S(2)}) collective-permute-start(bf16[128,1152]{1,0:T(8,128)(2,1)S(1)} %get-tuple-element.28), channel_id=1, source_target_pairs={{0,8},{8,0},{1,9},{9,1},{2,10},{10,2},{3,11},{11,3},{4,12},{12,4},... | collective-permute-start | bytes 884744 | tf_op jit(solution)/shard_map/ppermute | solution.py:395
  8.8 11.3 %collective-permute-start = (bf16[512,256]{1,0:T(8,128)(2,1)S(1)}, bf16[512,256]{1,0:T(8,128)(2,1)S(1)}, u32[]{:S(2)}, u32[]{:S(2)}) collective-permute-start(bf16[512,256]{1,0:T(8,128)(2,1)S(1)} %constant_dynamic-slice_fusion), channel_id=1, source_target_pairs={{0,1},{1,0},{2,3},{3,2},{4,5},{5,4},{6,7},{7,6},{8,9},{9,8},{10,11... | collective-permute-start | bytes 786440 | tf_op jit(solution)/shard_map/ppermute | solution.py:389
  11.1 22.0 %all-to-all-start = ((bf16[16,8,1152]{2,1,0:T(8,128)(2,1)}), bf16[16,8,1152]{2,1,0:T(8,128)(2,1)S(1)}, u32[]{:S(2)}, u32[]{:S(2)}) async-start(bf16[16,8,1152]{2,1,0:T(8,128)(2,1)} %bitcast.9), calls=%async_computation | async-start | bytes 589824 | tf_op jit(solution)/shard_map/all_to_all | solution.py:400
  20.3 36.0 %copy-start.1 = (bf16[2,512,256]{2,1,0:T(8,128)(2,1)}, bf16[2,512,256]{2,1,0:T(8,128)(2,1)S(1)}, u32[]{:S(2)}) copy-start(bf16[2,512,256]{2,1,0:T(8,128)(2,1)S(1)} %pad_maximum_fusion.refs_2_) | copy-start | bytes 1572868
  20.3 17.4 %collective-permute-start.2 = (bf16[2,512,256]{2,1,0:T(8,128)(2,1)S(1)}, bf16[2,512,256]{2,1,0:T(8,128)(2,1)S(1)}, u32[]{:S(2)}, u32[]{:S(2)}) collective-permute-start(bf16[2,512,256]{2,1,0:T(8,128)(2,1)S(1)} %pad_maximum_fusion.refs_2_), channel_id=1, source_target_pairs={{0,2},{2,4},{4,6},{6,0},{1,3},{3,5},{5,7},{7,1},{8,10},{10,12},{12... | collective-permute-start | bytes 1572872 | tf_op jit(solution)/shard_map/ppermute | solution.py:398
  21.6 17.4 %collective-permute-start.4 = (bf16[2,512,256]{2,1,0:T(8,128)(2,1)S(1)}, bf16[2,512,256]{2,1,0:T(8,128)(2,1)S(1)}, u32[]{:S(2)}, u32[]{:S(2)}) collective-permute-start(bf16[2,512,256]{2,1,0:T(8,128)(2,1)S(1)} %pad_maximum_fusion.refs_2_), channel_id=1, source_target_pairs={{0,6},{2,0},{4,2},{6,4},{1,7},{3,1},{5,3},{7,5},{8,14},{10,8},{12,... | collective-permute-start | bytes 1572872 | tf_op jit(solution)/shard_map/ppermute | solution.py:399
  34.1 15.3 %all-to-all-start.1 = ((bf16[16,8,1024]{2,1,0:T(8,128)(2,1)}), bf16[16,8,1024]{2,1,0:T(8,128)(2,1)S(1)}, u32[]{:S(2)}, u32[]{:S(2)}) async-start(bf16[16,8,1024]{2,1,0:T(8,128)(2,1)} %shard_map.48), calls=%async_computation.1 | async-start | bytes 524288 | tf_op jit(solution)/shard_map/all_to_all | solution.py:403
  37.7 18.6 %copy-start.3 = (bf16[2,512,256]{2,1,0:T(8,128)(2,1)}, bf16[2,512,256]{2,1,0:T(8,128)(2,1)S(1)}, u32[]{:S(2)}) copy-start(bf16[2,512,256]{2,1,0:T(8,128)(2,1)S(1)} %collective-permute-done.2.refs_3_) | copy-start | bytes 1572868
  37.7 7.3 %collective-permute-start.3 = (bf16[1,512,256]{2,1,0:T(8,128)(2,1)S(1)}, bf16[1,512,256]{2,1,0:T(8,128)(2,1)S(1)}, u32[]{:S(2)}, u32[]{:S(2)}) collective-permute-start(bf16[1,512,256]{2,1,0:T(8,128)(2,1)S(1)} %slice.8), channel_id=1, source_target_pairs={{0,2},{2,4},{4,6},{6,0},{1,3},{3,5},{5,7},{7,1},{8,10},{10,12},{12... | collective-permute-start | bytes 786440 | tf_op jit(solution)/shard_map/ppermute | solution.py:402
  39.1 17.2 %copy-start.2 = (bf16[2,512,256]{2,1,0:T(8,128)(2,1)}, bf16[2,512,256]{2,1,0:T(8,128)(2,1)S(1)}, u32[]{:S(2)}) copy-start(bf16[2,512,256]{2,1,0:T(8,128)(2,1)S(1)} %collective-permute-done.4.refs_4_) | copy-start | bytes 1572868
  39.1 5.9 %collective-permute-start.5 = (bf16[1,512,256]{2,1,0:T(8,128)(2,1)S(1)}, bf16[1,512,256]{2,1,0:T(8,128)(2,1)S(1)}, u32[]{:S(2)}, u32[]{:S(2)}) collective-permute-start(bf16[1,512,256]{2,1,0:T(8,128)(2,1)S(1)} %slice.9), channel_id=1, source_target_pairs={{0,6},{2,0},{4,2},{6,4},{1,7},{3,1},{5,3},{7,5},{8,14},{10,8},{12,... | collective-permute-start | bytes 786440 | tf_op jit(solution)/shard_map/ppermute | solution.py:402
  40.7 15.6 %collective-permute-start.8 = (bf16[2,512,256]{2,1,0:T(8,128)(2,1)S(1)}, bf16[2,512,256]{2,1,0:T(8,128)(2,1)S(1)}, u32[]{:S(2)}, u32[]{:S(2)}) collective-permute-start(bf16[2,512,256]{2,1,0:T(8,128)(2,1)S(1)} %pad_maximum_fusion.refs_2_), channel_id=1, source_target_pairs={{0,8},{8,0},{1,9},{9,1},{2,10},{10,2},{3,11},{11,3},{4,12},{12,4},... | collective-permute-start | bytes 1572872 | tf_op jit(solution)/shard_map/ppermute | solution.py:410
  45.0 7.0 %copy-start.7 = (bf16[1,512,256]{2,1,0:T(8,128)(2,1)}, bf16[1,512,256]{2,1,0:T(8,128)(2,1)S(1)}, u32[]{:S(2)}) copy-start(bf16[1,512,256]{2,1,0:T(8,128)(2,1)S(1)} %collective-permute-done.3.refs_5_) | copy-start | bytes 786436
  45.0 7.0 %copy-start.8 = (bf16[1,512,256]{2,1,0:T(8,128)(2,1)}, bf16[1,512,256]{2,1,0:T(8,128)(2,1)S(1)}, u32[]{:S(2)}) copy-start(bf16[1,512,256]{2,1,0:T(8,128)(2,1)S(1)} %collective-permute-done.5.refs_6_) | copy-start | bytes 786436
  49.4 3.7 %collective-permute-start.6 = (bf16[128,1024]{1,0:T(8,128)(2,1)S(1)}, bf16[128,1024]{1,0:T(8,128)(2,1)S(1)}, u32[]{:S(2)}, u32[]{:S(2)}) collective-permute-start(bf16[128,1024]{1,0:T(8,128)(2,1)S(1)} %bitcast.21), channel_id=1, source_target_pairs={{0,8},{8,0},{1,9},{9,1},{2,10},{10,2},{3,11},{11,3},{4,12},{12,4},... | collective-permute-start | bytes 786440 | tf_op jit(solution)/shard_map/ppermute | solution.py:405
  52.0 7.5 %collective-permute-start.9 = (bf16[2,512,256]{2,1,0:T(8,128)(2,1)S(1)}, bf16[2,512,256]{2,1,0:T(8,128)(2,1)S(1)}, u32[]{:S(2)}, u32[]{:S(2)}) collective-permute-start(bf16[2,512,256]{2,1,0:T(8,128)(2,1)S(1)} %collective-permute-done.2.refs_3_), channel_id=1, source_target_pairs={{0,8},{8,0},{1,9},{9,1},{2,10},{10,2},{3,11},{11,3},{4,12},{12,4},... | collective-permute-start | bytes 1572872 | tf_op jit(solution)/shard_map/ppermute | solution.py:410
  52.1 7.4 %collective-permute-start.10 = (bf16[2,512,256]{2,1,0:T(8,128)(2,1)S(1)}, bf16[2,512,256]{2,1,0:T(8,128)(2,1)S(1)}, u32[]{:S(2)}, u32[]{:S(2)}) collective-permute-start(bf16[2,512,256]{2,1,0:T(8,128)(2,1)S(1)} %collective-permute-done.4.refs_4_), channel_id=1, source_target_pairs={{0,8},{8,0},{1,9},{9,1},{2,10},{10,2},{3,11},{11,3},{4,12},{12,4},... | collective-permute-start | bytes 1572872 | tf_op jit(solution)/shard_map/ppermute | solution.py:410
  52.5 7.0 %collective-permute-start.11 = (bf16[1,512,256]{2,1,0:T(8,128)(2,1)}, bf16[1,512,256]{2,1,0:T(8,128)(2,1)S(1)}, u32[]{:S(2)}, u32[]{:S(2)}) collective-permute-start(bf16[1,512,256]{2,1,0:T(8,128)(2,1)} %copy-done.7), channel_id=1, source_target_pairs={{0,8},{8,0},{1,9},{9,1},{2,10},{10,2},{3,11},{11,3},{4,12},{12,4},... | collective-permute-start | bytes 786440 | tf_op jit(solution)/shard_map/ppermute | solution.py:410
  53.1 6.4 %collective-permute-start.12 = (bf16[1,512,256]{2,1,0:T(8,128)(2,1)}, bf16[1,512,256]{2,1,0:T(8,128)(2,1)S(1)}, u32[]{:S(2)}, u32[]{:S(2)}) collective-permute-start(bf16[1,512,256]{2,1,0:T(8,128)(2,1)} %copy-done.8), channel_id=1, source_target_pairs={{0,8},{8,0},{1,9},{9,1},{2,10},{10,2},{3,11},{11,3},{4,12},{12,4},... | collective-permute-start | bytes 786440 | tf_op jit(solution)/shard_map/ppermute | solution.py:410
  56.3 3.2 %copy-start.5 = (bf16[2,512,256]{2,1,0:T(8,128)(2,1)}, bf16[2,512,256]{2,1,0:T(8,128)(2,1)S(1)}, u32[]{:S(2)}) copy-start(bf16[2,512,256]{2,1,0:T(8,128)(2,1)S(1)} %collective-permute-done.8.refs_4_) | copy-start | bytes 1572868
  56.3 3.2 %collective-permute-start.7 = (bf16[128,1024]{1,0:T(8,128)(2,1)S(1)}, bf16[128,1024]{1,0:T(8,128)(2,1)S(1)}, u32[]{:S(2)}, u32[]{:S(2)}) collective-permute-start(bf16[128,1024]{1,0:T(8,128)(2,1)S(1)} %shard_map.49), channel_id=1, source_target_pairs={{0,8},{8,0},{1,9},{9,1},{2,10},{10,2},{3,11},{11,3},{4,12},{12,4},... | collective-permute-start | bytes 786440 | tf_op jit(solution)/shard_map/ppermute | solution.py:411
  59.5 9.5 %copy-start.6 = (bf16[2,512,256]{2,1,0:T(8,128)(2,1)}, bf16[2,512,256]{2,1,0:T(8,128)(2,1)S(1)}, u32[]{:S(2)}) copy-start(bf16[2,512,256]{2,1,0:T(8,128)(2,1)S(1)} %collective-permute-done.9.refs_5_) | copy-start | bytes 1572868
  59.5 19.5 %copy-start.4 = (bf16[2,512,256]{2,1,0:T(8,128)(2,1)}, bf16[2,512,256]{2,1,0:T(8,128)(2,1)S(1)}, u32[]{:S(2)}) copy-start(bf16[2,512,256]{2,1,0:T(8,128)(2,1)S(1)} %collective-permute-done.10.refs_7_) | copy-start | bytes 1572868
  59.5 1.0 copy-start.9
  59.5 1.0 copy-start.10
  60.5 21.6 %all-to-all-start.2 = ((bf16[64,2,8,128]{3,2,1,0:T(8,128)(2,1)}), bf16[64,2,8,128]{3,2,1,0:T(8,128)(2,1)S(1)}, u32[]{:S(2)}, u32[]{:S(2)}) async-start(bf16[64,2,8,128]{3,2,1,0:T(8,128)(2,1)} %bitcast.13.refs_6_), calls=%async_computation.2 | async-start | bytes 524288 | tf_op jit(solution)/shard_map/all_to_all | solution.py:418
  82.9 16.7 %all-to-all-start.3 = ((bf16[32,4,8,128]{3,2,1,0:T(8,128)(2,1)}), bf16[32,4,8,128]{3,2,1,0:T(8,128)(2,1)S(1)}, u32[]{:S(2)}, u32[]{:S(2)}) async-start(bf16[32,4,8,128]{3,2,1,0:T(8,128)(2,1)} %bitcast.18.refs_10_), calls=%async_computation.3 | async-start | bytes 524288 | tf_op jit(solution)/shard_map/all_to_all | solution.py:427
  99.6 3.8 %collective-permute-start.13 = (bf16[16,8,8,128]{3,2,1,0:T(8,128)(2,1)S(1)}, bf16[16,8,8,128]{3,2,1,0:T(8,128)(2,1)S(1)}, u32[]{:S(2)}, u32[]{:S(2)}) collective-permute-start(bf16[16,8,8,128]{3,2,1,0:T(8,128)(2,1)S(1)} %bitcast.23), channel_id=1, source_target_pairs={{0,8},{8,0},{1,9},{9,1},{2,10},{10,2},{3,11},{11,3},{4,12},{12,4},... | collective-permute-start | bytes 786440 | tf_op jit(solution)/shard_map/ppermute | solution.py:430

commit v7 on v6

--- a/solution.py
+++ b/solution.py
@@ -112,7 +112,7 @@
     send[...] = full[pl.ds(pl.multiple_of((1 - mine) * half, half), half), :].astype(BF16)
 
 
-def dispatch(core, tokens, slot_embed, parts=5):
+def dispatch(core, tokens, slot_embed, parts=6):
     count, width = tokens.shape
     slots = slot_embed.shape[1]
     shape = (slots // 2, width + TAIL)
@@ -372,8 +372,8 @@
     )(place, *map(far_memory, weights + scales), own, other)
 
 
-def shift(by):
-    return [(i, (i + by) % 4) for i in range(4)]
+def flip(bits):
+    return [(i, i ^ bits) for i in range(4)]
 
 
 def on_device(tokens, slot_embed, w_in, w_out):
@@ -387,7 +387,7 @@
 
     mine = lax.dynamic_slice_in_dim(slot_embed, core[0] * (features // 2), features // 2, 0)
     near = lax.ppermute(mine, "zl", SWAP)
-    rows_y = jnp.stack([y, y, y - 1, y - 1, y + 1, y + 1, y + 2, y + 2]) % ny
+    rows_y = jnp.stack([y, y, y ^ 1, y ^ 1, y ^ 3, y ^ 3, y ^ 2, y ^ 2])
     rows_l = jnp.stack([zl, 1 - zl] * 4)
     place = jnp.concatenate([core, rows_l * ny + rows_y]).astype(jnp.int32)
 
@@ -395,11 +395,11 @@
     merged = merge(own, lax.ppermute(send, "core", SWAP))
     near = lax.optimization_barrier((near, merged))[0]
     here = jnp.stack([mine, near])
-    down = lax.ppermute(here, "y", shift(1))
-    up = lax.ppermute(here, "y", shift(-1))
+    down = lax.ppermute(here, "y", flip(1))
+    up = lax.ppermute(here, "y", flip(3))
     got = lax.all_to_all(merged.reshape(nx * nh, part, -1), ("x", "zh"), 0, 0)
     spread = reduce_in(got)
-    far = [lax.ppermute(down[:1], "y", shift(1)), lax.ppermute(up[1:], "y", shift(-1))]
+    far = [lax.ppermute(down[:1], "y", flip(3)), lax.ppermute(up[1:], "y", flip(1))]
     slots_own = lax.all_to_all(spread, ("x", "zh"), 0, 0).reshape(half, features)
     slots_own, far = lax.optimization_barrier((slots_own, far))
     slots_other = lax.ppermute(slots_own, "core", SWAP)

time: 110 us -> 110 us (level)
    ppermute x4, waiting for transfers between devices: 1.94 us -> 3.22 us  [the longest x1 1.99 us: on_device(): lax.ppermute(down[:1], 'y', flip(3))]
    all_to_all x1, waiting for transfers between devices: 4.46 us -> 3.29 us  [on_device(): lax.all_to_all(spread, ('x', 'zh'), 0, 0).reshape(half, features)]
  transfers between devices with their start and end apart: 18 -> 18, of which waited for: 7 -> 8; matrix products, arithmetic and copies ran while one was open for 0% -> 0% of each run, Pallas kernels for 26% -> 26%
where the time goes in v7:
time: 110 us
  starting transfers between devices  45.3 us (41%)
  Pallas kernels  39.6 us (36%)
  waiting for transfers between devices  21.9 us (20%)
  other arithmetic  1.15 us (1%)
    pallas_call x2, Pallas kernels, combine_weights(): call(after(functools.partial(weights_kernel, len(pieces)), 2 + len(earlie...  20.5 us
    all_to_all x1, waiting for transfers between devices, on_device(): got = lax.all_to_all(merged.reshape(nx * nh, part, -1), ('x', 'zh'), 0, 0)  9.58 us
    all_to_all x1, starting transfers between devices, on_device(): got = lax.all_to_all(merged.reshape(nx * nh, part, -1), ('x', 'zh'), 0, 0)  9.02 us
    all_to_all x1, starting transfers between devices, on_device(): got = lax.all_to_all(cut, ('x', 'zh', 'y'), 0, 0)  8.28 us
    all_to_all x1, starting transfers between devices, on_device(): out_own = lax.all_to_all(spread, ('x', 'zh', 'zl'), 0, 0)  6.05 us
    pallas_call x1, Pallas kernels, dispatch(): call(functools.partial(dispatch_kernel, parts), micros=6, outs=[kept(shap...  5.76 us
    pallas_call x1, Pallas kernels, output(): call(functools.partial(output_kernel, parts, steps), jax.ShapeDtypeStruct...  5.75 us
    pallas_call x2, Pallas kernels, experts(): call(after(functools.partial(expert_kernel, slots.shape[0] // count), 4,...  5.48 us
  transfers between devices with their start and end apart: 18, of which 8 were waited for; matrix products, arithmetic and copies ran while one was open for 0% of the time, Pallas kernels for 26%

profile of v7, /device:TPU:1, one launch (start us, length us, event | category | flops | bytes accessed | tf_op | source)
XLA Modules:
  0.0 109.5 jit_solution(7100479028286626658)
XLA Ops:
  0.0 5.8 %shard_map.46 = (f32[128,1152]{1,0:T(8,128)S(1)}, bf16[128,1152]{1,0:T(8,128)(2,1)S(1)}) custom-call(s32[1]{0:T(128)} %bitcast.core.refs_0_, bf16[1920,1024]{1,0:T(8,128)(2,1)} %refs_1_.3, bf16[1024,256]{1,0:T(8,128)(2,1)} %embed_any.1), custom_call_target="tpu_custom_call" | custom-call | bytes 180000 | tf_op jit(solution)/shard_map/pallas_call | solution.py:119
  5.8 3.3 %collective-permute-start.1 = (bf16[128,1152]{1,0:T(8,128)(2,1)S(1)}, bf16[128,1152]{1,0:T(8,128)(2,1)S(1)}, u32[]{:S(2)}, u32[]{:S(2)}) collective-permute-start(bf16[128,1152]{1,0:T(8,128)(2,1)S(1)} %get-tuple-element.28), channel_id=1, source_target_pairs={{0,8},{8,0},{1,9},{9,1},{2,10},{10,2},{3,11},{11,3},{4,12},{12,4},... | collective-permute-start | bytes 884744 | tf_op jit(solution)/shard_map/ppermute | solution.py:395
  9.1 0.1 collective-permute-start
  9.2 1.1 collective-permute-done.1.got
  10.3 1.1 %shard_map.47 = bf16[128,1152]{1,0:T(8,128)(2,1)} custom-call(f32[128,1152]{1,0:T(8,128)S(1)} %get-tuple-element.27.own, bf16[128,1152]{1,0:T(8,128)(2,1)S(1)} %collective-permute-done.1.got), custom_call_target="tpu_custom_call" | custom-call | bytes 30000 | tf_op jit(solution)/shard_map/pallas_call | solution.py:151
  11.4 9.0 %all-to-all-start = ((bf16[16,8,1152]{2,1,0:T(8,128)(2,1)}), bf16[16,8,1152]{2,1,0:T(8,128)(2,1)S(1)}, u32[]{:S(2)}, u32[]{:S(2)}) async-start(bf16[16,8,1152]{2,1,0:T(8,128)(2,1)} %bitcast.9), calls=%async_computation | async-start | bytes 589824 | tf_op jit(solution)/shard_map/all_to_all | solution.py:400
  20.5 0.0 collective-permute-done
  20.5 0.1 pad_maximum_fusion.refs_2_
  20.6 1.4 %collective-permute-start.2 = (bf16[2,512,256]{2,1,0:T(8,128)(2,1)S(1)}, bf16[2,512,256]{2,1,0:T(8,128)(2,1)S(1)}, u32[]{:S(2)}, u32[]{:S(2)}) collective-permute-start(bf16[2,512,256]{2,1,0:T(8,128)(2,1)S(1)} %pad_maximum_fusion.refs_2_), channel_id=1, source_target_pairs={{0,2},{2,0},{4,6},{6,4},{1,3},{3,1},{5,7},{7,5},{8,10},{10,8},{12,... | collective-permute-start | bytes 1572872 | tf_op jit(solution)/shard_map/ppermute | solution.py:398
  21.9 1.9 %collective-permute-start.4 = (bf16[2,512,256]{2,1,0:T(8,128)(2,1)S(1)}, bf16[2,512,256]{2,1,0:T(8,128)(2,1)S(1)}, u32[]{:S(2)}, u32[]{:S(2)}) collective-permute-start(bf16[2,512,256]{2,1,0:T(8,128)(2,1)S(1)} %pad_maximum_fusion.refs_2_), channel_id=1, source_target_pairs={{0,6},{2,4},{4,2},{6,0},{1,7},{3,5},{5,3},{7,1},{8,14},{10,12},{12... | collective-permute-start | bytes 1572872 | tf_op jit(solution)/shard_map/ppermute | solution.py:399
  23.8 9.6 %all-to-all-done.got = bf16[16,8,1152]{2,1,0:T(8,128)(2,1)S(1)} async-done(((bf16[16,8,1152]{2,1,0:T(8,128)(2,1)}), bf16[16,8,1152]{2,1,0:T(8,128)(2,1)S(1)}, u32[]{:S(2)}, u32[]{:S(2)}) %all-to-all-start) | async-done | bytes 294944 | tf_op jit(solution)/shard_map/all_to_all | solution.py:400
  33.4 1.0 shard_map.48
  34.4 3.5 %all-to-all-start.1 = ((bf16[16,8,1024]{2,1,0:T(8,128)(2,1)}), bf16[16,8,1024]{2,1,0:T(8,128)(2,1)S(1)}, u32[]{:S(2)}, u32[]{:S(2)}) async-start(bf16[16,8,1024]{2,1,0:T(8,128)(2,1)} %shard_map.48), calls=%async_computation.1 | async-start | bytes 524288 | tf_op jit(solution)/shard_map/all_to_all | solution.py:403
  37.9 0.0 collective-permute-done.2.refs_3_
  38.0 2.8 %collective-permute-start.3 = (bf16[1,512,256]{2,1,0:T(8,128)(2,1)S(1)}, bf16[1,512,256]{2,1,0:T(8,128)(2,1)S(1)}, u32[]{:S(2)}, u32[]{:S(2)}) collective-permute-start(bf16[1,512,256]{2,1,0:T(8,128)(2,1)S(1)} %slice.8), channel_id=1, source_target_pairs={{0,6},{2,4},{4,2},{6,0},{1,7},{3,5},{5,3},{7,1},{8,14},{10,12},{12... | collective-permute-start | bytes 786440 | tf_op jit(solution)/shard_map/ppermute | solution.py:402
  40.8 0.0 collective-permute-done.4.refs_4_
  40.8 0.1 collective-permute-start.5
  40.9 2.3 %collective-permute-start.8 = (bf16[2,512,256]{2,1,0:T(8,128)(2,1)S(1)}, bf16[2,512,256]{2,1,0:T(8,128)(2,1)S(1)}, u32[]{:S(2)}, u32[]{:S(2)}) collective-permute-start(bf16[2,512,256]{2,1,0:T(8,128)(2,1)S(1)} %pad_maximum_fusion.refs_2_), channel_id=1, source_target_pairs={{0,8},{8,0},{1,9},{9,1},{2,10},{10,2},{3,11},{11,3},{4,12},{12,4},... | collective-permute-start | bytes 1572872 | tf_op jit(solution)/shard_map/ppermute | solution.py:410
  43.3 2.0 %collective-permute-done.3.refs_5_ = bf16[1,512,256]{2,1,0:T(8,128)(2,1)S(1)} collective-permute-done((bf16[1,512,256]{2,1,0:T(8,128)(2,1)S(1)}, bf16[1,512,256]{2,1,0:T(8,128)(2,1)S(1)}, u32[]{:S(2)}, u32[]{:S(2)}) %collective-permute-start.3) | collective-permute-done | bytes 262176 | tf_op jit(solution)/shard_map/ppermute | solution.py:402
  45.3 1.2 %collective-permute-done.5.refs_6_ = bf16[1,512,256]{2,1,0:T(8,128)(2,1)S(1)} collective-permute-done((bf16[1,512,256]{2,1,0:T(8,128)(2,1)S(1)}, bf16[1,512,256]{2,1,0:T(8,128)(2,1)S(1)}, u32[]{:S(2)}, u32[]{:S(2)}) %collective-permute-start.5) | collective-permute-done | bytes 262176 | tf_op jit(solution)/shard_map/ppermute | solution.py:402
  46.5 3.3 %all-to-all-done.1 = bf16[16,8,1024]{2,1,0:T(8,128)(2,1)S(1)} async-done(((bf16[16,8,1024]{2,1,0:T(8,128)(2,1)}), bf16[16,8,1024]{2,1,0:T(8,128)(2,1)S(1)}, u32[]{:S(2)}, u32[]{:S(2)}) %all-to-all-start.1) | async-done | bytes 262176 | tf_op jit(solution)/shard_map/all_to_all | solution.py:403
  49.8 2.5 %collective-permute-start.6 = (bf16[128,1024]{1,0:T(8,128)(2,1)S(1)}, bf16[128,1024]{1,0:T(8,128)(2,1)S(1)}, u32[]{:S(2)}, u32[]{:S(2)}) collective-permute-start(bf16[128,1024]{1,0:T(8,128)(2,1)S(1)} %bitcast.21), channel_id=1, source_target_pairs={{0,8},{8,0},{1,9},{9,1},{2,10},{10,2},{3,11},{11,3},{4,12},{12,4},... | collective-permute-start | bytes 786440 | tf_op jit(solution)/shard_map/ppermute | solution.py:405
  52.2 0.1 collective-permute-start.9
  52.3 0.4 collective-permute-start.10
  52.8 0.1 collective-permute-start.11
  52.8 0.6 collective-permute-done.6.refs_1_
  53.4 0.4 collective-permute-start.12
  53.8 2.7 %shard_map.49 = bf16[128,1024]{1,0:T(8,128)(2,1)S(1)} custom-call(s32[1]{0:T(128)S(6)} %sub.7.refs_0_, bf16[128,1024]{1,0:T(8,128)(2,1)S(1)} %collective-permute-done.6.refs_1_, bf16[16,1024,128]{2,1,0:T(8,128)(2,1)} %refs_2_.3, bf16[16,128,1024]{2,1,0:T(8,128)(2,1)} %refs_3_.3), custom_call_target="tpu_custom_call" | custom-call | bytes 90000 | tf_op jit(solution)/shard_map/pallas_call | solution.py:221
  56.6 0.0 collective-permute-done.8.refs_4_
  56.6 0.4 collective-permute-start.7
  57.0 2.7 %shard_map.50 = f32[128,1024]{1,0:T(8,128)S(1)} custom-call(s32[1]{0:T(128)} %bitcast.core.refs_0_, bf16[128,1024]{1,0:T(8,128)(2,1)S(1)} %bitcast.22, bf16[16,1024,128]{2,1,0:T(8,128)(2,1)} %refs_2_.3, bf16[16,128,1024]{2,1,0:T(8,128)(2,1)} %refs_3_.3), custom_call_target="tpu_custom_call" | custom-call | bytes 90000 | tf_op jit(solution)/shard_map/pallas_call | solution.py:221
  59.7 0.0 collective-permute-done.9.refs_5_
  59.8 0.0 collective-permute-done.10.refs_7_
  59.8 0.0 collective-permute-done.11.refs_8_
  59.8 1.0 add_convert_fusion
  60.8 8.3 %all-to-all-start.2 = ((bf16[64,2,8,128]{3,2,1,0:T(8,128)(2,1)}), bf16[64,2,8,128]{3,2,1,0:T(8,128)(2,1)S(1)}, u32[]{:S(2)}, u32[]{:S(2)}) async-start(bf16[64,2,8,128]{3,2,1,0:T(8,128)(2,1)} %bitcast.13.refs_6_), calls=%async_computation.2 | async-start | bytes 524288 | tf_op jit(solution)/shard_map/all_to_all | solution.py:418
  69.1 10.1 %shard_map.51 = (bf16[1920,1024]{1,0:T(8,128)(2,1)}, f32[1920,128]{1,0:T(8,128)}, f32[1920,128]{1,0:T(8,128)}) custom-call(s32[1]{0:T(128)} %bitcast.core.refs_0_, bf16[1920,1024]{1,0:T(8,128)(2,1)} %refs_1_.3, bf16[2,512,256]{2,1,0:T(8,128)(2,1)} %copy-done.1, bf16[2,512,256]{2,1,0:T(8,128)(2,1)} %copy-done.3, bf16[2,512,256]{2,1,0:T(8,128)(2,1)} %copy-done.5, ...), custom_call_target="tpu_custom_call" | custom-call | bytes 240000 | tf_op jit(solution)/shard_map/pallas_call | solution.py:290
  79.2 3.1 %all-to-all-done.2 = bf16[64,2,8,128]{3,2,1,0:T(8,128)(2,1)S(1)} async-done(((bf16[64,2,8,128]{3,2,1,0:T(8,128)(2,1)}), bf16[64,2,8,128]{3,2,1,0:T(8,128)(2,1)S(1)}, u32[]{:S(2)}, u32[]{:S(2)}) %all-to-all-start.2) | async-done | bytes 262176 | tf_op jit(solution)/shard_map/all_to_all | solution.py:418
  82.3 0.8 broadcast_in_dim.2
  83.1 6.0 %all-to-all-start.3 = ((bf16[32,4,8,128]{3,2,1,0:T(8,128)(2,1)}), bf16[32,4,8,128]{3,2,1,0:T(8,128)(2,1)S(1)}, u32[]{:S(2)}, u32[]{:S(2)}) async-start(bf16[32,4,8,128]{3,2,1,0:T(8,128)(2,1)} %bitcast.18.refs_10_), calls=%async_computation.3 | async-start | bytes 524288 | tf_op jit(solution)/shard_map/all_to_all | solution.py:427
  89.2 0.1 stack.45
  89.2 0.1 stack.50
  89.3 10.4 %shard_map.52 = (bf16[1920,1024]{1,0:T(8,128)(2,1)}, f32[1920,128]{1,0:T(8,128)}) custom-call(s32[1]{0:T(128)} %bitcast.core.refs_0_, bf16[1920,1024]{1,0:T(8,128)(2,1)} %refs_1_.3, f32[1920,128]{1,0:T(8,128)} %get-tuple-element.39.refs_2_, f32[1920,128]{1,0:T(8,128)} %get-tuple-element.40.refs_3_, bf16[2,512,256]{2,1,0:T(8,128)(2,1)} %copy-done.2, ...), custom_call_target="tpu_custom_call" | custom-call | bytes 240000 | tf_op jit(solution)/shard_map/pallas_call | solution.py:290
  99.8 0.0 all-to-all-done.3
  99.8 2.7 %collective-permute-start.13 = (bf16[16,8,8,128]{3,2,1,0:T(8,128)(2,1)S(1)}, bf16[16,8,8,128]{3,2,1,0:T(8,128)(2,1)S(1)}, u32[]{:S(2)}, u32[]{:S(2)}) collective-permute-start(bf16[16,8,8,128]{3,2,1,0:T(8,128)(2,1)S(1)} %bitcast.23), channel_id=1, source_target_pairs={{0,8},{8,0},{1,9},{9,1},{2,10},{10,2},{3,11},{11,3},{4,12},{12,4},... | collective-permute-start | bytes 786440 | tf_op jit(solution)/shard_map/ppermute | solution.py:430
  102.5 0.1 pad_add_fusion.place
  102.5 1.1 collective-permute-done.13.refs_4_
  103.6 5.7 %shard_map.53 = bf16[1920,128]{1,0:T(8,128)(2,1)} custom-call(s32[9]{0:T(128)S(1)} %pad_add_fusion.place, bf16[1920,1024]{1,0:T(8,128)(2,1)} %get-tuple-element.36.refs_0_, bf16[1920,1024]{1,0:T(8,128)(2,1)} %get-tuple-element.45.refs_1_, f32[1920,128]{1,0:T(8,128)} %get-tuple-element.47.refs_2_, bf16[16,8,8,128]{3,2,1,0:T(8,128)(2,1)S(1)} %bitcast.24, ...), custom_call_target="tpu_custom_call" | custom-call | bytes 30000 | tf_op jit(solution)/shard_map/pallas_call | solution.py:359
  (31 shorter events, 0.2 us)
Async XLA Ops:
  0.0 9.1 %copy-start = (bf16[1024,256]{1,0:T(8,128)(2,1)S(1)}, bf16[1024,256]{1,0:T(8,128)(2,1)}, u32[]{:S(2)}) copy-start(bf16[1024,256]{1,0:T(8,128)(2,1)} %embed_any.1) | copy-start | bytes 1572868
  5.8 4.5 %collective-permute-start.1 = (bf16[128,1152]{1,0:T(8,128)(2,1)S(1)}, bf16[128,1152]{1,0:T(8,128)(2,1)S(1)}, u32[]{:S(2)}, u32[]{:S(2)}) collective-permute-start(bf16[128,1152]{1,0:T(8,128)(2,1)S(1)} %get-tuple-element.28), channel_id=1, source_target_pairs={{0,8},{8,0},{1,9},{9,1},{2,10},{10,2},{3,11},{11,3},{4,12},{12,4},... | collective-permute-start | bytes 884744 | tf_op jit(solution)/shard_map/ppermute | solution.py:395
  9.1 11.4 %collective-permute-start = (bf16[512,256]{1,0:T(8,128)(2,1)S(1)}, bf16[512,256]{1,0:T(8,128)(2,1)S(1)}, u32[]{:S(2)}, u32[]{:S(2)}) collective-permute-start(bf16[512,256]{1,0:T(8,128)(2,1)S(1)} %constant_dynamic-slice_fusion), channel_id=1, source_target_pairs={{0,1},{1,0},{2,3},{3,2},{4,5},{5,4},{6,7},{7,6},{8,9},{9,8},{10,11... | collective-permute-start | bytes 786440 | tf_op jit(solution)/shard_map/ppermute | solution.py:389
  11.4 22.0 %all-to-all-start = ((bf16[16,8,1152]{2,1,0:T(8,128)(2,1)}), bf16[16,8,1152]{2,1,0:T(8,128)(2,1)S(1)}, u32[]{:S(2)}, u32[]{:S(2)}) async-start(bf16[16,8,1152]{2,1,0:T(8,128)(2,1)} %bitcast.9), calls=%async_computation | async-start | bytes 589824 | tf_op jit(solution)/shard_map/all_to_all | solution.py:400
  20.5 36.0 %copy-start.1 = (bf16[2,512,256]{2,1,0:T(8,128)(2,1)}, bf16[2,512,256]{2,1,0:T(8,128)(2,1)S(1)}, u32[]{:S(2)}) copy-start(bf16[2,512,256]{2,1,0:T(8,128)(2,1)S(1)} %pad_maximum_fusion.refs_2_) | copy-start | bytes 1572868
  20.6 17.4 %collective-permute-start.2 = (bf16[2,512,256]{2,1,0:T(8,128)(2,1)S(1)}, bf16[2,512,256]{2,1,0:T(8,128)(2,1)S(1)}, u32[]{:S(2)}, u32[]{:S(2)}) collective-permute-start(bf16[2,512,256]{2,1,0:T(8,128)(2,1)S(1)} %pad_maximum_fusion.refs_2_), channel_id=1, source_target_pairs={{0,2},{2,0},{4,6},{6,4},{1,3},{3,1},{5,7},{7,5},{8,10},{10,8},{12,... | collective-permute-start | bytes 1572872 | tf_op jit(solution)/shard_map/ppermute | solution.py:398
  21.9 18.9 %collective-permute-start.4 = (bf16[2,512,256]{2,1,0:T(8,128)(2,1)S(1)}, bf16[2,512,256]{2,1,0:T(8,128)(2,1)S(1)}, u32[]{:S(2)}, u32[]{:S(2)}) collective-permute-start(bf16[2,512,256]{2,1,0:T(8,128)(2,1)S(1)} %pad_maximum_fusion.refs_2_), channel_id=1, source_target_pairs={{0,6},{2,4},{4,2},{6,0},{1,7},{3,5},{5,3},{7,1},{8,14},{10,12},{12... | collective-permute-start | bytes 1572872 | tf_op jit(solution)/shard_map/ppermute | solution.py:399
  34.4 15.4 %all-to-all-start.1 = ((bf16[16,8,1024]{2,1,0:T(8,128)(2,1)}), bf16[16,8,1024]{2,1,0:T(8,128)(2,1)S(1)}, u32[]{:S(2)}, u32[]{:S(2)}) async-start(bf16[16,8,1024]{2,1,0:T(8,128)(2,1)} %shard_map.48), calls=%async_computation.1 | async-start | bytes 524288 | tf_op jit(solution)/shard_map/all_to_all | solution.py:403
  38.0 18.6 %copy-start.3 = (bf16[2,512,256]{2,1,0:T(8,128)(2,1)}, bf16[2,512,256]{2,1,0:T(8,128)(2,1)S(1)}, u32[]{:S(2)}) copy-start(bf16[2,512,256]{2,1,0:T(8,128)(2,1)S(1)} %collective-permute-done.2.refs_3_) | copy-start | bytes 1572868
  38.0 7.3 %collective-permute-start.3 = (bf16[1,512,256]{2,1,0:T(8,128)(2,1)S(1)}, bf16[1,512,256]{2,1,0:T(8,128)(2,1)S(1)}, u32[]{:S(2)}, u32[]{:S(2)}) collective-permute-start(bf16[1,512,256]{2,1,0:T(8,128)(2,1)S(1)} %slice.8), channel_id=1, source_target_pairs={{0,6},{2,4},{4,2},{6,0},{1,7},{3,5},{5,3},{7,1},{8,14},{10,12},{12... | collective-permute-start | bytes 786440 | tf_op jit(solution)/shard_map/ppermute | solution.py:402
  40.8 15.7 %copy-start.2 = (bf16[2,512,256]{2,1,0:T(8,128)(2,1)}, bf16[2,512,256]{2,1,0:T(8,128)(2,1)S(1)}, u32[]{:S(2)}) copy-start(bf16[2,512,256]{2,1,0:T(8,128)(2,1)S(1)} %collective-permute-done.4.refs_4_) | copy-start | bytes 1572868
  40.8 5.7 %collective-permute-start.5 = (bf16[1,512,256]{2,1,0:T(8,128)(2,1)S(1)}, bf16[1,512,256]{2,1,0:T(8,128)(2,1)S(1)}, u32[]{:S(2)}, u32[]{:S(2)}) collective-permute-start(bf16[1,512,256]{2,1,0:T(8,128)(2,1)S(1)} %slice.9), channel_id=1, source_target_pairs={{0,2},{2,0},{4,6},{6,4},{1,3},{3,1},{5,7},{7,5},{8,10},{10,8},{12,... | collective-permute-start | bytes 786440 | tf_op jit(solution)/shard_map/ppermute | solution.py:402
  40.9 15.6 %collective-permute-start.8 = (bf16[2,512,256]{2,1,0:T(8,128)(2,1)S(1)}, bf16[2,512,256]{2,1,0:T(8,128)(2,1)S(1)}, u32[]{:S(2)}, u32[]{:S(2)}) collective-permute-start(bf16[2,512,256]{2,1,0:T(8,128)(2,1)S(1)} %pad_maximum_fusion.refs_2_), channel_id=1, source_target_pairs={{0,8},{8,0},{1,9},{9,1},{2,10},{10,2},{3,11},{11,3},{4,12},{12,4},... | collective-permute-start | bytes 1572872 | tf_op jit(solution)/shard_map/ppermute | solution.py:410
  45.3 7.0 %copy-start.7 = (bf16[1,512,256]{2,1,0:T(8,128)(2,1)}, bf16[1,512,256]{2,1,0:T(8,128)(2,1)S(1)}, u32[]{:S(2)}) copy-start(bf16[1,512,256]{2,1,0:T(8,128)(2,1)S(1)} %collective-permute-done.3.refs_5_) | copy-start | bytes 786436
  46.5 5.8 %copy-start.8 = (bf16[1,512,256]{2,1,0:T(8,128)(2,1)}, bf16[1,512,256]{2,1,0:T(8,128)(2,1)S(1)}, u32[]{:S(2)}) copy-start(bf16[1,512,256]{2,1,0:T(8,128)(2,1)S(1)} %collective-permute-done.5.refs_6_) | copy-start | bytes 786436
  49.8 3.6 %collective-permute-start.6 = (bf16[128,1024]{1,0:T(8,128)(2,1)S(1)}, bf16[128,1024]{1,0:T(8,128)(2,1)S(1)}, u32[]{:S(2)}, u32[]{:S(2)}) collective-permute-start(bf16[128,1024]{1,0:T(8,128)(2,1)S(1)} %bitcast.21), channel_id=1, source_target_pairs={{0,8},{8,0},{1,9},{9,1},{2,10},{10,2},{3,11},{11,3},{4,12},{12,4},... | collective-permute-start | bytes 786440 | tf_op jit(solution)/shard_map/ppermute | solution.py:405
  52.2 7.5 %collective-permute-start.9 = (bf16[2,512,256]{2,1,0:T(8,128)(2,1)S(1)}, bf16[2,512,256]{2,1,0:T(8,128)(2,1)S(1)}, u32[]{:S(2)}, u32[]{:S(2)}) collective-permute-start(bf16[2,512,256]{2,1,0:T(8,128)(2,1)S(1)} %collective-permute-done.2.refs_3_), channel_id=1, source_target_pairs={{0,8},{8,0},{1,9},{9,1},{2,10},{10,2},{3,11},{11,3},{4,12},{12,4},... | collective-permute-start | bytes 1572872 | tf_op jit(solution)/shard_map/ppermute | solution.py:410
  52.3 7.4 %collective-permute-start.10 = (bf16[2,512,256]{2,1,0:T(8,128)(2,1)S(1)}, bf16[2,512,256]{2,1,0:T(8,128)(2,1)S(1)}, u32[]{:S(2)}, u32[]{:S(2)}) collective-permute-start(bf16[2,512,256]{2,1,0:T(8,128)(2,1)S(1)} %collective-permute-done.4.refs_4_), channel_id=1, source_target_pairs={{0,8},{8,0},{1,9},{9,1},{2,10},{10,2},{3,11},{11,3},{4,12},{12,4},... | collective-permute-start | bytes 1572872 | tf_op jit(solution)/shard_map/ppermute | solution.py:410
  52.8 7.0 %collective-permute-start.11 = (bf16[1,512,256]{2,1,0:T(8,128)(2,1)}, bf16[1,512,256]{2,1,0:T(8,128)(2,1)S(1)}, u32[]{:S(2)}, u32[]{:S(2)}) collective-permute-start(bf16[1,512,256]{2,1,0:T(8,128)(2,1)} %copy-done.7), channel_id=1, source_target_pairs={{0,8},{8,0},{1,9},{9,1},{2,10},{10,2},{3,11},{11,3},{4,12},{12,4},... | collective-permute-start | bytes 786440 | tf_op jit(solution)/shard_map/ppermute | solution.py:410
  53.4 6.4 %collective-permute-start.12 = (bf16[1,512,256]{2,1,0:T(8,128)(2,1)}, bf16[1,512,256]{2,1,0:T(8,128)(2,1)S(1)}, u32[]{:S(2)}, u32[]{:S(2)}) collective-permute-start(bf16[1,512,256]{2,1,0:T(8,128)(2,1)} %copy-done.8), channel_id=1, source_target_pairs={{0,8},{8,0},{1,9},{9,1},{2,10},{10,2},{3,11},{11,3},{4,12},{12,4},... | collective-permute-start | bytes 786440 | tf_op jit(solution)/shard_map/ppermute | solution.py:410
  56.6 3.2 %copy-start.5 = (bf16[2,512,256]{2,1,0:T(8,128)(2,1)}, bf16[2,512,256]{2,1,0:T(8,128)(2,1)S(1)}, u32[]{:S(2)}) copy-start(bf16[2,512,256]{2,1,0:T(8,128)(2,1)S(1)} %collective-permute-done.8.refs_4_) | copy-start | bytes 1572868
  56.6 3.2 %collective-permute-start.7 = (bf16[128,1024]{1,0:T(8,128)(2,1)S(1)}, bf16[128,1024]{1,0:T(8,128)(2,1)S(1)}, u32[]{:S(2)}, u32[]{:S(2)}) collective-permute-start(bf16[128,1024]{1,0:T(8,128)(2,1)S(1)} %shard_map.49), channel_id=1, source_target_pairs={{0,8},{8,0},{1,9},{9,1},{2,10},{10,2},{3,11},{11,3},{4,12},{12,4},... | collective-permute-start | bytes 786440 | tf_op jit(solution)/shard_map/ppermute | solution.py:411
  59.8 9.3 %copy-start.6 = (bf16[2,512,256]{2,1,0:T(8,128)(2,1)}, bf16[2,512,256]{2,1,0:T(8,128)(2,1)S(1)}, u32[]{:S(2)}) copy-start(bf16[2,512,256]{2,1,0:T(8,128)(2,1)S(1)} %collective-permute-done.9.refs_5_) | copy-start | bytes 1572868
  59.8 19.4 %copy-start.4 = (bf16[2,512,256]{2,1,0:T(8,128)(2,1)}, bf16[2,512,256]{2,1,0:T(8,128)(2,1)S(1)}, u32[]{:S(2)}) copy-start(bf16[2,512,256]{2,1,0:T(8,128)(2,1)S(1)} %collective-permute-done.10.refs_7_) | copy-start | bytes 1572868
  59.8 1.0 copy-start.9
  59.8 1.0 copy-start.10
  60.8 21.5 %all-to-all-start.2 = ((bf16[64,2,8,128]{3,2,1,0:T(8,128)(2,1)}), bf16[64,2,8,128]{3,2,1,0:T(8,128)(2,1)S(1)}, u32[]{:S(2)}, u32[]{:S(2)}) async-start(bf16[64,2,8,128]{3,2,1,0:T(8,128)(2,1)} %bitcast.13.refs_6_), calls=%async_computation.2 | async-start | bytes 524288 | tf_op jit(solution)/shard_map/all_to_all | solution.py:418
  83.1 16.7 %all-to-all-start.3 = ((bf16[32,4,8,128]{3,2,1,0:T(8,128)(2,1)}), bf16[32,4,8,128]{3,2,1,0:T(8,128)(2,1)S(1)}, u32[]{:S(2)}, u32[]{:S(2)}) async-start(bf16[32,4,8,128]{3,2,1,0:T(8,128)(2,1)} %bitcast.18.refs_10_), calls=%async_computation.3 | async-start | bytes 524288 | tf_op jit(solution)/shard_map/all_to_all | solution.py:427
  99.8 3.8 %collective-permute-start.13 = (bf16[16,8,8,128]{3,2,1,0:T(8,128)(2,1)S(1)}, bf16[16,8,8,128]{3,2,1,0:T(8,128)(2,1)S(1)}, u32[]{:S(2)}, u32[]{:S(2)}) collective-permute-start(bf16[16,8,8,128]{3,2,1,0:T(8,128)(2,1)S(1)} %bitcast.23), channel_id=1, source_target_pairs={{0,8},{8,0},{1,9},{9,1},{2,10},{10,2},{3,11},{11,3},{4,12},{12,4},... | collective-permute-start | bytes 786440 | tf_op jit(solution)/shard_map/ppermute | solution.py:430
